TPU v7x, 32 devices: a whole 2x2x4 slice. The times are simulated.
32 devices in a mesh: energy: 8 (over z, x), mom: 4 (over y, core).
Axes of the slice: x: 2, y: 2, z: 4, core: 2. Of those that a mesh axis runs over, the one named last changes fastest.
Arguments:
- inverse_blocks: bfloat16 [2, 16, 4, 2048, 256], P(None, 'energy', 'mom'), may hold values from -0.25 to 0.25
- coupling_blocks: bfloat16 [2, 4, 2048, 256], P(None, 'mom'), may hold values from -0.10595703 to 0.10595703
- shifts: int32 [4], replicated, may hold values from 0 to 1, as said below
- emission_weight: float32 [4, 4, 4], replicated, may hold values from 0.5 to 4
- absorption_weight: float32 [4, 4, 4], replicated, may hold values from 0.5 to 4
- deform_potential: float32 [2048], replicated, may hold values from 0.5 to 2
- range_rows: int32 [32], replicated, may hold values from 1 to 128, 2048 in all
Outputs:
- sigma: bfloat16 [2, 16, 4, 2048, 256], P(None, 'energy', 'mom')
- charge: float32 [32], P(('energy', 'mom'))
Inputs may be any that keep to these rules, and one draw needn't show every extreme that they name: `shifts`: one mode's shift is exactly 1. `range_rows`: the counts add up to 2048; the largest is exactly 128.
All inputs are finite; a program needn't handle non-finite values.
Results may differ from a plain program's by a relative error of at most 0.015.
Values may be sent and summed in bfloat16 or wider, within the bound.
No kernel may reach another device: no remote copies, remote signals or barrier semaphores. Data moves between devices by JAX's collectives and lax.ppermute only.
A program may use at most 192 MiB of HBM per device.

v0:
```python
import functools

import jax
import jax.numpy as jnp
from jax import lax
from jax.experimental import pallas as pl
from jax.experimental.pallas import tpu as pltpu
from jax.sharding import PartitionSpec as P

CHUNKS = (("early", 0, 2), ("late", 2, 2), ("early", 4, 2), ("late", 6, 2))
VMEM = 63 * 2**20
TILE = 16
UNROLL = 4
ANY = pl.BlockSpec(memory_space=pltpu.HBM)
FACTOR = 100.0


def cost(us):
    return pl.CostEstimate(
        flops=int(us * FACTOR * 1.15e9), bytes_accessed=0, transcendentals=0
    )


F32 = jnp.float32
BF16 = jnp.bfloat16


def dot(left, right, transpose=False):
    dims = (((1,), (1 if transpose else 0,)), ((), ()))
    return lax.dot_general(left, right, dims, preferred_element_type=F32)


def complex_dot(left, right):
    re = dot(left[0], right[0]) - dot(left[1], right[1])
    im = dot(left[0], right[1]) + dot(left[1], right[0])
    return re.astype(BF16), im.astype(BF16)


def complex_dot_adjoint(left, right):
    re = dot(left[0], right[0], True) + dot(left[1], right[1], True)
    im = dot(left[1], right[0], True) - dot(left[0], right[1], True)
    return re.astype(BF16), im.astype(BF16)


def solve_kernel(first, edges, *refs):
    refs = list(refs)
    a_ref, t_ref = refs[:2]
    previous_ref = None if first else refs[2]
    carry = refs.pop()
    low_ref, high_ref = refs[-2:] if edges else (None, None)
    outs = refs[:-2] if edges else refs
    green_ref, density_ref = outs[-2:]
    energies = a_ref.shape[1]
    width = a_ref.shape[-1]
    t = (t_ref[0, 0], t_ref[1, 0])
    if not first:

        @pl.when(pl.program_id(0) == 0)
        def _():
            carry[...] = previous_ref[0]

    rows = lax.broadcasted_iota(jnp.int32, (width, width), 0)
    columns = lax.broadcasted_iota(jnp.int32, (width, width), 1)
    total = jnp.zeros((8, width), F32)
    if first:

        @pl.when(pl.program_id(0) == 0)
        def _():
            couple = complex_dot_adjoint(t, t)
            for e in range(energies):
                carry[0, e], carry[1, e] = couple

        @pl.when(pl.program_id(0) > 0)
        def _():
            for e in range(energies):
                left = complex_dot(t, (carry[0, e], carry[1, e]))
                carry[0, e], carry[1, e] = complex_dot_adjoint(left, t)

    for e in range(energies):
        a = (a_ref[0, e, 0], a_ref[1, e, 0])
        if first:
            couple = (carry[0, e], carry[1, e])
        else:
            left = complex_dot(t, (carry[0, e], carry[1, e]))
            couple = complex_dot_adjoint(left, t)
        inner = complex_dot(a, couple)
        re = a[0].astype(F32) + (dot(inner[0], a[0]) - dot(inner[1], a[1]))
        im = a[1].astype(F32) + (dot(inner[0], a[1]) + dot(inner[1], a[0]))
        re, im = re.astype(BF16), im.astype(BF16)
        carry[0, e] = re
        carry[1, e] = im
        green_ref[0, 0, e] = re
        green_ref[0, 1, e] = im
        if edges and e == 0:
            low_ref[0, 0] = re
            low_ref[0, 1] = im
        if edges and e == energies - 1:
            high_ref[0, 0] = re
            high_ref[0, 1] = im
        diagonal = jnp.where(rows == columns, im.astype(F32), 0.0)
        total = total + jnp.sum(diagonal.reshape(width // 8, 8, width), axis=0)
    density_ref[0] = total


def solve(inverse, coupled, previous, start, count, edges, after=()):
    _, energies, _, total_rows, width = inverse.shape
    first = previous is None
    args = [inverse, coupled]
    in_specs = [
        pl.BlockSpec((2, energies, 1, width, width), lambda i: (0, 0, 0, start + i, 0)),
        pl.BlockSpec((2, 1, width, width), lambda i: (0, 0, start + i, 0)),
    ]
    if not first:
        last = previous.shape[0] - 1
        args.append(previous)
        in_specs.append(
            pl.BlockSpec((1, 2, energies, width, width), lambda i: (last, 0, 0, 0, 0))
        )
    args.extend(after)
    in_specs.extend([ANY] * len(after))
    out_shape = [
        jax.ShapeDtypeStruct((count, 2, energies, width, width), BF16),
        jax.ShapeDtypeStruct((count, 8, width), F32),
    ]
    out_specs = [
        pl.BlockSpec((1, 2, energies, width, width), lambda i: (i, 0, 0, 0, 0)),
        pl.BlockSpec((1, 8, width), lambda i: (i, 0, 0)),
    ]
    if edges:
        for _ in range(2):
            out_shape.append(jax.ShapeDtypeStruct((count, 2, width, width), BF16))
            out_specs.append(pl.BlockSpec((1, 2, width, width), lambda i: (i, 0, 0, 0)))
    return pl.pallas_call(
        functools.partial(solve_kernel, first, edges),
        grid=(count,),
        in_specs=in_specs,
        out_specs=out_specs,
        out_shape=out_shape,
        scratch_shapes=[pltpu.VMEM((2, energies, width, width), BF16)],
        compiler_params=pltpu.CompilerParams(vmem_limit_bytes=VMEM),
        cost_estimate=cost(2.5 * count),
        name="solve",
    )(*args)


def grid_spec(energies, width):
    return pl.BlockSpec((1, 2, energies, width, width), lambda i: (i, 0, 0, 0, 0))


def edge_spec(width):
    return pl.BlockSpec((1, 2, width, width), lambda i: (i, 0, 0, 0))


def member_spec(which, energies, width):
    return pl.BlockSpec(
        (None, 1, 2, energies, width, width), lambda i: (which, i, 0, 0, 0, 0)
    )


def early_members(own, crossed, other):
    count, _, energies, width, _ = own.shape
    spec = grid_spec(energies, width)
    specs = [spec, member_spec(0, energies, width), spec, member_spec(1, energies, width)]
    return [own, other, crossed, other], specs


def late_members(own, before, behind, other):
    count, _, energies, width, _ = own.shape
    edge = edge_spec(width)
    specs = [grid_spec(energies, width), edge, edge, grid_spec(energies + 2, width)]
    return [own, before, behind, other], specs


def join_early_kernel(own_ref, crossed_ref, *refs):
    out_ref = refs[-1]
    out_ref[0] = own_ref[...]
    out_ref[1] = crossed_ref[...]


def join_late_kernel(own_ref, before_ref, behind_ref, *refs):
    out_ref = refs[-1]
    energies = own_ref.shape[2]
    for part in range(2):
        out_ref[0, part, 0] = before_ref[0, part]
        for e in range(energies):
            out_ref[0, part, e + 1] = own_ref[0, part, e]
        out_ref[0, part, energies + 1] = behind_ref[0, part]


def join_early(own, crossed, after):
    count, _, energies, width, _ = own.shape
    spec = grid_spec(energies, width)
    return pl.pallas_call(
        join_early_kernel,
        grid=(count,),
        in_specs=[spec, spec] + [ANY] * len(after),
        out_specs=pl.BlockSpec(
            (2, 1, 2, energies, width, width), lambda i: (0, i, 0, 0, 0, 0)
        ),
        out_shape=jax.ShapeDtypeStruct((2,) + own.shape, BF16),
        compiler_params=pltpu.CompilerParams(vmem_limit_bytes=VMEM),
        cost_estimate=cost(1.3 * count),
        name="join_early",
    )(own, crossed, *after)


def join_late(own, before, behind, after):
    count, _, energies, width, _ = own.shape
    edge = edge_spec(width)
    return pl.pallas_call(
        join_late_kernel,
        grid=(count,),
        in_specs=[grid_spec(energies, width), edge, edge] + [ANY] * len(after),
        out_specs=grid_spec(energies + 2, width),
        out_shape=jax.ShapeDtypeStruct((count, 2, energies + 2, width, width), BF16),
        compiler_params=pltpu.CompilerParams(vmem_limit_bytes=VMEM),
        cost_estimate=cost(1.3 * count),
        name="join_late",
    )(own, before, behind, *after)


def tiles(width):
    steps = width // TILE

    def run(step_body):
        for part in range(2):

            @pl.loop(0, steps, unroll=UNROLL)
            def _(step):
                step_body(part, pl.ds(pl.multiple_of(step * TILE, TILE), TILE))

    return run


def weighted(terms):
    total = None
    for weight, value in terms:
        term = value if weight is None else weight * value
        total = term if total is None else total + term
    return total


def early_edges_kernel(w_ref, *refs):
    grids, (high_ref, low_ref) = refs[:4], refs[-2:]
    last = grids[0].shape[2] - 1
    width = grids[0].shape[-1]
    above = [w_ref[0, 0, j] for j in range(4)]
    below = [w_ref[0, 2, j] for j in range(4)]

    @tiles(width)
    def _(part, rows):
        high = [(above[j], grids[j][0, part, last, rows, :].astype(F32)) for j in range(4)]
        low = [(below[j], grids[j][0, part, 0, rows, :].astype(F32)) for j in range(4)]
        high_ref[0, part, rows, :] = weighted(high).astype(BF16)
        low_ref[0, part, rows, :] = weighted(low).astype(BF16)


def early_edges(weights, members, after):
    args, specs = early_members(*members)
    count, _, energies, width, _ = args[0].shape
    edge = jax.ShapeDtypeStruct((count, 2, width, width), BF16)
    return pl.pallas_call(
        early_edges_kernel,
        grid=(count,),
        in_specs=[pl.BlockSpec(memory_space=pltpu.SMEM)] + specs + [ANY] * len(after),
        out_specs=[edge_spec(width)] * 2,
        out_shape=[edge, edge],
        compiler_params=pltpu.CompilerParams(vmem_limit_bytes=VMEM),
        cost_estimate=cost(1.7 * count),
        name="early_edges",
    )(weights, *args, *after)


def late_line(refs, part, rows):
    own, before, behind, other = refs
    energies = own.shape[2]
    mine = [before[0, part, rows, :]]
    mine += [own[0, part, e, rows, :] for e in range(energies)]
    mine += [behind[0, part, rows, :]]
    theirs = [other[0, part, e, rows, :] for e in range(energies + 2)]
    return [[value.astype(F32) for value in line] for line in (mine, theirs)]


def late_sum_kernel(w_ref, *refs):
    members, out_ref = refs[:4], refs[-1]
    energies, width = members[0].shape[2:4]
    w = [[w_ref[1, o, j] for j in range(2)] for o in range(3)]

    @tiles(width)
    def _(part, rows):
        line = late_line(members, part, rows)
        for e in range(energies):
            terms = [(w[o][j], line[j][e + o]) for j in range(2) for o in range(3)]
            out_ref[0, part, e, rows, :] = weighted(terms).astype(BF16)


def late_sum(weights, members, after):
    args, specs = late_members(*members)
    count, _, energies, width, _ = args[0].shape
    return pl.pallas_call(
        late_sum_kernel,
        grid=(count,),
        in_specs=[pl.BlockSpec(memory_space=pltpu.SMEM)] + specs + [ANY] * len(after),
        out_specs=grid_spec(energies, width),
        out_shape=jax.ShapeDtypeStruct(args[0].shape, BF16),
        compiler_params=pltpu.CompilerParams(vmem_limit_bytes=VMEM),
        cost_estimate=cost(1.8 * count),
        name="late_sum",
    )(weights, *args, *after)


def finish_kernel(late, w_ref, across_ref, down_ref, *refs):
    members, received, out_ref = refs[:4], refs[4 : 5 if late else 6], refs[-1]
    energies, width = members[0].shape[2:4]
    w = [[w_ref[0, o, j] for j in range(4)] for o in range(3)]
    across = across_ref[0]

    @tiles(width)
    def _(part, rows):
        scale = down_ref[rows, :] * across
        if late:
            line = late_line(members, part, rows)
        else:
            line = [
                [None] + [ref[0, part, e, rows, :].astype(F32) for e in range(energies)] + [None]
                for ref in members
            ]
        for e in range(energies):
            terms = [
                (w[o][j], line[j][e + o])
                for j in range(len(line))
                for o in range(3)
                if line[j][e + o] is not None
            ]
            if late:
                terms.append((None, received[0][0, part, e, rows, :].astype(F32)))
            if not late and e == 0:
                terms.append((None, received[0][0, part, rows, :].astype(F32)))
            if not late and e == energies - 1:
                terms.append((None, received[1][0, part, rows, :].astype(F32)))
            out_ref[part, e, 0, rows, :] = (weighted(terms) * scale).astype(BF16)


def finish(sigma, shape, start, weights, across, down, late, members, received, after):
    args, specs = late_members(*members) if late else early_members(*members)
    count, _, energies, width, _ = args[0].shape
    args = [weights, across, down, *args, *received, *after]
    in_specs = [
        pl.BlockSpec(memory_space=pltpu.SMEM),
        pl.BlockSpec((1, 1, width), lambda i: (start + i, 0, 0)),
        pl.BlockSpec((width, 1), lambda i: (start + i, 0)),
    ] + specs
    in_specs += [grid_spec(energies, width)] if late else [edge_spec(width)] * 2
    in_specs += [ANY] * len(after)
    aliases = {}
    if sigma is not None:
        aliases = {len(args): 0}
        args.append(sigma)
        in_specs.append(ANY)
    return pl.pallas_call(
        functools.partial(finish_kernel, late),
        grid=(count,),
        in_specs=in_specs,
        out_specs=pl.BlockSpec(
            (2, energies, 1, width, width), lambda i: (0, 0, 0, start + i, 0)
        ),
        out_shape=jax.ShapeDtypeStruct(shape, BF16),
        input_output_aliases=aliases,
        compiler_params=pltpu.CompilerParams(vmem_limit_bytes=VMEM),
        cost_estimate=cost(2.2 * count),
        name="finish",
    )(*args)


def range_parts_kernel(count, range_ref, *refs):
    densities, out_ref = refs[:count], refs[-1]
    width = densities[0].shape[-1]
    lanes = lax.broadcasted_iota(jnp.int32, (8, 128), 1)
    pieces = []
    base = 0
    for ref in densities:
        for i in range(ref.shape[0]):
            for half in range(width // 128):
                pieces.append((base, ref[i, :, half * 128 : (half + 1) * 128]))
                base += 128

    def one_range(d, begin):
        end = begin + range_ref[d]
        total = jnp.zeros((8, 128), F32)
        for offset, value in pieces:
            inside = (lanes >= begin - offset) & (lanes < end - offset)
            total = total + jnp.where(inside, value, 0.0)
        out_ref[d] = -total
        return end

    lax.fori_loop(0, out_ref.shape[0], one_range, jnp.int32(0))


def range_parts(range_rows, densities, after):
    devices = range_rows.shape[0]
    return pl.pallas_call(
        functools.partial(range_parts_kernel, len(densities)),
        in_specs=[pl.BlockSpec(memory_space=pltpu.SMEM)]
        + [pl.BlockSpec(memory_space=pltpu.VMEM)] * len(densities)
        + [ANY] * len(after),
        out_specs=pl.BlockSpec(memory_space=pltpu.VMEM),
        out_shape=jax.ShapeDtypeStruct((devices, 8, 128), F32),
        compiler_params=pltpu.CompilerParams(vmem_limit_bytes=VMEM),
        cost_estimate=cost(2.2),
        name="range_parts",
    )(range_rows, *densities, *after)


def range_total_kernel(parts_ref, *refs):
    out_ref = refs[-1]
    out_ref[...] = jnp.sum(parts_ref[...], axis=0)


def range_total(received, after):
    return pl.pallas_call(
        range_total_kernel,
        in_specs=[pl.BlockSpec(memory_space=pltpu.VMEM)] + [ANY] * len(after),
        out_specs=pl.BlockSpec(memory_space=pltpu.VMEM),
        out_shape=jax.ShapeDtypeStruct(received.shape[1:], F32),
        compiler_params=pltpu.CompilerParams(vmem_limit_bytes=VMEM),
        cost_estimate=cost(1),
        name="range_total",
    )(received, *after)


def own_weights(shifts, emission, absorption):
    me = lax.axis_index("mom")
    folded = []
    for offset in (-1, 0, 1):
        lower = (shifts == -offset).astype(F32)[:, None, None]
        upper = (shifts == offset).astype(F32)[:, None, None]
        folded.append(jnp.sum(lower * emission + upper * absorption, axis=0))
    folded = jnp.stack(folded)
    momenta = jnp.arange(4, dtype=jnp.int32)
    targets = ((me ^ jnp.array([0, 2], jnp.int32))[:, None] == momenta[None]).astype(F32)
    sources = ((me ^ momenta)[:, None] == momenta[None]).astype(F32)
    picked = folded[None, :, None] * targets[:, None, None, :, None] * sources[None, None, :, None, :]
    return jnp.sum(picked, axis=(3, 4))


def body(
    inverse_blocks,
    coupling_blocks,
    shifts,
    emission_weight,
    absorption_weight,
    deform_potential,
    range_rows,
):
    n_energy = lax.axis_size("energy")
    width = inverse_blocks.shape[-1]
    up = [(i, i + 1) for i in range(n_energy - 1)]
    down = [(i + 1, i) for i in range(n_energy - 1)]

    def send(value, axis, pairs, name):
        with jax.named_scope(name):
            return lax.ppermute(value, axis, pairs)

    def core(value, name):
        return send(value, "mom", [(i, i ^ 1) for i in range(4)], name)

    def pair(value, name):
        return send(value, "mom", [(i, i ^ 2) for i in range(4)], name)

    def halo(low, high, name):
        return (
            send(high, "energy", up, "up" + name),
            send(low, "energy", down, "down" + name),
        )

    weights = own_weights(shifts, emission_weight, absorption_weight)
    across_scale = deform_potential.reshape(-1, 1, width)
    down_scale = deform_potential.reshape(-1, 1)

    def run(chunk, previous, after=()):
        kind, start, count = CHUNKS[chunk]
        return solve(
            inverse_blocks, coupling_blocks, previous, start, count, kind == "late", after
        )

    g0, n0 = run(0, None)
    y0 = pair(g0, "pair0")
    g1, n1, low1, high1 = run(1, g0)
    edges1 = halo(low1, high1, "1")
    g2, n2 = run(2, g1)
    y2 = pair(g2, "pair2")
    g3, n3, low3, high3 = run(3, g2)
    edges3 = halo(low3, high3, "3")
    j0 = join_early(g0, y0, (g3,))
    k0 = core(j0, "core0")
    j1 = join_late(g1, *edges1, (j0,))
    k1 = core(j1, "core1")
    members0 = (g0, y0, k0)
    high0, low0 = early_edges(weights, members0, (j1,))
    members1 = (g1, *edges1, k1)
    total1 = late_sum(weights, members1, (low0,))
    x1 = pair(total1, "pair1")
    edges0 = halo(low0, high0, "0")

    j2 = join_early(g2, y2, (total1,))
    k2 = core(j2, "core2")
    j3 = join_late(g3, *edges3, (j2,))
    k3 = core(j3, "core3")
    members2 = (g2, y2, k2)
    high2, low2 = early_edges(weights, members2, (j3,))
    members3 = (g3, *edges3, k3)
    total3 = late_sum(weights, members3, (low2,))
    x3 = pair(total3, "pair3")
    edges2 = halo(low2, high2, "2")

    parts = range_parts(range_rows, [n0, n1, n2, n3], (total3,))
    received = lax.all_to_all(parts, ("energy", "mom"), split_axis=0, concat_axis=0, tiled=True)
    charge = range_total(received, (x3,))

    sigma = None
    for index, late, members, got, after in (
        (1, True, members1, (x1,), (parts,)),
        (0, False, members0, edges0, ()),
        (3, True, members3, (x3,), ()),
        (2, False, members2, edges2, (charge,)),
    ):
        sigma = finish(
            sigma,
            inverse_blocks.shape,
            CHUNKS[index][1],
            weights,
            across_scale,
            down_scale,
            late,
            members,
            got,
            after,
        )
    return sigma, jnp.sum(charge).reshape(1)


def solution(mesh):
    in_specs = (
        P(None, "energy", "mom", None, None),
        P(None, "mom", None, None),
        P(),
        P(),
        P(),
        P(),
        P(),
    )
    out_specs = (P(None, "energy", "mom", None, None), P(("energy", "mom")))
    return jax.shard_map(body, mesh=mesh, in_specs=in_specs, out_specs=out_specs, check_vma=False)
```

profile of v0, /device:TPU:24, one launch (start us, length us, event | category | flops | bytes accessed | tf_op | source)
XLA Modules:
  0.0 129.3 jit_solution(7976538322875231010)
XLA Ops:
  0.6 5.1 %solve.4 = (bf16[2,2,2,256,256]{4,3,2,1,0:T(8,128)(2,1)}, f32[2,8,256]{2,1,0:T(8,128)}) custom-call(bf16[2,2,1,2048,256]{4,3,2,1,0:T(8,128)(2,1)} %refs_0_.7, bf16[2,1,2048,256]{3,2,1,0:T(8,128)(2,1)} %refs_1_.7), custom_call_target="tpu_custom_call" | custom-call | flops 575000018944 | tf_op jit(solution)/shard_map/solve/pallas_call | solution.py:133
  5.7 1.5 %collective-permute-start.3 = (bf16[2,2,2,256,256]{4,3,2,1,0:T(8,128)(2,1)}, bf16[2,2,2,256,256]{4,3,2,1,0:T(8,128)(2,1)}, u32[]{:S(2)}, u32[]{:S(2)}) collective-permute-start(bf16[2,2,2,256,256]{4,3,2,1,0:T(8,128)(2,1)} %get-tuple-element.18.refs_2_.own_ref.refs_0_), channel_id=1, source_target_pairs={{0,2},{1,3},{2,0},{3,1},{4,6},{5,7},{6,4},{7,5},{8,10},{9,11},{10,... | collective-permute-start | bytes 3145736 | tf_op jit(solution)/shard_map/pair0/ppermute | solution.py:462
  7.2 6.2 %solve.5 = (bf16[2,2,2,256,256]{4,3,2,1,0:T(8,128)(2,1)}, f32[2,8,256]{2,1,0:T(8,128)}, bf16[2,2,256,256]{3,2,1,0:T(8,128)(2,1)}, bf16[2,2,256,256]{3,2,1,0:T(8,128)(2,1)}) custom-call(bf16[2,2,1,2048,256]{4,3,2,1,0:T(8,128)(2,1)} %refs_0_.7, bf16[2,1,2048,256]{3,2,1,0:T(8,128)(2,1)} %refs_1_.7, ...), custom_call_target="tpu_custom_call" | custom-call | flops 575000018944 | tf_op jit(solution)/shard_map/solve/pallas_call | solution.py:133
  13.4 3.4 %collective-permute-start.1 = (bf16[2,2,256,256]{3,2,1,0:T(8,128)(2,1)}, bf16[2,2,256,256]{3,2,1,0:T(8,128)(2,1)}, u32[]{:S(2)}, u32[]{:S(2)}) collective-permute-start(bf16[2,2,256,256]{3,2,1,0:T(8,128)(2,1)} %get-tuple-element.21), channel_id=1, source_target_pairs={{0,4},{4,8},{8,12},{12,16},{16,20},{20,24},{24,28},{1,5},{5,9},{9,... | collective-permute-start | bytes 1572872 | tf_op jit(solution)/shard_map/up1/ppermute | solution.py:462
  16.8 3.3 %collective-permute-start.2 = (bf16[2,2,256,256]{3,2,1,0:T(8,128)(2,1)}, bf16[2,2,256,256]{3,2,1,0:T(8,128)(2,1)}, u32[]{:S(2)}, u32[]{:S(2)}) collective-permute-start(bf16[2,2,256,256]{3,2,1,0:T(8,128)(2,1)} %get-tuple-element.22), channel_id=1, source_target_pairs={{4,0},{8,4},{12,8},{16,12},{20,16},{24,20},{28,24},{5,1},{9,5},{13... | collective-permute-start | bytes 1572872 | tf_op jit(solution)/shard_map/down1/ppermute | solution.py:462
  20.1 6.0 %solve.6 = (bf16[2,2,2,256,256]{4,3,2,1,0:T(8,128)(2,1)}, f32[2,8,256]{2,1,0:T(8,128)}) custom-call(bf16[2,2,1,2048,256]{4,3,2,1,0:T(8,128)(2,1)} %refs_0_.7, bf16[2,1,2048,256]{3,2,1,0:T(8,128)(2,1)} %refs_1_.7, bf16[2,2,2,256,256]{4,3,2,1,0:T(8,128)(2,1)} %get-tuple-element.19.refs_2_.own_ref.refs_0_), custom_call_target="tpu_custom_call" | custom-call | flops 575000018944 | tf_op jit(solution)/shard_map/solve/pallas_call | solution.py:133
  26.1 0.5 collective-permute-start
  26.6 0.0 copy-start.3
  26.6 6.2 %solve.7 = (bf16[2,2,2,256,256]{4,3,2,1,0:T(8,128)(2,1)}, f32[2,8,256]{2,1,0:T(8,128)}, bf16[2,2,256,256]{3,2,1,0:T(8,128)(2,1)}, bf16[2,2,256,256]{3,2,1,0:T(8,128)(2,1)}) custom-call(bf16[2,2,1,2048,256]{4,3,2,1,0:T(8,128)(2,1)} %refs_0_.7, bf16[2,1,2048,256]{3,2,1,0:T(8,128)(2,1)} %refs_1_.7, ...), custom_call_target="tpu_custom_call" | custom-call | flops 575000018944 | tf_op jit(solution)/shard_map/solve/pallas_call | solution.py:133
  32.8 3.3 %collective-permute-start.7 = (bf16[2,2,256,256]{3,2,1,0:T(8,128)(2,1)}, bf16[2,2,256,256]{3,2,1,0:T(8,128)(2,1)}, u32[]{:S(2)}, u32[]{:S(2)}) collective-permute-start(bf16[2,2,256,256]{3,2,1,0:T(8,128)(2,1)} %get-tuple-element.25), channel_id=1, source_target_pairs={{0,4},{4,8},{8,12},{12,16},{16,20},{20,24},{24,28},{1,5},{5,9},{9,... | collective-permute-start | bytes 1572872 | tf_op jit(solution)/shard_map/up3/ppermute | solution.py:462
  36.1 0.0 copy-done.3
  36.2 0.0 copy-done
  36.2 1.4 %copy.20.down_ref = f32[2048,1]{1,0:T(8,128)} copy(f32[2048,1]{0,1:T(1,128)S(1)} %bitcast.10) | data formatting | bytes 16384 | tf_op jit(solution)/shard_map/reshape | solution.py:478
  37.6 0.0 copy-done.1
  37.6 0.0 copy-done.2
  37.6 0.1 add_reduce_fusion.1
  37.7 0.1 compare_convert_fusion
  37.8 0.1 fusion
  37.9 0.1 broadcast_multiply_fusion
  37.9 0.7 multiply_reduce_fusion.w_ref
  38.6 0.0 collective-permute-done.3.crossed_ref.refs_2_
  38.6 3.5 %collective-permute-start.8 = (bf16[2,2,256,256]{3,2,1,0:T(8,128)(2,1)}, bf16[2,2,256,256]{3,2,1,0:T(8,128)(2,1)}, u32[]{:S(2)}, u32[]{:S(2)}) collective-permute-start(bf16[2,2,256,256]{3,2,1,0:T(8,128)(2,1)} %get-tuple-element.26), channel_id=1, source_target_pairs={{4,0},{8,4},{12,8},{16,12},{20,16},{24,20},{28,24},{5,1},{9,5},{13... | collective-permute-start | bytes 1572872 | tf_op jit(solution)/shard_map/down3/ppermute | solution.py:462
  42.1 2.6 %join_early.2.refs_0_ = bf16[2,2,2,2,256,256]{5,4,3,2,1,0:T(8,128)(2,1)} custom-call(bf16[2,2,2,256,256]{4,3,2,1,0:T(8,128)(2,1)} %get-tuple-element.18.refs_2_.own_ref.refs_0_, bf16[2,2,2,256,256]{4,3,2,1,0:T(8,128)(2,1)} %collective-permute-done.3.crossed_ref.refs_2_, bf16[2,2,2,256,256]{4,3,2,1,0:T(8,128)(2,1)} %get-tuple-element.23.refs_0_.own_ref), custom_call_target="tpu_custom_call" | custom-call | flops 299000004608 | tf_op jit(solution)/shard_map/join_early/pallas_call | solution.py:193
  44.7 0.0 collective-permute-done.1.before_ref.refs_1_
  44.7 0.0 collective-permute-start.5
  44.7 7.7 %collective-permute-done.2.behind_ref.refs_2_ = bf16[2,2,256,256]{3,2,1,0:T(8,128)(2,1)} collective-permute-done((bf16[2,2,256,256]{3,2,1,0:T(8,128)(2,1)}, bf16[2,2,256,256]{3,2,1,0:T(8,128)(2,1)}, u32[]{:S(2)}, u32[]{:S(2)}) %collective-permute-start.2) | collective-permute-done | bytes 524320 | tf_op jit(solution)/shard_map/down1/ppermute | solution.py:462
  52.4 2.6 %join_late.2.refs_4_ = bf16[2,2,4,256,256]{4,3,2,1,0:T(8,128)(2,1)} custom-call(bf16[2,2,2,256,256]{4,3,2,1,0:T(8,128)(2,1)} %get-tuple-element.19.refs_2_.own_ref.refs_0_, bf16[2,2,256,256]{3,2,1,0:T(8,128)(2,1)} %collective-permute-done.1.before_ref.refs_1_, bf16[2,2,256,256]{3,2,1,0:T(8,128)(2,1)} %collective-permute-done.2.behind_ref.refs_2_, ...), custom_call_target="tpu_custom_call" | custom-call | flops 299000004608 | tf_op jit(solution)/shard_map/join_late/pallas_call | solution.py:210
  55.0 0.0 collective-permute-start.4
  55.0 0.0 collective-permute-done.5.refs_1_.refs_3_
  55.0 3.5 %early_edges.2 = (bf16[2,2,256,256]{3,2,1,0:T(8,128)(2,1)}, bf16[2,2,256,256]{3,2,1,0:T(8,128)(2,1)}) custom-call(f32[2,3,4]{2,1,0:T(4,128)} %multiply_reduce_fusion.w_ref, bf16[2,2,2,256,256]{4,3,2,1,0:T(8,128)(2,1)} %get-tuple-element.18.refs_2_.own_ref.refs_0_, bf16[2,2,2,2,256,256]{5,4,3,2,1,0:T(8,128)(2,1)} %collective-permute-done.5.refs_1_.refs_3_, ...), custom_call_target="tpu_custom_call" | custom-call | flops 390999998464 | tf_op jit(solution)/shard_map/early_edges/pallas_call | solution.py:262
  58.5 1.9 %collective-permute-start.13 = (bf16[2,2,256,256]{3,2,1,0:T(8,128)(2,1)}, bf16[2,2,256,256]{3,2,1,0:T(8,128)(2,1)}, u32[]{:S(2)}, u32[]{:S(2)}) collective-permute-start(bf16[2,2,256,256]{3,2,1,0:T(8,128)(2,1)} %get-tuple-element.33), channel_id=1, source_target_pairs={{0,4},{4,8},{8,12},{12,16},{16,20},{20,24},{24,28},{1,5},{5,9},{9,... | collective-permute-start | bytes 1572872 | tf_op jit(solution)/shard_map/up0/ppermute | solution.py:462
  60.4 0.0 collective-permute-done.4.refs_3_
  60.4 4.8 %collective-permute-start.14 = (bf16[2,2,256,256]{3,2,1,0:T(8,128)(2,1)}, bf16[2,2,256,256]{3,2,1,0:T(8,128)(2,1)}, u32[]{:S(2)}, u32[]{:S(2)}) collective-permute-start(bf16[2,2,256,256]{3,2,1,0:T(8,128)(2,1)} %get-tuple-element.24.refs_4_), channel_id=1, source_target_pairs={{4,0},{8,4},{12,8},{16,12},{20,16},{24,20},{28,24},{5,1},{9,5},{13... | collective-permute-start | bytes 1572872 | tf_op jit(solution)/shard_map/down0/ppermute | solution.py:462
  65.2 3.6 %late_sum.2.refs_0_ = bf16[2,2,2,256,256]{4,3,2,1,0:T(8,128)(2,1)} custom-call(f32[2,3,4]{2,1,0:T(4,128)} %multiply_reduce_fusion.w_ref, bf16[2,2,2,256,256]{4,3,2,1,0:T(8,128)(2,1)} %get-tuple-element.19.refs_2_.own_ref.refs_0_, bf16[2,2,256,256]{3,2,1,0:T(8,128)(2,1)} %collective-permute-done.1.before_ref.refs_1_, ...), custom_call_target="tpu_custom_call" | custom-call | flops 413999988736 | tf_op jit(solution)/shard_map/late_sum/pallas_call | solution.py:300
  68.9 0.0 collective-permute-done.crossed_ref.refs_2_
  68.9 0.5 collective-permute-start.15
  69.4 2.6 %join_early.3.refs_0_ = bf16[2,2,2,2,256,256]{5,4,3,2,1,0:T(8,128)(2,1)} custom-call(bf16[2,2,2,256,256]{4,3,2,1,0:T(8,128)(2,1)} %get-tuple-element.20.refs_2_.own_ref.refs_0_, bf16[2,2,2,256,256]{4,3,2,1,0:T(8,128)(2,1)} %collective-permute-done.crossed_ref.refs_2_, bf16[2,2,2,256,256]{4,3,2,1,0:T(8,128)(2,1)} %late_sum.2.refs_0_), custom_call_target="tpu_custom_call" | custom-call | flops 299000004608 | tf_op jit(solution)/shard_map/join_early/pallas_call | solution.py:193
  71.9 0.0 collective-permute-done.7.before_ref.refs_1_
  71.9 0.0 collective-permute-start.6
  71.9 0.0 collective-permute-done.8.behind_ref.refs_2_
  72.0 2.6 %join_late.3.refs_4_ = bf16[2,2,4,256,256]{4,3,2,1,0:T(8,128)(2,1)} custom-call(bf16[2,2,2,256,256]{4,3,2,1,0:T(8,128)(2,1)} %get-tuple-element.23.refs_0_.own_ref, bf16[2,2,256,256]{3,2,1,0:T(8,128)(2,1)} %collective-permute-done.7.before_ref.refs_1_, bf16[2,2,256,256]{3,2,1,0:T(8,128)(2,1)} %collective-permute-done.8.behind_ref.refs_2_, ...), custom_call_target="tpu_custom_call" | custom-call | flops 299000004608 | tf_op jit(solution)/shard_map/join_late/pallas_call | solution.py:210
  74.6 0.5 collective-permute-start.11
  75.1 1.4 %collective-permute-done.6.refs_1_.refs_3_ = bf16[2,2,2,2,256,256]{5,4,3,2,1,0:T(8,128)(2,1)} collective-permute-done((bf16[2,2,2,2,256,256]{5,4,3,2,1,0:T(8,128)(2,1)}, bf16[2,2,2,2,256,256]{5,4,3,2,1,0:T(8,128)(2,1)}, u32[]{:S(2)}, u32[]{:S(2)}) %collective-permute-start.6) | collective-permute-done | bytes 2097184 | tf_op jit(solution)/shard_map/core2/ppermute | solution.py:462
  76.4 3.4 %early_edges.3 = (bf16[2,2,256,256]{3,2,1,0:T(8,128)(2,1)}, bf16[2,2,256,256]{3,2,1,0:T(8,128)(2,1)}) custom-call(f32[2,3,4]{2,1,0:T(4,128)} %multiply_reduce_fusion.w_ref, bf16[2,2,2,256,256]{4,3,2,1,0:T(8,128)(2,1)} %get-tuple-element.20.refs_2_.own_ref.refs_0_, bf16[2,2,2,2,256,256]{5,4,3,2,1,0:T(8,128)(2,1)} %collective-permute-done.6.refs_1_.refs_3_, ...), custom_call_target="tpu_custom_call" | custom-call | flops 390999998464 | tf_op jit(solution)/shard_map/early_edges/pallas_call | solution.py:262
  79.9 1.9 %collective-permute-start.10 = (bf16[2,2,256,256]{3,2,1,0:T(8,128)(2,1)}, bf16[2,2,256,256]{3,2,1,0:T(8,128)(2,1)}, u32[]{:S(2)}, u32[]{:S(2)}) collective-permute-start(bf16[2,2,256,256]{3,2,1,0:T(8,128)(2,1)} %get-tuple-element.28.refs_4_), channel_id=1, source_target_pairs={{4,0},{8,4},{12,8},{16,12},{20,16},{24,20},{28,24},{5,1},{9,5},{13... | collective-permute-start | bytes 1572872 | tf_op jit(solution)/shard_map/down2/ppermute | solution.py:462
  81.8 0.0 collective-permute-done.11.refs_3_
  81.8 3.6 %late_sum.3.refs_4_ = bf16[2,2,2,256,256]{4,3,2,1,0:T(8,128)(2,1)} custom-call(f32[2,3,4]{2,1,0:T(4,128)} %multiply_reduce_fusion.w_ref, bf16[2,2,2,256,256]{4,3,2,1,0:T(8,128)(2,1)} %get-tuple-element.23.refs_0_.own_ref, bf16[2,2,256,256]{3,2,1,0:T(8,128)(2,1)} %collective-permute-done.7.before_ref.refs_1_, ...), custom_call_target="tpu_custom_call" | custom-call | flops 413999988736 | tf_op jit(solution)/shard_map/late_sum/pallas_call | solution.py:300
  85.4 1.5 %collective-permute-start.12 = (bf16[2,2,2,256,256]{4,3,2,1,0:T(8,128)(2,1)}, bf16[2,2,2,256,256]{4,3,2,1,0:T(8,128)(2,1)}, u32[]{:S(2)}, u32[]{:S(2)}) collective-permute-start(bf16[2,2,2,256,256]{4,3,2,1,0:T(8,128)(2,1)} %late_sum.3.refs_4_), channel_id=1, source_target_pairs={{0,2},{1,3},{2,0},{3,1},{4,6},{5,7},{6,4},{7,5},{8,10},{9,11},{10,... | collective-permute-start | bytes 3145736 | tf_op jit(solution)/shard_map/pair3/ppermute | solution.py:462
  86.9 2.2 %range_parts.1.refs_5_ = f32[32,8,128]{2,1,0:T(8,128)} custom-call(s32[32]{0:T(128)} %range_ref.1, f32[2,8,256]{2,1,0:T(8,128)} %get-tuple-element.29.refs_0_, f32[2,8,256]{2,1,0:T(8,128)} %get-tuple-element.30.refs_1_, f32[2,8,256]{2,1,0:T(8,128)} %get-tuple-element.31.refs_2_, f32[2,8,256]{2,1,0:T(8,128)} %get-tuple-element.32.refs_3_, ...), custom_call_target="tpu_custom_call" | custom-call | flops 253000007680 | tf_op jit(solution)/shard_map/range_parts/pallas_call | solution.py:401
  89.1 6.3 %all-to-all-start = ((f32[32,8,128]{2,1,0:T(8,128)}), f32[32,8,128]{2,1,0:T(8,128)}, u32[]{:S(2)}, u32[]{:S(2)}) async-start(f32[32,8,128]{2,1,0:T(8,128)} %range_parts.1.refs_5_), calls=%async_computation | async-start | bytes 262144 | tf_op jit(solution)/shard_map/all_to_all | solution.py:517
  95.4 0.0 collective-permute-done.15.refs_4_
  95.5 3.4 %collective-permute-start.9 = (bf16[2,2,256,256]{3,2,1,0:T(8,128)(2,1)}, bf16[2,2,256,256]{3,2,1,0:T(8,128)(2,1)}, u32[]{:S(2)}, u32[]{:S(2)}) collective-permute-start(bf16[2,2,256,256]{3,2,1,0:T(8,128)(2,1)} %get-tuple-element.27), channel_id=1, source_target_pairs={{0,4},{4,8},{8,12},{12,16},{16,20},{20,24},{24,28},{1,5},{5,9},{9,... | collective-permute-start | bytes 1572872 | tf_op jit(solution)/shard_map/up2/ppermute | solution.py:462
  98.9 4.2 %finish.4.refs_6_ = bf16[2,2,1,2048,256]{4,3,2,1,0:T(8,128)(2,1)} custom-call(f32[2,3,4]{2,1,0:T(4,128)} %multiply_reduce_fusion.w_ref, f32[8,1,256]{2,1,0:T(1,128)} %bitcast.6, f32[2048,1]{1,0:T(8,128)} %copy.20.down_ref, bf16[2,2,2,256,256]{4,3,2,1,0:T(8,128)(2,1)} %get-tuple-element.19.refs_2_.own_ref.refs_0_, ...), custom_call_target="tpu_custom_call" | custom-call | flops 506000015360 | tf_op jit(solution)/shard_map/finish/pallas_call | solution.py:360
  103.0 0.0 collective-permute-done.13.refs_4_
  103.0 0.0 collective-permute-done.14.refs_5_
  103.0 4.4 %finish.5.refs_5_ = bf16[2,2,1,2048,256]{4,3,2,1,0:T(8,128)(2,1)} custom-call(f32[2,3,4]{2,1,0:T(4,128)} %multiply_reduce_fusion.w_ref, f32[8,1,256]{2,1,0:T(1,128)} %bitcast.7, f32[2048,1]{1,0:T(8,128)} %copy.20.down_ref, bf16[2,2,2,256,256]{4,3,2,1,0:T(8,128)(2,1)} %get-tuple-element.18.refs_2_.own_ref.refs_0_, ...), custom_call_target="tpu_custom_call", output_to_operand_aliasing={{}: (9, {})} | custom-call | flops 506000015360 | tf_op jit(solution)/shard_map/finish/pallas_call | solution.py:360
  107.4 10.6 %collective-permute-done.12.refs_0_.refs_4_ = bf16[2,2,2,256,256]{4,3,2,1,0:T(8,128)(2,1)} collective-permute-done((bf16[2,2,2,256,256]{4,3,2,1,0:T(8,128)(2,1)}, bf16[2,2,2,256,256]{4,3,2,1,0:T(8,128)(2,1)}, u32[]{:S(2)}, u32[]{:S(2)}) %collective-permute-start.12) | collective-permute-done | bytes 1048608 | tf_op jit(solution)/shard_map/pair3/ppermute | solution.py:462
  118.0 4.1 %finish.6.refs_7_ = bf16[2,2,1,2048,256]{4,3,2,1,0:T(8,128)(2,1)} custom-call(f32[2,3,4]{2,1,0:T(4,128)} %multiply_reduce_fusion.w_ref, f32[8,1,256]{2,1,0:T(1,128)} %bitcast.8, f32[2048,1]{1,0:T(8,128)} %copy.20.down_ref, bf16[2,2,2,256,256]{4,3,2,1,0:T(8,128)(2,1)} %get-tuple-element.23.refs_0_.own_ref, ...), custom_call_target="tpu_custom_call", output_to_operand_aliasing={{}: (8, {})} | custom-call | flops 506000015360 | tf_op jit(solution)/shard_map/finish/pallas_call | solution.py:360
  122.1 0.0 all-to-all-done.parts_ref
  122.1 1.5 %range_total.1.refs_6_ = f32[8,128]{1,0:T(8,128)} custom-call(f32[32,8,128]{2,1,0:T(8,128)} %all-to-all-done.parts_ref, bf16[2,2,2,256,256]{4,3,2,1,0:T(8,128)(2,1)} %collective-permute-done.12.refs_0_.refs_4_), custom_call_target="tpu_custom_call" | custom-call | flops 115000000512 | tf_op jit(solution)/shard_map/range_total/pallas_call | solution.py:420
  123.6 1.3 reduce_sum.49
  124.9 0.0 collective-permute-done.9.refs_4_
  124.9 0.0 collective-permute-done.10.refs_5_
  124.9 4.4 %finish.7 = bf16[2,2,1,2048,256]{4,3,2,1,0:T(8,128)(2,1)} custom-call(f32[2,3,4]{2,1,0:T(4,128)} %multiply_reduce_fusion.w_ref, f32[8,1,256]{2,1,0:T(1,128)} %bitcast.9, f32[2048,1]{1,0:T(8,128)} %copy.20.down_ref, bf16[2,2,2,256,256]{4,3,2,1,0:T(8,128)(2,1)} %get-tuple-element.20.refs_2_.own_ref.refs_0_, ...), custom_call_target="tpu_custom_call", output_to_operand_aliasing={{}: (10, {})} | custom-call | flops 506000015360 | tf_op jit(solution)/shard_map/finish/pallas_call | solution.py:360
  (7 shorter events, 0.0 us)
Async XLA Ops:
  5.7 32.9 %collective-permute-start.3 = (bf16[2,2,2,256,256]{4,3,2,1,0:T(8,128)(2,1)}, bf16[2,2,2,256,256]{4,3,2,1,0:T(8,128)(2,1)}, u32[]{:S(2)}, u32[]{:S(2)}) collective-permute-start(bf16[2,2,2,256,256]{4,3,2,1,0:T(8,128)(2,1)} %get-tuple-element.18.refs_2_.own_ref.refs_0_), channel_id=1, source_target_pairs={{0,2},{1,3},{2,0},{3,1},{4,6},{5,7},{6,4},{7,5},{8,10},{9,11},{10,... | collective-permute-start | bytes 3145736 | tf_op jit(solution)/shard_map/pair0/ppermute | solution.py:462
  13.4 31.3 %collective-permute-start.1 = (bf16[2,2,256,256]{3,2,1,0:T(8,128)(2,1)}, bf16[2,2,256,256]{3,2,1,0:T(8,128)(2,1)}, u32[]{:S(2)}, u32[]{:S(2)}) collective-permute-start(bf16[2,2,256,256]{3,2,1,0:T(8,128)(2,1)} %get-tuple-element.21), channel_id=1, source_target_pairs={{0,4},{4,8},{8,12},{12,16},{16,20},{20,24},{24,28},{1,5},{5,9},{9,... | collective-permute-start | bytes 1572872 | tf_op jit(solution)/shard_map/up1/ppermute | solution.py:462
  16.8 35.7 %collective-permute-start.2 = (bf16[2,2,256,256]{3,2,1,0:T(8,128)(2,1)}, bf16[2,2,256,256]{3,2,1,0:T(8,128)(2,1)}, u32[]{:S(2)}, u32[]{:S(2)}) collective-permute-start(bf16[2,2,256,256]{3,2,1,0:T(8,128)(2,1)} %get-tuple-element.22), channel_id=1, source_target_pairs={{4,0},{8,4},{12,8},{16,12},{20,16},{24,20},{28,24},{5,1},{9,5},{13... | collective-permute-start | bytes 1572872 | tf_op jit(solution)/shard_map/down1/ppermute | solution.py:462
  26.1 42.7 %collective-permute-start = (bf16[2,2,2,256,256]{4,3,2,1,0:T(8,128)(2,1)}, bf16[2,2,2,256,256]{4,3,2,1,0:T(8,128)(2,1)}, u32[]{:S(2)}, u32[]{:S(2)}) collective-permute-start(bf16[2,2,2,256,256]{4,3,2,1,0:T(8,128)(2,1)} %get-tuple-element.20.refs_2_.own_ref.refs_0_), channel_id=1, source_target_pairs={{0,2},{1,3},{2,0},{3,1},{4,6},{5,7},{6,4},{7,5},{8,10},{9,11},{10,... | collective-permute-start | bytes 3145736 | tf_op jit(solution)/shard_map/pair2/ppermute | solution.py:462
  26.6 9.5 %copy-start.3 = (s32[4]{0:T(128)S(1)}, s32[4]{0:T(128)}, u32[]{:S(2)}) copy-start(s32[4]{0:T(128)} %param.10) | copy-start | bytes 52
  26.6 9.5 %copy-start = (f32[2048]{0:T(1024)S(1)}, f32[2048]{0:T(1024)}, u32[]{:S(2)}) copy-start(f32[2048]{0:T(1024)} %param.13) | copy-start | bytes 24580
  26.6 11.0 %copy-start.1 = (f32[4,4,4]{2,1,0:T(4,128)S(1)}, f32[4,4,4]{2,1,0:T(4,128)}, u32[]{:S(2)}) copy-start(f32[4,4,4]{2,1,0:T(4,128)} %param.12) | copy-start | bytes 772
  26.6 11.0 %copy-start.2 = (f32[4,4,4]{2,1,0:T(4,128)S(1)}, f32[4,4,4]{2,1,0:T(4,128)}, u32[]{:S(2)}) copy-start(f32[4,4,4]{2,1,0:T(4,128)} %param.11) | copy-start | bytes 772
  32.8 39.1 %collective-permute-start.7 = (bf16[2,2,256,256]{3,2,1,0:T(8,128)(2,1)}, bf16[2,2,256,256]{3,2,1,0:T(8,128)(2,1)}, u32[]{:S(2)}, u32[]{:S(2)}) collective-permute-start(bf16[2,2,256,256]{3,2,1,0:T(8,128)(2,1)} %get-tuple-element.25), channel_id=1, source_target_pairs={{0,4},{4,8},{8,12},{12,16},{16,20},{20,24},{24,28},{1,5},{5,9},{9,... | collective-permute-start | bytes 1572872 | tf_op jit(solution)/shard_map/up3/ppermute | solution.py:462
  38.6 33.3 %collective-permute-start.8 = (bf16[2,2,256,256]{3,2,1,0:T(8,128)(2,1)}, bf16[2,2,256,256]{3,2,1,0:T(8,128)(2,1)}, u32[]{:S(2)}, u32[]{:S(2)}) collective-permute-start(bf16[2,2,256,256]{3,2,1,0:T(8,128)(2,1)} %get-tuple-element.26), channel_id=1, source_target_pairs={{4,0},{8,4},{12,8},{16,12},{20,16},{24,20},{28,24},{5,1},{9,5},{13... | collective-permute-start | bytes 1572872 | tf_op jit(solution)/shard_map/down3/ppermute | solution.py:462
  44.7 10.3 %collective-permute-start.5 = (bf16[2,2,2,2,256,256]{5,4,3,2,1,0:T(8,128)(2,1)}, bf16[2,2,2,2,256,256]{5,4,3,2,1,0:T(8,128)(2,1)}, u32[]{:S(2)}, u32[]{:S(2)}) collective-permute-start(bf16[2,2,2,2,256,256]{5,4,3,2,1,0:T(8,128)(2,1)} %join_early.2.refs_0_), channel_id=1, source_target_pairs={{0,1},{1,0},{2,3},{3,2},{4,5},{5,4},{6,7},{7,6},{8,9},{9,8},{10,11... | collective-permute-start | bytes 6291464 | tf_op jit(solution)/shard_map/core0/ppermute | solution.py:462
  55.0 5.4 %collective-permute-start.4 = (bf16[2,2,4,256,256]{4,3,2,1,0:T(8,128)(2,1)}, bf16[2,2,4,256,256]{4,3,2,1,0:T(8,128)(2,1)}, u32[]{:S(2)}, u32[]{:S(2)}) collective-permute-start(bf16[2,2,4,256,256]{4,3,2,1,0:T(8,128)(2,1)} %join_late.2.refs_4_), channel_id=1, source_target_pairs={{0,1},{1,0},{2,3},{3,2},{4,5},{5,4},{6,7},{7,6},{8,9},{9,8},{10,11... | collective-permute-start | bytes 6291464 | tf_op jit(solution)/shard_map/core1/ppermute | solution.py:462
  58.5 44.5 %collective-permute-start.13 = (bf16[2,2,256,256]{3,2,1,0:T(8,128)(2,1)}, bf16[2,2,256,256]{3,2,1,0:T(8,128)(2,1)}, u32[]{:S(2)}, u32[]{:S(2)}) collective-permute-start(bf16[2,2,256,256]{3,2,1,0:T(8,128)(2,1)} %get-tuple-element.33), channel_id=1, source_target_pairs={{0,4},{4,8},{8,12},{12,16},{16,20},{20,24},{24,28},{1,5},{5,9},{9,... | collective-permute-start | bytes 1572872 | tf_op jit(solution)/shard_map/up0/ppermute | solution.py:462
  60.4 42.6 %collective-permute-start.14 = (bf16[2,2,256,256]{3,2,1,0:T(8,128)(2,1)}, bf16[2,2,256,256]{3,2,1,0:T(8,128)(2,1)}, u32[]{:S(2)}, u32[]{:S(2)}) collective-permute-start(bf16[2,2,256,256]{3,2,1,0:T(8,128)(2,1)} %get-tuple-element.24.refs_4_), channel_id=1, source_target_pairs={{4,0},{8,4},{12,8},{16,12},{20,16},{24,20},{28,24},{5,1},{9,5},{13... | collective-permute-start | bytes 1572872 | tf_op jit(solution)/shard_map/down0/ppermute | solution.py:462
  68.9 26.6 %collective-permute-start.15 = (bf16[2,2,2,256,256]{4,3,2,1,0:T(8,128)(2,1)}, bf16[2,2,2,256,256]{4,3,2,1,0:T(8,128)(2,1)}, u32[]{:S(2)}, u32[]{:S(2)}) collective-permute-start(bf16[2,2,2,256,256]{4,3,2,1,0:T(8,128)(2,1)} %late_sum.2.refs_0_), channel_id=1, source_target_pairs={{0,2},{1,3},{2,0},{3,1},{4,6},{5,7},{6,4},{7,5},{8,10},{9,11},{10,... | collective-permute-start | bytes 3145736 | tf_op jit(solution)/shard_map/pair1/ppermute | solution.py:462
  71.9 4.5 %collective-permute-start.6 = (bf16[2,2,2,2,256,256]{5,4,3,2,1,0:T(8,128)(2,1)}, bf16[2,2,2,2,256,256]{5,4,3,2,1,0:T(8,128)(2,1)}, u32[]{:S(2)}, u32[]{:S(2)}) collective-permute-start(bf16[2,2,2,2,256,256]{5,4,3,2,1,0:T(8,128)(2,1)} %join_early.3.refs_0_), channel_id=1, source_target_pairs={{0,1},{1,0},{2,3},{3,2},{4,5},{5,4},{6,7},{7,6},{8,9},{9,8},{10,11... | collective-permute-start | bytes 6291464 | tf_op jit(solution)/shard_map/core2/ppermute | solution.py:462
  74.6 7.2 %collective-permute-start.11 = (bf16[2,2,4,256,256]{4,3,2,1,0:T(8,128)(2,1)}, bf16[2,2,4,256,256]{4,3,2,1,0:T(8,128)(2,1)}, u32[]{:S(2)}, u32[]{:S(2)}) collective-permute-start(bf16[2,2,4,256,256]{4,3,2,1,0:T(8,128)(2,1)} %join_late.3.refs_4_), channel_id=1, source_target_pairs={{0,1},{1,0},{2,3},{3,2},{4,5},{5,4},{6,7},{7,6},{8,9},{9,8},{10,11... | collective-permute-start | bytes 6291464 | tf_op jit(solution)/shard_map/core3/ppermute | solution.py:462
  79.9 45.1 %collective-permute-start.10 = (bf16[2,2,256,256]{3,2,1,0:T(8,128)(2,1)}, bf16[2,2,256,256]{3,2,1,0:T(8,128)(2,1)}, u32[]{:S(2)}, u32[]{:S(2)}) collective-permute-start(bf16[2,2,256,256]{3,2,1,0:T(8,128)(2,1)} %get-tuple-element.28.refs_4_), channel_id=1, source_target_pairs={{4,0},{8,4},{12,8},{16,12},{20,16},{24,20},{28,24},{5,1},{9,5},{13... | collective-permute-start | bytes 1572872 | tf_op jit(solution)/shard_map/down2/ppermute | solution.py:462
  85.4 32.6 %collective-permute-start.12 = (bf16[2,2,2,256,256]{4,3,2,1,0:T(8,128)(2,1)}, bf16[2,2,2,256,256]{4,3,2,1,0:T(8,128)(2,1)}, u32[]{:S(2)}, u32[]{:S(2)}) collective-permute-start(bf16[2,2,2,256,256]{4,3,2,1,0:T(8,128)(2,1)} %late_sum.3.refs_4_), channel_id=1, source_target_pairs={{0,2},{1,3},{2,0},{3,1},{4,6},{5,7},{6,4},{7,5},{8,10},{9,11},{10,... | collective-permute-start | bytes 3145736 | tf_op jit(solution)/shard_map/pair3/ppermute | solution.py:462
  89.1 33.0 %all-to-all-start = ((f32[32,8,128]{2,1,0:T(8,128)}), f32[32,8,128]{2,1,0:T(8,128)}, u32[]{:S(2)}, u32[]{:S(2)}) async-start(f32[32,8,128]{2,1,0:T(8,128)} %range_parts.1.refs_5_), calls=%async_computation | async-start | bytes 262144 | tf_op jit(solution)/shard_map/all_to_all | solution.py:517
  95.5 29.5 %collective-permute-start.9 = (bf16[2,2,256,256]{3,2,1,0:T(8,128)(2,1)}, bf16[2,2,256,256]{3,2,1,0:T(8,128)(2,1)}, u32[]{:S(2)}, u32[]{:S(2)}) collective-permute-start(bf16[2,2,256,256]{3,2,1,0:T(8,128)(2,1)} %get-tuple-element.27), channel_id=1, source_target_pairs={{0,4},{4,8},{8,12},{12,16},{16,20},{20,24},{24,28},{1,5},{5,9},{9,... | collective-permute-start | bytes 1572872 | tf_op jit(solution)/shard_map/up2/ppermute | solution.py:462
where the time goes:
time: 130 us; the launch traced here: 129 us
  Pallas kernels  68.7 us (53%)
  starting transfers between devices  36.3 us (28%)
  waiting for transfers between devices  19.7 us (15%)
  other arithmetic  2.32 us (2%)
  local copies, waits for them, and re-layouts  1.44 us (1%)
    ppermute x16, starting transfers between devices, send(): return lax.ppermute(value, axis, pairs)  30 us
    pallas_call x4, Pallas kernels, solve(): pl.pallas_call(functools.partial(solve_kernel, first, edges), grid=(count...  23.4 us
    ppermute x16, waiting for transfers between devices, send(): return lax.ppermute(value, axis, pairs)  19.7 us
    pallas_call x4, Pallas kernels, finish(): pl.pallas_call(functools.partial(finish_kernel, late), grid=(count,), in_...  17 us
    pallas_call x2, Pallas kernels, late_sum(): pl.pallas_call(late_sum_kernel, grid=(count,), in_specs=[pl.BlockSpec(mem...  7.22 us
    pallas_call x2, Pallas kernels, early_edges(): pl.pallas_call(early_edges_kernel, grid=(count,), in_specs=[pl.BlockSpec(...  6.86 us
    all_to_all x1, starting transfers between devices, body(): lax.all_to_all(parts, ('energy', 'mom'), split_axis=0, concat_axis=0, til...  6.29 us
    pallas_call x2, Pallas kernels, join_late(): pl.pallas_call(join_late_kernel, grid=(count,), in_specs=[grid_spec(energ...  5.24 us
  transfers between devices with their start and end apart: 17, of which 3 were waited for; matrix products, arithmetic and copies ran while one was open for 3% of the time, Pallas kernels for 46%

commit v1 on v0

--- a/solution.py
+++ b/solution.py
@@ -31,22 +31,25 @@
 
 
 def complex_dot(left, right):
-    re = dot(left[0], right[0]) - dot(left[1], right[1])
-    im = dot(left[0], right[1]) + dot(left[1], right[0])
+    wide = jnp.concatenate(left, axis=1)
+    re = dot(wide, jnp.concatenate([right[0], -right[1]], axis=0))
+    im = dot(wide, jnp.concatenate([right[1], right[0]], axis=0))
     return re.astype(BF16), im.astype(BF16)
 
 
 def complex_dot_adjoint(left, right):
-    re = dot(left[0], right[0], True) + dot(left[1], right[1], True)
-    im = dot(left[1], right[0], True) - dot(left[0], right[1], True)
+    wide = jnp.concatenate(left, axis=1)
+    re = dot(wide, jnp.concatenate([right[0], right[1]], axis=1), True)
+    im = dot(wide, jnp.concatenate([-right[1], right[0]], axis=1), True)
     return re.astype(BF16), im.astype(BF16)
 
 
-def solve_kernel(first, edges, *refs):
+def solve_kernel(first, edges, again, *refs):
     refs = list(refs)
     a_ref, t_ref = refs[:2]
     previous_ref = None if first else refs[2]
     carry = refs.pop()
+    again_ref = refs.pop() if again else None
     low_ref, high_ref = refs[-2:] if edges else (None, None)
     outs = refs[:-2] if edges else refs
     green_ref, density_ref = outs[-2:]
@@ -76,21 +79,25 @@
                 left = complex_dot(t, (carry[0, e], carry[1, e]))
                 carry[0, e], carry[1, e] = complex_dot_adjoint(left, t)
 
+    blocks = [(a_ref[0, e, 0], a_ref[1, e, 0]) for e in range(energies)]
+    couples = [(carry[0, e], carry[1, e]) for e in range(energies)]
+    if not first:
+        lefts = [complex_dot(t, green) for green in couples]
+        couples = [complex_dot_adjoint(left, t) for left in lefts]
+    inners = [complex_dot(a, couple) for a, couple in zip(blocks, couples)]
     for e in range(energies):
-        a = (a_ref[0, e, 0], a_ref[1, e, 0])
-        if first:
-            couple = (carry[0, e], carry[1, e])
-        else:
-            left = complex_dot(t, (carry[0, e], carry[1, e]))
-            couple = complex_dot_adjoint(left, t)
-        inner = complex_dot(a, couple)
-        re = a[0].astype(F32) + (dot(inner[0], a[0]) - dot(inner[1], a[1]))
-        im = a[1].astype(F32) + (dot(inner[0], a[1]) + dot(inner[1], a[0]))
+        a, inner = blocks[e], inners[e]
+        wide = jnp.concatenate(inner, axis=1)
+        re = a[0].astype(F32) + dot(wide, jnp.concatenate([a[0], -a[1]], axis=0))
+        im = a[1].astype(F32) + dot(wide, jnp.concatenate([a[1], a[0]], axis=0))
         re, im = re.astype(BF16), im.astype(BF16)
         carry[0, e] = re
         carry[1, e] = im
         green_ref[0, 0, e] = re
         green_ref[0, 1, e] = im
+        if again:
+            again_ref[0, 0, e] = re
+            again_ref[0, 1, e] = im
         if edges and e == 0:
             low_ref[0, 0] = re
             low_ref[0, 1] = im
@@ -102,7 +109,7 @@
     density_ref[0] = total
 
 
-def solve(inverse, coupled, previous, start, count, edges, after=()):
+def solve(inverse, coupled, previous, start, count, edges, again, after=()):
     _, energies, _, total_rows, width = inverse.shape
     first = previous is None
     args = [inverse, coupled]
@@ -130,8 +137,11 @@
         for _ in range(2):
             out_shape.append(jax.ShapeDtypeStruct((count, 2, width, width), BF16))
             out_specs.append(pl.BlockSpec((1, 2, width, width), lambda i: (i, 0, 0, 0)))
-    return pl.pallas_call(
-        functools.partial(solve_kernel, first, edges),
+    if again:
+        out_shape.append(out_shape[0])
+        out_specs.append(out_specs[0])
+    return pl.pallas_call(
+        functools.partial(solve_kernel, first, edges, again),
         grid=(count,),
         in_specs=in_specs,
         out_specs=out_specs,
@@ -151,72 +161,33 @@
     return pl.BlockSpec((1, 2, width, width), lambda i: (i, 0, 0, 0))
 
 
-def member_spec(which, energies, width):
-    return pl.BlockSpec(
-        (None, 1, 2, energies, width, width), lambda i: (which, i, 0, 0, 0, 0)
-    )
-
-
-def early_members(own, crossed, other):
+def early_members(*blocks):
+    count, _, energies, width, _ = blocks[0].shape
+    return list(blocks), [grid_spec(energies, width)] * 4
+
+
+def late_members(own, other, *edges):
     count, _, energies, width, _ = own.shape
-    spec = grid_spec(energies, width)
-    specs = [spec, member_spec(0, energies, width), spec, member_spec(1, energies, width)]
-    return [own, other, crossed, other], specs
-
-
-def late_members(own, before, behind, other):
-    count, _, energies, width, _ = own.shape
-    edge = edge_spec(width)
-    specs = [grid_spec(energies, width), edge, edge, grid_spec(energies + 2, width)]
-    return [own, before, behind, other], specs
-
-
-def join_early_kernel(own_ref, crossed_ref, *refs):
-    out_ref = refs[-1]
-    out_ref[0] = own_ref[...]
-    out_ref[1] = crossed_ref[...]
-
-
-def join_late_kernel(own_ref, before_ref, behind_ref, *refs):
-    out_ref = refs[-1]
-    energies = own_ref.shape[2]
-    for part in range(2):
-        out_ref[0, part, 0] = before_ref[0, part]
-        for e in range(energies):
-            out_ref[0, part, e + 1] = own_ref[0, part, e]
-        out_ref[0, part, energies + 1] = behind_ref[0, part]
-
-
-def join_early(own, crossed, after):
-    count, _, energies, width, _ = own.shape
-    spec = grid_spec(energies, width)
-    return pl.pallas_call(
-        join_early_kernel,
-        grid=(count,),
-        in_specs=[spec, spec] + [ANY] * len(after),
-        out_specs=pl.BlockSpec(
-            (2, 1, 2, energies, width, width), lambda i: (0, i, 0, 0, 0, 0)
-        ),
-        out_shape=jax.ShapeDtypeStruct((2,) + own.shape, BF16),
-        compiler_params=pltpu.CompilerParams(vmem_limit_bytes=VMEM),
-        cost_estimate=cost(1.3 * count),
-        name="join_early",
-    )(own, crossed, *after)
-
-
-def join_late(own, before, behind, after):
-    count, _, energies, width, _ = own.shape
-    edge = edge_spec(width)
-    return pl.pallas_call(
-        join_late_kernel,
-        grid=(count,),
-        in_specs=[grid_spec(energies, width), edge, edge] + [ANY] * len(after),
-        out_specs=grid_spec(energies + 2, width),
-        out_shape=jax.ShapeDtypeStruct((count, 2, energies + 2, width, width), BF16),
-        compiler_params=pltpu.CompilerParams(vmem_limit_bytes=VMEM),
-        cost_estimate=cost(1.3 * count),
-        name="join_late",
-    )(own, before, behind, *after)
+    specs = [grid_spec(energies, width)] * 2 + [edge_spec(width)] * 4
+    return [own, other, *edges], specs
+
+
+def gate_kernel(*refs):
+    pass
+
+
+def gate(values, after):
+    count = len(values)
+    return pl.pallas_call(
+        gate_kernel,
+        in_specs=[ANY] * (count + len(after)),
+        out_specs=[ANY] * count,
+        out_shape=[jax.ShapeDtypeStruct(value.shape, value.dtype) for value in values],
+        input_output_aliases={i: i for i in range(count)},
+        compiler_params=pltpu.CompilerParams(vmem_limit_bytes=VMEM),
+        cost_estimate=cost(2.0),
+        name="gate",
+    )(*values, *after)
 
 
 def tiles(width):
@@ -272,17 +243,18 @@
 
 
 def late_line(refs, part, rows):
-    own, before, behind, other = refs
-    energies = own.shape[2]
-    mine = [before[0, part, rows, :]]
-    mine += [own[0, part, e, rows, :] for e in range(energies)]
-    mine += [behind[0, part, rows, :]]
-    theirs = [other[0, part, e, rows, :] for e in range(energies + 2)]
-    return [[value.astype(F32) for value in line] for line in (mine, theirs)]
+    grids, edges = refs[:2], refs[2:]
+    lines = []
+    for j in range(2):
+        line = [edges[2 * j][0, part, rows, :]]
+        line += [grids[j][0, part, e, rows, :] for e in range(grids[j].shape[2])]
+        line += [edges[2 * j + 1][0, part, rows, :]]
+        lines.append([value.astype(F32) for value in line])
+    return lines
 
 
 def late_sum_kernel(w_ref, *refs):
-    members, out_ref = refs[:4], refs[-1]
+    members, out_ref = refs[:6], refs[-1]
     energies, width = members[0].shape[2:4]
     w = [[w_ref[1, o, j] for j in range(2)] for o in range(3)]
 
@@ -310,7 +282,7 @@
 
 
 def finish_kernel(late, w_ref, across_ref, down_ref, *refs):
-    members, received, out_ref = refs[:4], refs[4 : 5 if late else 6], refs[-1]
+    members, received, out_ref = refs[: 6 if late else 4], refs[6:7] if late else refs[4:6], refs[-1]
     energies, width = members[0].shape[2:4]
     w = [[w_ref[0, o, j] for j in range(4)] for o in range(3)]
     across = across_ref[0]
@@ -413,15 +385,15 @@
 
 def range_total_kernel(parts_ref, *refs):
     out_ref = refs[-1]
-    out_ref[...] = jnp.sum(parts_ref[...], axis=0)
+    out_ref[0] = jnp.sum(parts_ref[...])
 
 
 def range_total(received, after):
     return pl.pallas_call(
         range_total_kernel,
         in_specs=[pl.BlockSpec(memory_space=pltpu.VMEM)] + [ANY] * len(after),
-        out_specs=pl.BlockSpec(memory_space=pltpu.VMEM),
-        out_shape=jax.ShapeDtypeStruct(received.shape[1:], F32),
+        out_specs=pl.BlockSpec(memory_space=pltpu.SMEM),
+        out_shape=jax.ShapeDtypeStruct((1,), F32),
         compiler_params=pltpu.CompilerParams(vmem_limit_bytes=VMEM),
         cost_estimate=cost(1),
         name="range_total",
@@ -467,76 +439,90 @@
     def pair(value, name):
         return send(value, "mom", [(i, i ^ 2) for i in range(4)], name)
 
-    def halo(low, high, name):
-        return (
-            send(high, "energy", up, "up" + name),
-            send(low, "energy", down, "down" + name),
-        )
-
     weights = own_weights(shifts, emission_weight, absorption_weight)
     across_scale = deform_potential.reshape(-1, 1, width)
     down_scale = deform_potential.reshape(-1, 1)
 
-    def run(chunk, previous, after=()):
+    def run(chunk, previous, after=(), again=False):
         kind, start, count = CHUNKS[chunk]
         return solve(
-            inverse_blocks, coupling_blocks, previous, start, count, kind == "late", after
+            inverse_blocks, coupling_blocks, previous, start, count, kind == "late", again, after
         )
 
-    g0, n0 = run(0, None)
-    y0 = pair(g0, "pair0")
-    g1, n1, low1, high1 = run(1, g0)
-    edges1 = halo(low1, high1, "1")
-    g2, n2 = run(2, g1)
-    y2 = pair(g2, "pair2")
-    g3, n3, low3, high3 = run(3, g2)
-    edges3 = halo(low3, high3, "3")
-    j0 = join_early(g0, y0, (g3,))
-    k0 = core(j0, "core0")
-    j1 = join_late(g1, *edges1, (j0,))
-    k1 = core(j1, "core1")
-    members0 = (g0, y0, k0)
-    high0, low0 = early_edges(weights, members0, (j1,))
-    members1 = (g1, *edges1, k1)
-    total1 = late_sum(weights, members1, (low0,))
-    x1 = pair(total1, "pair1")
-    edges0 = halo(low0, high0, "0")
-
-    j2 = join_early(g2, y2, (total1,))
-    k2 = core(j2, "core2")
-    j3 = join_late(g3, *edges3, (j2,))
-    k3 = core(j3, "core3")
-    members2 = (g2, y2, k2)
-    high2, low2 = early_edges(weights, members2, (j3,))
-    members3 = (g3, *edges3, k3)
-    total3 = late_sum(weights, members3, (low2,))
-    x3 = pair(total3, "pair3")
-    edges2 = halo(low2, high2, "2")
-
-    parts = range_parts(range_rows, [n0, n1, n2, n3], (total3,))
-    received = lax.all_to_all(parts, ("energy", "mom"), split_axis=0, concat_axis=0, tiled=True)
-    charge = range_total(received, (x3,))
-
-    sigma = None
-    for index, late, members, got, after in (
-        (1, True, members1, (x1,), (parts,)),
-        (0, False, members0, edges0, ()),
-        (3, True, members3, (x3,), ()),
-        (2, False, members2, edges2, (charge,)),
-    ):
-        sigma = finish(
+    def rise(value, name):
+        return send(value, "energy", up, "up" + name)
+
+    def fall(value, name):
+        return send(value, "energy", down, "down" + name)
+
+    def done(sigma, chunk, members, got, after=()):
+        kind, start, _ = CHUNKS[chunk]
+        return finish(
             sigma,
             inverse_blocks.shape,
-            CHUNKS[index][1],
+            start,
             weights,
             across_scale,
             down_scale,
-            late,
+            kind == "late",
             members,
             got,
             after,
         )
-    return sigma, jnp.sum(charge).reshape(1)
+
+    g0, n0 = run(0, None)
+    y0, c0 = pair(g0, "pair0"), core(g0, "core0")
+    g1, n1, low1, high1 = run(1, g0)
+    up1, down1, c1 = rise(high1, "1"), fall(low1, "1"), core(g1, "core1")
+    g2, n2, h2 = run(2, g1, (c0,), True)
+    y2 = pair(g2, "pair2")
+    g3, n3, low3, high3, h3 = run(3, g2, (c1,), True)
+
+    (y0,) = gate([y0], (g3,))
+    core_y0 = core(y0, "core_pair0")
+    (c0,) = gate([c0], (y0,))
+    members0 = (g0, c0, y0, core_y0)
+    high0, low0 = early_edges(weights, members0, ())
+
+    low3, high3, h3 = gate([low3, high3, h3], (low0,))
+    up3, down3, c3 = rise(high3, "3"), fall(low3, "3"), core(h3, "core3")
+    (n0,) = gate([n0], (low3,))
+
+    up1, down1 = gate([up1, down1], (n0, c3))
+    core_up1, core_down1 = core(up1, "core_up1"), core(down1, "core_down1")
+    (c1,) = gate([c1], (up1,))
+    members1 = (g1, c1, up1, down1, core_up1, core_down1)
+    total1 = late_sum(weights, members1, ())
+    x1 = pair(total1, "pair1")
+
+    y2, high0, low0, h2 = gate([y2, high0, low0, h2], (total1,))
+    up0, down0, c2 = rise(high0, "0"), fall(low0, "0"), core(h2, "core2")
+
+    (n1,) = gate([n1], (y2,))
+    parts = range_parts(range_rows, [n0, n1, n2, n3], (c2,))
+    received = lax.all_to_all(parts, ("energy", "mom"), split_axis=0, concat_axis=0, tiled=True)
+
+    (y2,) = gate([y2], (parts,))
+    core_y2 = core(y2, "core_pair2")
+    (c2,) = gate([c2], (y2,))
+    members2 = (g2, c2, y2, core_y2)
+    high2, low2 = early_edges(weights, members2, ())
+
+    up3, down3 = gate([up3, down3], (low2,))
+    core_up3, core_down3 = core(up3, "core_up3"), core(down3, "core_down3")
+    (c3,) = gate([c3], (up3,))
+    members3 = (g3, c3, up3, down3, core_up3, core_down3)
+    total3 = late_sum(weights, members3, ())
+    x3 = pair(total3, "pair3")
+    x1, high2, low2 = gate([x1, high2, low2], (total3,))
+    up2, down2 = rise(high2, "2"), fall(low2, "2")
+
+    sigma = done(None, 1, members1, (x1,))
+    sigma = done(sigma, 0, members0, (up0, down0))
+    charge = range_total(received, (sigma,))
+    sigma = done(sigma, 3, members3, (x3,), (charge,))
+    sigma = done(sigma, 2, members2, (up2, down2))
+    return sigma, charge
 
 
 def solution(mesh):

time: 130 us -> 121 us (0.931)
  Pallas kernels: 68.7 us -> 55.1 us
  starting transfers between devices: 36.3 us -> 39.5 us
  waiting for transfers between devices: 19.7 us -> 22.1 us
    pallas_call x8 -> x17, Pallas kernels: 33.8 us -> 19.6 us  [the longest x4 19.6 us: solve(): pl.pallas_call(functools.partial(solve_kernel, first, edges, again), grid...]
    ppermute x16 -> x22, starting transfers between devices: 30 us -> 34 us  [send(): return lax.ppermute(value, axis, pairs)]
    ppermute x16 -> x22, waiting for transfers between devices: 19.7 us -> 22.1 us  [send(): return lax.ppermute(value, axis, pairs)]
  transfers between devices with their start and end apart: 17 -> 23, of which waited for: 3 -> 9; matrix products, arithmetic and copies ran while one was open for 3% -> 2% of each run, Pallas kernels for 46% -> 38%
where the time goes in v1:
time: 121 us; the launch traced here: 120 us
  Pallas kernels  55.1 us (46%)
  starting transfers between devices  39.5 us (33%)
  waiting for transfers between devices  22.1 us (18%)
  local copies, waits for them, and re-layouts  1.38 us (1%)
    ppermute x22, starting transfers between devices, send(): return lax.ppermute(value, axis, pairs)  34 us
    ppermute x22, waiting for transfers between devices, send(): return lax.ppermute(value, axis, pairs)  22.1 us
    pallas_call x4, Pallas kernels, solve(): pl.pallas_call(functools.partial(solve_kernel, first, edges, again), grid...  19.6 us
    pallas_call x4, Pallas kernels, finish(): pl.pallas_call(functools.partial(finish_kernel, late), grid=(count,), in_...  17.7 us
    pallas_call x2, Pallas kernels, late_sum(): pl.pallas_call(late_sum_kernel, grid=(count,), in_specs=[pl.BlockSpec(mem...  7.13 us
    pallas_call x2, Pallas kernels, early_edges(): pl.pallas_call(early_edges_kernel, grid=(count,), in_specs=[pl.BlockSpec(...  6.86 us
    all_to_all x1, starting transfers between devices, body(): lax.all_to_all(parts, ('energy', 'mom'), split_axis=0, concat_axis=0, til...  5.5 us
  transfers between devices with their start and end apart: 23, of which 9 were waited for; matrix products, arithmetic and copies ran while one was open for 2% of the time, Pallas kernels for 38%

profile of v1, /device:TPU:24, one launch (start us, length us, event | category | flops | bytes accessed | tf_op | source)
XLA Modules:
  0.0 120.1 jit_solution(2976127271401843020)
XLA Ops:
  0.6 4.6 %solve.4 = (bf16[2,2,2,256,256]{4,3,2,1,0:T(8,128)(2,1)}, f32[2,8,256]{2,1,0:T(8,128)}) custom-call(bf16[2,2,1,2048,256]{4,3,2,1,0:T(8,128)(2,1)} %refs_0_.7, bf16[2,1,2048,256]{3,2,1,0:T(8,128)(2,1)} %refs_1_.7), custom_call_target="tpu_custom_call" | custom-call | flops 575000018944 | tf_op jit(solution)/shard_map/solve/pallas_call | solution.py:143
  5.2 0.0 collective-permute-start
  5.2 1.6 %collective-permute-start.2 = (bf16[2,2,2,256,256]{4,3,2,1,0:T(8,128)(2,1)}, bf16[2,2,2,256,256]{4,3,2,1,0:T(8,128)(2,1)}, u32[]{:S(2)}, u32[]{:S(2)}) collective-permute-start(bf16[2,2,2,256,256]{4,3,2,1,0:T(8,128)(2,1)} %get-tuple-element.34.refs_2_.refs_0_), channel_id=1, source_target_pairs={{0,2},{1,3},{2,0},{3,1},{4,6},{5,7},{6,4},{7,5},{8,10},{9,11},{10,... | collective-permute-start | bytes 3145736 | tf_op jit(solution)/shard_map/pair0/ppermute | solution.py:434
  6.8 5.0 %solve.5 = (bf16[2,2,2,256,256]{4,3,2,1,0:T(8,128)(2,1)}, f32[2,8,256]{2,1,0:T(8,128)}, bf16[2,2,256,256]{3,2,1,0:T(8,128)(2,1)}, bf16[2,2,256,256]{3,2,1,0:T(8,128)(2,1)}) custom-call(bf16[2,2,1,2048,256]{4,3,2,1,0:T(8,128)(2,1)} %refs_0_.7, bf16[2,1,2048,256]{3,2,1,0:T(8,128)(2,1)} %refs_1_.7, bf16[2,2,2,256,256]{4,3,2,1,0:T(8,128)(2,1)} %get-tuple-element.34.refs_2_.refs_0_), custom_call_target="tpu_custom_call" | custom-call | flops 575000018944 | tf_op jit(solution)/shard_map/solve/pallas_call | solution.py:143
  11.8 0.2 collective-permute-start.3
  12.0 3.4 %collective-permute-start.5 = (bf16[2,2,256,256]{3,2,1,0:T(8,128)(2,1)}, bf16[2,2,256,256]{3,2,1,0:T(8,128)(2,1)}, u32[]{:S(2)}, u32[]{:S(2)}) collective-permute-start(bf16[2,2,256,256]{3,2,1,0:T(8,128)(2,1)} %get-tuple-element.41), channel_id=1, source_target_pairs={{0,4},{4,8},{8,12},{12,16},{16,20},{20,24},{24,28},{1,5},{5,9},{9,... | collective-permute-start | bytes 1572872 | tf_op jit(solution)/shard_map/up1/ppermute | solution.py:434
  15.4 3.3 %collective-permute-start.6 = (bf16[2,2,256,256]{3,2,1,0:T(8,128)(2,1)}, bf16[2,2,256,256]{3,2,1,0:T(8,128)(2,1)}, u32[]{:S(2)}, u32[]{:S(2)}) collective-permute-start(bf16[2,2,256,256]{3,2,1,0:T(8,128)(2,1)} %get-tuple-element.42), channel_id=1, source_target_pairs={{4,0},{8,4},{12,8},{16,12},{20,16},{24,20},{28,24},{5,1},{9,5},{13... | collective-permute-start | bytes 1572872 | tf_op jit(solution)/shard_map/down1/ppermute | solution.py:434
  18.8 1.4 %copy.42.down_ref = f32[2048,1]{1,0:T(8,128)} copy(f32[2048,1]{0,1:T(1,128)S(1)} %bitcast.9) | data formatting | bytes 16384 | tf_op jit(solution)/shard_map/reshape | solution.py:444
  20.2 0.1 add_reduce_fusion.1
  20.3 0.1 compare_convert_fusion
  20.4 0.1 fusion
  20.4 0.1 broadcast_multiply_fusion
  20.5 0.7 multiply_reduce_fusion.w_ref
  21.2 0.0 collective-permute-done.refs_3_.refs_0_
  21.2 4.9 %solve.6 = (bf16[2,2,2,256,256]{4,3,2,1,0:T(8,128)(2,1)}, f32[2,8,256]{2,1,0:T(8,128)}, bf16[2,2,2,256,256]{4,3,2,1,0:T(8,128)(2,1)}) custom-call(bf16[2,2,1,2048,256]{4,3,2,1,0:T(8,128)(2,1)} %refs_0_.7, bf16[2,1,2048,256]{3,2,1,0:T(8,128)(2,1)} %refs_1_.7, bf16[2,2,2,256,256]{4,3,2,1,0:T(8,128)(2,1)} %get-tuple-element.35.refs_2_.refs_0_, ...), custom_call_target="tpu_custom_call" | custom-call | flops 575000018944 | tf_op jit(solution)/shard_map/solve/pallas_call | solution.py:143
  26.1 0.5 collective-permute-start.1
  26.6 0.0 collective-permute-done.3.refs_3_.refs_0_
  26.6 5.1 %solve.7 = (bf16[2,2,2,256,256]{4,3,2,1,0:T(8,128)(2,1)}, f32[2,8,256]{2,1,0:T(8,128)}, bf16[2,2,256,256]{3,2,1,0:T(8,128)(2,1)}, bf16[2,2,256,256]{3,2,1,0:T(8,128)(2,1)}, bf16[2,2,2,256,256]{4,3,2,1,0:T(8,128)(2,1)}) custom-call(bf16[2,2,1,2048,256]{4,3,2,1,0:T(8,128)(2,1)} %refs_0_.7, bf16[2,1,2048,256]{3,2,1,0:T(8,128)(2,1)} %refs_1_.7, ...), custom_call_target="tpu_custom_call" | custom-call | flops 575000018944 | tf_op jit(solution)/shard_map/solve/pallas_call | solution.py:143
  31.7 0.0 collective-permute-done.2.refs_0_
  31.7 0.1 collective-permute-start.4
  31.8 3.0 %collective-permute-done.4.refs_3_ = bf16[2,2,2,256,256]{4,3,2,1,0:T(8,128)(2,1)} collective-permute-done((bf16[2,2,2,256,256]{4,3,2,1,0:T(8,128)(2,1)}, bf16[2,2,2,256,256]{4,3,2,1,0:T(8,128)(2,1)}, u32[]{:S(2)}, u32[]{:S(2)}) %collective-permute-start.4) | collective-permute-done | bytes 1048608 | tf_op jit(solution)/shard_map/core_pair0/ppermute | solution.py:434
  34.8 3.4 %early_edges.2 = (bf16[2,2,256,256]{3,2,1,0:T(8,128)(2,1)}, bf16[2,2,256,256]{3,2,1,0:T(8,128)(2,1)}) custom-call(f32[2,3,4]{2,1,0:T(4,128)} %multiply_reduce_fusion.w_ref, bf16[2,2,2,256,256]{4,3,2,1,0:T(8,128)(2,1)} %get-tuple-element.34.refs_2_.refs_0_, bf16[2,2,2,256,256]{4,3,2,1,0:T(8,128)(2,1)} %gate.14.refs_1_, ...), custom_call_target="tpu_custom_call" | custom-call | flops 390999998464 | tf_op jit(solution)/shard_map/early_edges/pallas_call | solution.py:233
  38.2 0.1 collective-permute-start.7
  38.3 3.1 %collective-permute-start.14 = (bf16[2,2,256,256]{3,2,1,0:T(8,128)(2,1)}, bf16[2,2,256,256]{3,2,1,0:T(8,128)(2,1)}, u32[]{:S(2)}, u32[]{:S(2)}) collective-permute-start(bf16[2,2,256,256]{3,2,1,0:T(8,128)(2,1)} %get-tuple-element.47.refs_1_), channel_id=1, source_target_pairs={{4,0},{8,4},{12,8},{16,12},{20,16},{24,20},{28,24},{5,1},{9,5},{13... | collective-permute-start | bytes 1572872 | tf_op jit(solution)/shard_map/down3/ppermute | solution.py:434
  41.4 0.0 collective-permute-done.5.refs_0_
  41.4 3.5 %collective-permute-start.13 = (bf16[2,2,256,256]{3,2,1,0:T(8,128)(2,1)}, bf16[2,2,256,256]{3,2,1,0:T(8,128)(2,1)}, u32[]{:S(2)}, u32[]{:S(2)}) collective-permute-start(bf16[2,2,256,256]{3,2,1,0:T(8,128)(2,1)} %get-tuple-element.58), channel_id=1, source_target_pairs={{0,4},{4,8},{8,12},{12,16},{16,20},{20,24},{24,28},{1,5},{5,9},{9,... | collective-permute-start | bytes 1572872 | tf_op jit(solution)/shard_map/up3/ppermute | solution.py:434
  45.0 0.0 collective-permute-done.6.refs_1_
  45.0 0.0 collective-permute-done.7.refs_3_.refs_0_
  45.0 0.1 collective-permute-start.8
  45.1 0.5 collective-permute-start.9
  45.6 1.7 %collective-permute-done.8.refs_4_ = bf16[2,2,256,256]{3,2,1,0:T(8,128)(2,1)} collective-permute-done((bf16[2,2,256,256]{3,2,1,0:T(8,128)(2,1)}, bf16[2,2,256,256]{3,2,1,0:T(8,128)(2,1)}, u32[]{:S(2)}, u32[]{:S(2)}) %collective-permute-start.8) | collective-permute-done | bytes 524320 | tf_op jit(solution)/shard_map/core_up1/ppermute | solution.py:434
  47.3 0.7 collective-permute-done.9.refs_5_
  48.1 3.6 %late_sum.2.refs_4_ = bf16[2,2,2,256,256]{4,3,2,1,0:T(8,128)(2,1)} custom-call(f32[2,3,4]{2,1,0:T(4,128)} %multiply_reduce_fusion.w_ref, bf16[2,2,2,256,256]{4,3,2,1,0:T(8,128)(2,1)} %get-tuple-element.35.refs_2_.refs_0_, bf16[2,2,2,256,256]{4,3,2,1,0:T(8,128)(2,1)} %gate.18.refs_1_, bf16[2,2,256,256]{3,2,1,0:T(8,128)(2,1)} %get-tuple-element.49.refs_1_.refs_2_, ...), custom_call_target="tpu_custom_call" | custom-call | flops 413999988736 | tf_op jit(solution)/shard_map/late_sum/pallas_call | solution.py:272
  51.6 1.5 %collective-permute-start.12 = (bf16[2,2,2,256,256]{4,3,2,1,0:T(8,128)(2,1)}, bf16[2,2,2,256,256]{4,3,2,1,0:T(8,128)(2,1)}, u32[]{:S(2)}, u32[]{:S(2)}) collective-permute-start(bf16[2,2,2,256,256]{4,3,2,1,0:T(8,128)(2,1)} %late_sum.2.refs_4_), channel_id=1, source_target_pairs={{0,2},{1,3},{2,0},{3,1},{4,6},{5,7},{6,4},{7,5},{8,10},{9,11},{10,... | collective-permute-start | bytes 3145736 | tf_op jit(solution)/shard_map/pair1/ppermute | solution.py:434
  53.2 0.4 collective-permute-done.1.refs_0_
  53.6 0.0 collective-permute-start.10
  53.6 3.8 %collective-permute-start.20 = (bf16[2,2,256,256]{3,2,1,0:T(8,128)(2,1)}, bf16[2,2,256,256]{3,2,1,0:T(8,128)(2,1)}, u32[]{:S(2)}, u32[]{:S(2)}) collective-permute-start(bf16[2,2,256,256]{3,2,1,0:T(8,128)(2,1)} %get-tuple-element.63), channel_id=1, source_target_pairs={{0,4},{4,8},{8,12},{12,16},{16,20},{20,24},{24,28},{1,5},{5,9},{9,... | collective-permute-start | bytes 1572872 | tf_op jit(solution)/shard_map/up0/ppermute | solution.py:434
  57.5 0.0 collective-permute-done.10.refs_4_.refs_0_
  57.5 2.2 %range_parts.1.refs_1_ = f32[32,8,128]{2,1,0:T(8,128)} custom-call(s32[32]{0:T(128)} %range_ref.1, f32[2,8,256]{2,1,0:T(8,128)} %gate.16.refs_2_.refs_0_, f32[2,8,256]{2,1,0:T(8,128)} %gate.20.refs_1_, f32[2,8,256]{2,1,0:T(8,128)} %get-tuple-element.54.refs_2_, f32[2,8,256]{2,1,0:T(8,128)} %get-tuple-element.55.refs_3_, ...), custom_call_target="tpu_custom_call" | custom-call | flops 253000007680 | tf_op jit(solution)/shard_map/range_parts/pallas_call | solution.py:373
  59.7 5.5 %all-to-all-start = ((f32[32,8,128]{2,1,0:T(8,128)}), f32[32,8,128]{2,1,0:T(8,128)}, u32[]{:S(2)}, u32[]{:S(2)}) async-start(f32[32,8,128]{2,1,0:T(8,128)} %range_parts.1.refs_1_), calls=%async_computation | async-start | bytes 262144 | tf_op jit(solution)/shard_map/all_to_all | solution.py:503
  65.2 0.2 collective-permute-start.11
  65.4 2.9 %collective-permute-done.11.refs_3_ = bf16[2,2,2,256,256]{4,3,2,1,0:T(8,128)(2,1)} collective-permute-done((bf16[2,2,2,256,256]{4,3,2,1,0:T(8,128)(2,1)}, bf16[2,2,2,256,256]{4,3,2,1,0:T(8,128)(2,1)}, u32[]{:S(2)}, u32[]{:S(2)}) %collective-permute-start.11) | collective-permute-done | bytes 1048608 | tf_op jit(solution)/shard_map/core_pair2/ppermute | solution.py:434
  68.3 3.3 %collective-permute-start.21 = (bf16[2,2,256,256]{3,2,1,0:T(8,128)(2,1)}, bf16[2,2,256,256]{3,2,1,0:T(8,128)(2,1)}, u32[]{:S(2)}, u32[]{:S(2)}) collective-permute-start(bf16[2,2,256,256]{3,2,1,0:T(8,128)(2,1)} %get-tuple-element.64), channel_id=1, source_target_pairs={{4,0},{8,4},{12,8},{16,12},{20,16},{24,20},{28,24},{5,1},{9,5},{13... | collective-permute-start | bytes 1572872 | tf_op jit(solution)/shard_map/down0/ppermute | solution.py:434
  71.6 3.5 %early_edges.3 = (bf16[2,2,256,256]{3,2,1,0:T(8,128)(2,1)}, bf16[2,2,256,256]{3,2,1,0:T(8,128)(2,1)}) custom-call(f32[2,3,4]{2,1,0:T(4,128)} %multiply_reduce_fusion.w_ref, bf16[2,2,2,256,256]{4,3,2,1,0:T(8,128)(2,1)} %get-tuple-element.36.refs_2_.refs_0_, bf16[2,2,2,256,256]{4,3,2,1,0:T(8,128)(2,1)} %gate.22.refs_1_, ...), custom_call_target="tpu_custom_call" | custom-call | flops 390999998464 | tf_op jit(solution)/shard_map/early_edges/pallas_call | solution.py:233
  75.1 0.0 collective-permute-done.13.refs_0_
  75.1 3.7 %collective-permute-done.14.refs_1_ = bf16[2,2,256,256]{3,2,1,0:T(8,128)(2,1)} collective-permute-done((bf16[2,2,256,256]{3,2,1,0:T(8,128)(2,1)}, bf16[2,2,256,256]{3,2,1,0:T(8,128)(2,1)}, u32[]{:S(2)}, u32[]{:S(2)}) %collective-permute-start.14) | collective-permute-done | bytes 524320 | tf_op jit(solution)/shard_map/down3/ppermute | solution.py:434
  78.8 0.0 collective-permute-start.15
  78.8 0.5 collective-permute-start.16
  79.3 1.7 %collective-permute-done.15.refs_4_ = bf16[2,2,256,256]{3,2,1,0:T(8,128)(2,1)} collective-permute-done((bf16[2,2,256,256]{3,2,1,0:T(8,128)(2,1)}, bf16[2,2,256,256]{3,2,1,0:T(8,128)(2,1)}, u32[]{:S(2)}, u32[]{:S(2)}) %collective-permute-start.15) | collective-permute-done | bytes 524320 | tf_op jit(solution)/shard_map/core_up3/ppermute | solution.py:434
  81.1 0.7 collective-permute-done.16.refs_5_
  81.8 3.6 %late_sum.3.refs_3_ = bf16[2,2,2,256,256]{4,3,2,1,0:T(8,128)(2,1)} custom-call(f32[2,3,4]{2,1,0:T(4,128)} %multiply_reduce_fusion.w_ref, bf16[2,2,2,256,256]{4,3,2,1,0:T(8,128)(2,1)} %get-tuple-element.37.refs_1_.refs_0_, bf16[2,2,2,256,256]{4,3,2,1,0:T(8,128)(2,1)} %gate.24.refs_1_, bf16[2,2,256,256]{3,2,1,0:T(8,128)(2,1)} %get-tuple-element.59.refs_1_.refs_2_, ...), custom_call_target="tpu_custom_call" | custom-call | flops 413999988736 | tf_op jit(solution)/shard_map/late_sum/pallas_call | solution.py:272
  85.4 1.5 %collective-permute-start.19 = (bf16[2,2,2,256,256]{4,3,2,1,0:T(8,128)(2,1)}, bf16[2,2,2,256,256]{4,3,2,1,0:T(8,128)(2,1)}, u32[]{:S(2)}, u32[]{:S(2)}) collective-permute-start(bf16[2,2,2,256,256]{4,3,2,1,0:T(8,128)(2,1)} %late_sum.3.refs_3_), channel_id=1, source_target_pairs={{0,2},{1,3},{2,0},{3,1},{4,6},{5,7},{6,4},{7,5},{8,10},{9,11},{10,... | collective-permute-start | bytes 3145736 | tf_op jit(solution)/shard_map/pair3/ppermute | solution.py:434
  86.9 0.0 collective-permute-done.12.refs_0_
  86.9 1.9 %collective-permute-start.17 = (bf16[2,2,256,256]{3,2,1,0:T(8,128)(2,1)}, bf16[2,2,256,256]{3,2,1,0:T(8,128)(2,1)}, u32[]{:S(2)}, u32[]{:S(2)}) collective-permute-start(bf16[2,2,256,256]{3,2,1,0:T(8,128)(2,1)} %get-tuple-element.61), channel_id=1, source_target_pairs={{0,4},{4,8},{8,12},{12,16},{16,20},{20,24},{24,28},{1,5},{5,9},{9,... | collective-permute-start | bytes 1572872 | tf_op jit(solution)/shard_map/up2/ppermute | solution.py:434
  88.8 4.8 %collective-permute-start.18 = (bf16[2,2,256,256]{3,2,1,0:T(8,128)(2,1)}, bf16[2,2,256,256]{3,2,1,0:T(8,128)(2,1)}, u32[]{:S(2)}, u32[]{:S(2)}) collective-permute-start(bf16[2,2,256,256]{3,2,1,0:T(8,128)(2,1)} %get-tuple-element.62), channel_id=1, source_target_pairs={{4,0},{8,4},{12,8},{16,12},{20,16},{24,20},{28,24},{5,1},{9,5},{13... | collective-permute-start | bytes 1572872 | tf_op jit(solution)/shard_map/down2/ppermute | solution.py:434
  93.6 4.1 %finish.4.refs_6_ = bf16[2,2,1,2048,256]{4,3,2,1,0:T(8,128)(2,1)} custom-call(f32[2,3,4]{2,1,0:T(4,128)} %multiply_reduce_fusion.w_ref, f32[8,1,256]{2,1,0:T(1,128)} %bitcast.5, f32[2048,1]{1,0:T(8,128)} %copy.42.down_ref, bf16[2,2,2,256,256]{4,3,2,1,0:T(8,128)(2,1)} %get-tuple-element.35.refs_2_.refs_0_, bf16[2,2,2,256,256]{4,3,2,1,0:T(8,128)(2,1)} %gate.18.refs_1_, ...), custom_call_target="tpu_custom_call" | custom-call | flops 506000015360 | tf_op jit(solution)/shard_map/finish/pallas_call | solution.py:332
  97.8 0.0 collective-permute-done.20.refs_4_
  97.8 4.4 %finish.5.refs_0_.refs_8_ = bf16[2,2,1,2048,256]{4,3,2,1,0:T(8,128)(2,1)} custom-call(f32[2,3,4]{2,1,0:T(4,128)} %multiply_reduce_fusion.w_ref, f32[8,1,256]{2,1,0:T(1,128)} %bitcast.6, f32[2048,1]{1,0:T(8,128)} %copy.42.down_ref, bf16[2,2,2,256,256]{4,3,2,1,0:T(8,128)(2,1)} %get-tuple-element.34.refs_2_.refs_0_, ...), custom_call_target="tpu_custom_call", output_to_operand_aliasing={{}: (9, {})} | custom-call | flops 506000015360 | tf_op jit(solution)/shard_map/finish/pallas_call | solution.py:332
  102.2 0.0 all-to-all-done.parts_ref
  102.2 1.6 %range_total.1.refs_7_ = f32[1]{0:T(128)} custom-call(f32[32,8,128]{2,1,0:T(8,128)} %all-to-all-done.parts_ref, bf16[2,2,1,2048,256]{4,3,2,1,0:T(8,128)(2,1)} %finish.5.refs_0_.refs_8_), custom_call_target="tpu_custom_call" | custom-call | flops 115000000512 | tf_op jit(solution)/shard_map/range_total/pallas_call | solution.py:392
  103.8 7.1 %collective-permute-done.19.refs_6_ = bf16[2,2,2,256,256]{4,3,2,1,0:T(8,128)(2,1)} collective-permute-done((bf16[2,2,2,256,256]{4,3,2,1,0:T(8,128)(2,1)}, bf16[2,2,2,256,256]{4,3,2,1,0:T(8,128)(2,1)}, u32[]{:S(2)}, u32[]{:S(2)}) %collective-permute-start.19) | collective-permute-done | bytes 1048608 | tf_op jit(solution)/shard_map/pair3/ppermute | solution.py:434
  110.9 4.8 %finish.6.refs_6_ = bf16[2,2,1,2048,256]{4,3,2,1,0:T(8,128)(2,1)} custom-call(f32[2,3,4]{2,1,0:T(4,128)} %multiply_reduce_fusion.w_ref, f32[8,1,256]{2,1,0:T(1,128)} %bitcast.7, f32[2048,1]{1,0:T(8,128)} %copy.42.down_ref, bf16[2,2,2,256,256]{4,3,2,1,0:T(8,128)(2,1)} %get-tuple-element.37.refs_1_.refs_0_, ...), custom_call_target="tpu_custom_call", output_to_operand_aliasing={{}: (11, {})} | custom-call | flops 506000015360 | tf_op jit(solution)/shard_map/finish/pallas_call | solution.py:332
  115.7 0.0 collective-permute-done.18.refs_5_
  115.7 4.4 %finish.7 = bf16[2,2,1,2048,256]{4,3,2,1,0:T(8,128)(2,1)} custom-call(f32[2,3,4]{2,1,0:T(4,128)} %multiply_reduce_fusion.w_ref, f32[8,1,256]{2,1,0:T(1,128)} %bitcast.8, f32[2048,1]{1,0:T(8,128)} %copy.42.down_ref, bf16[2,2,2,256,256]{4,3,2,1,0:T(8,128)(2,1)} %get-tuple-element.36.refs_2_.refs_0_, ...), custom_call_target="tpu_custom_call", output_to_operand_aliasing={{}: (9, {})} | custom-call | flops 506000015360 | tf_op jit(solution)/shard_map/finish/pallas_call | solution.py:332
  (27 shorter events, 0.1 us)
Async XLA Ops:
  5.2 16.0 %collective-permute-start = (bf16[2,2,2,256,256]{4,3,2,1,0:T(8,128)(2,1)}, bf16[2,2,2,256,256]{4,3,2,1,0:T(8,128)(2,1)}, u32[]{:S(2)}, u32[]{:S(2)}) collective-permute-start(bf16[2,2,2,256,256]{4,3,2,1,0:T(8,128)(2,1)} %get-tuple-element.34.refs_2_.refs_0_), channel_id=1, source_target_pairs={{0,1},{1,0},{2,3},{3,2},{4,5},{5,4},{6,7},{7,6},{8,9},{9,8},{10,11... | collective-permute-start | bytes 3145736 | tf_op jit(solution)/shard_map/core0/ppermute | solution.py:434
  5.2 26.5 %collective-permute-start.2 = (bf16[2,2,2,256,256]{4,3,2,1,0:T(8,128)(2,1)}, bf16[2,2,2,256,256]{4,3,2,1,0:T(8,128)(2,1)}, u32[]{:S(2)}, u32[]{:S(2)}) collective-permute-start(bf16[2,2,2,256,256]{4,3,2,1,0:T(8,128)(2,1)} %get-tuple-element.34.refs_2_.refs_0_), channel_id=1, source_target_pairs={{0,2},{1,3},{2,0},{3,1},{4,6},{5,7},{6,4},{7,5},{8,10},{9,11},{10,... | collective-permute-start | bytes 3145736 | tf_op jit(solution)/shard_map/pair0/ppermute | solution.py:434
  6.8 12.0 %copy-start.3 = (s32[4]{0:T(128)S(1)}, s32[4]{0:T(128)}, u32[]{:S(2)}) copy-start(s32[4]{0:T(128)} %param.10) | copy-start | bytes 52
  6.8 12.0 %copy-start = (f32[2048]{0:T(1024)S(1)}, f32[2048]{0:T(1024)}, u32[]{:S(2)}) copy-start(f32[2048]{0:T(1024)} %param.13) | copy-start | bytes 24580
  6.8 13.4 %copy-start.1 = (f32[4,4,4]{2,1,0:T(4,128)S(1)}, f32[4,4,4]{2,1,0:T(4,128)}, u32[]{:S(2)}) copy-start(f32[4,4,4]{2,1,0:T(4,128)} %param.12) | copy-start | bytes 772
  6.8 13.4 %copy-start.2 = (f32[4,4,4]{2,1,0:T(4,128)S(1)}, f32[4,4,4]{2,1,0:T(4,128)}, u32[]{:S(2)}) copy-start(f32[4,4,4]{2,1,0:T(4,128)} %param.11) | copy-start | bytes 772
  11.8 14.8 %collective-permute-start.3 = (bf16[2,2,2,256,256]{4,3,2,1,0:T(8,128)(2,1)}, bf16[2,2,2,256,256]{4,3,2,1,0:T(8,128)(2,1)}, u32[]{:S(2)}, u32[]{:S(2)}) collective-permute-start(bf16[2,2,2,256,256]{4,3,2,1,0:T(8,128)(2,1)} %get-tuple-element.35.refs_2_.refs_0_), channel_id=1, source_target_pairs={{0,1},{1,0},{2,3},{3,2},{4,5},{5,4},{6,7},{7,6},{8,9},{9,8},{10,11... | collective-permute-start | bytes 3145736 | tf_op jit(solution)/shard_map/core1/ppermute | solution.py:434
  12.0 29.4 %collective-permute-start.5 = (bf16[2,2,256,256]{3,2,1,0:T(8,128)(2,1)}, bf16[2,2,256,256]{3,2,1,0:T(8,128)(2,1)}, u32[]{:S(2)}, u32[]{:S(2)}) collective-permute-start(bf16[2,2,256,256]{3,2,1,0:T(8,128)(2,1)} %get-tuple-element.41), channel_id=1, source_target_pairs={{0,4},{4,8},{8,12},{12,16},{16,20},{20,24},{24,28},{1,5},{5,9},{9,... | collective-permute-start | bytes 1572872 | tf_op jit(solution)/shard_map/up1/ppermute | solution.py:434
  15.4 29.6 %collective-permute-start.6 = (bf16[2,2,256,256]{3,2,1,0:T(8,128)(2,1)}, bf16[2,2,256,256]{3,2,1,0:T(8,128)(2,1)}, u32[]{:S(2)}, u32[]{:S(2)}) collective-permute-start(bf16[2,2,256,256]{3,2,1,0:T(8,128)(2,1)} %get-tuple-element.42), channel_id=1, source_target_pairs={{4,0},{8,4},{12,8},{16,12},{20,16},{24,20},{28,24},{5,1},{9,5},{13... | collective-permute-start | bytes 1572872 | tf_op jit(solution)/shard_map/down1/ppermute | solution.py:434
  26.1 27.5 %collective-permute-start.1 = (bf16[2,2,2,256,256]{4,3,2,1,0:T(8,128)(2,1)}, bf16[2,2,2,256,256]{4,3,2,1,0:T(8,128)(2,1)}, u32[]{:S(2)}, u32[]{:S(2)}) collective-permute-start(bf16[2,2,2,256,256]{4,3,2,1,0:T(8,128)(2,1)} %get-tuple-element.36.refs_2_.refs_0_), channel_id=1, source_target_pairs={{0,2},{1,3},{2,0},{3,1},{4,6},{5,7},{6,4},{7,5},{8,10},{9,11},{10,... | collective-permute-start | bytes 3145736 | tf_op jit(solution)/shard_map/pair2/ppermute | solution.py:434
  31.7 3.1 %collective-permute-start.4 = (bf16[2,2,2,256,256]{4,3,2,1,0:T(8,128)(2,1)}, bf16[2,2,2,256,256]{4,3,2,1,0:T(8,128)(2,1)}, u32[]{:S(2)}, u32[]{:S(2)}) collective-permute-start(bf16[2,2,2,256,256]{4,3,2,1,0:T(8,128)(2,1)} %gate.13.refs_1_.refs_2_), channel_id=1, source_target_pairs={{0,1},{1,0},{2,3},{3,2},{4,5},{5,4},{6,7},{7,6},{8,9},{9,8},{10,11... | collective-permute-start | bytes 3145736 | tf_op jit(solution)/shard_map/core_pair0/ppermute | solution.py:434
  38.2 6.8 %collective-permute-start.7 = (bf16[2,2,2,256,256]{4,3,2,1,0:T(8,128)(2,1)}, bf16[2,2,2,256,256]{4,3,2,1,0:T(8,128)(2,1)}, u32[]{:S(2)}, u32[]{:S(2)}) collective-permute-start(bf16[2,2,2,256,256]{4,3,2,1,0:T(8,128)(2,1)} %get-tuple-element.48), channel_id=1, source_target_pairs={{0,1},{1,0},{2,3},{3,2},{4,5},{5,4},{6,7},{7,6},{8,9},{9,8},{10,11... | collective-permute-start | bytes 3145736 | tf_op jit(solution)/shard_map/core3/ppermute | solution.py:434
  38.3 40.5 %collective-permute-start.14 = (bf16[2,2,256,256]{3,2,1,0:T(8,128)(2,1)}, bf16[2,2,256,256]{3,2,1,0:T(8,128)(2,1)}, u32[]{:S(2)}, u32[]{:S(2)}) collective-permute-start(bf16[2,2,256,256]{3,2,1,0:T(8,128)(2,1)} %get-tuple-element.47.refs_1_), channel_id=1, source_target_pairs={{4,0},{8,4},{12,8},{16,12},{20,16},{24,20},{28,24},{5,1},{9,5},{13... | collective-permute-start | bytes 1572872 | tf_op jit(solution)/shard_map/down3/ppermute | solution.py:434
  41.4 33.6 %collective-permute-start.13 = (bf16[2,2,256,256]{3,2,1,0:T(8,128)(2,1)}, bf16[2,2,256,256]{3,2,1,0:T(8,128)(2,1)}, u32[]{:S(2)}, u32[]{:S(2)}) collective-permute-start(bf16[2,2,256,256]{3,2,1,0:T(8,128)(2,1)} %get-tuple-element.58), channel_id=1, source_target_pairs={{0,4},{4,8},{8,12},{12,16},{16,20},{20,24},{24,28},{1,5},{5,9},{9,... | collective-permute-start | bytes 1572872 | tf_op jit(solution)/shard_map/up3/ppermute | solution.py:434
  45.0 2.3 %collective-permute-start.8 = (bf16[2,2,256,256]{3,2,1,0:T(8,128)(2,1)}, bf16[2,2,256,256]{3,2,1,0:T(8,128)(2,1)}, u32[]{:S(2)}, u32[]{:S(2)}) collective-permute-start(bf16[2,2,256,256]{3,2,1,0:T(8,128)(2,1)} %get-tuple-element.49.refs_1_.refs_2_), channel_id=1, source_target_pairs={{0,1},{1,0},{2,3},{3,2},{4,5},{5,4},{6,7},{7,6},{8,9},{9,8},{10,11... | collective-permute-start | bytes 1572872 | tf_op jit(solution)/shard_map/core_up1/ppermute | solution.py:434
  45.1 3.0 %collective-permute-start.9 = (bf16[2,2,256,256]{3,2,1,0:T(8,128)(2,1)}, bf16[2,2,256,256]{3,2,1,0:T(8,128)(2,1)}, u32[]{:S(2)}, u32[]{:S(2)}) collective-permute-start(bf16[2,2,256,256]{3,2,1,0:T(8,128)(2,1)} %get-tuple-element.50.refs_3_), channel_id=1, source_target_pairs={{0,1},{1,0},{2,3},{3,2},{4,5},{5,4},{6,7},{7,6},{8,9},{9,8},{10,11... | collective-permute-start | bytes 1572872 | tf_op jit(solution)/shard_map/core_down1/ppermute | solution.py:434
  51.6 35.3 %collective-permute-start.12 = (bf16[2,2,2,256,256]{4,3,2,1,0:T(8,128)(2,1)}, bf16[2,2,2,256,256]{4,3,2,1,0:T(8,128)(2,1)}, u32[]{:S(2)}, u32[]{:S(2)}) collective-permute-start(bf16[2,2,2,256,256]{4,3,2,1,0:T(8,128)(2,1)} %late_sum.2.refs_4_), channel_id=1, source_target_pairs={{0,2},{1,3},{2,0},{3,1},{4,6},{5,7},{6,4},{7,5},{8,10},{9,11},{10,... | collective-permute-start | bytes 3145736 | tf_op jit(solution)/shard_map/pair1/ppermute | solution.py:434
  53.6 3.9 %collective-permute-start.10 = (bf16[2,2,2,256,256]{4,3,2,1,0:T(8,128)(2,1)}, bf16[2,2,2,256,256]{4,3,2,1,0:T(8,128)(2,1)}, u32[]{:S(2)}, u32[]{:S(2)}) collective-permute-start(bf16[2,2,2,256,256]{4,3,2,1,0:T(8,128)(2,1)} %get-tuple-element.51), channel_id=1, source_target_pairs={{0,1},{1,0},{2,3},{3,2},{4,5},{5,4},{6,7},{7,6},{8,9},{9,8},{10,11... | collective-permute-start | bytes 3145736 | tf_op jit(solution)/shard_map/core2/ppermute | solution.py:434
  53.6 44.2 %collective-permute-start.20 = (bf16[2,2,256,256]{3,2,1,0:T(8,128)(2,1)}, bf16[2,2,256,256]{3,2,1,0:T(8,128)(2,1)}, u32[]{:S(2)}, u32[]{:S(2)}) collective-permute-start(bf16[2,2,256,256]{3,2,1,0:T(8,128)(2,1)} %get-tuple-element.63), channel_id=1, source_target_pairs={{0,4},{4,8},{8,12},{12,16},{16,20},{20,24},{24,28},{1,5},{5,9},{9,... | collective-permute-start | bytes 1572872 | tf_op jit(solution)/shard_map/up0/ppermute | solution.py:434
  59.7 42.5 %all-to-all-start = ((f32[32,8,128]{2,1,0:T(8,128)}), f32[32,8,128]{2,1,0:T(8,128)}, u32[]{:S(2)}, u32[]{:S(2)}) async-start(f32[32,8,128]{2,1,0:T(8,128)} %range_parts.1.refs_1_), calls=%async_computation | async-start | bytes 262144 | tf_op jit(solution)/shard_map/all_to_all | solution.py:503
  65.2 3.1 %collective-permute-start.11 = (bf16[2,2,2,256,256]{4,3,2,1,0:T(8,128)(2,1)}, bf16[2,2,2,256,256]{4,3,2,1,0:T(8,128)(2,1)}, u32[]{:S(2)}, u32[]{:S(2)}) collective-permute-start(bf16[2,2,2,256,256]{4,3,2,1,0:T(8,128)(2,1)} %gate.21.refs_1_.refs_2_), channel_id=1, source_target_pairs={{0,1},{1,0},{2,3},{3,2},{4,5},{5,4},{6,7},{7,6},{8,9},{9,8},{10,11... | collective-permute-start | bytes 3145736 | tf_op jit(solution)/shard_map/core_pair2/ppermute | solution.py:434
  68.3 29.5 %collective-permute-start.21 = (bf16[2,2,256,256]{3,2,1,0:T(8,128)(2,1)}, bf16[2,2,256,256]{3,2,1,0:T(8,128)(2,1)}, u32[]{:S(2)}, u32[]{:S(2)}) collective-permute-start(bf16[2,2,256,256]{3,2,1,0:T(8,128)(2,1)} %get-tuple-element.64), channel_id=1, source_target_pairs={{4,0},{8,4},{12,8},{16,12},{20,16},{24,20},{28,24},{5,1},{9,5},{13... | collective-permute-start | bytes 1572872 | tf_op jit(solution)/shard_map/down0/ppermute | solution.py:434
  78.8 2.3 %collective-permute-start.15 = (bf16[2,2,256,256]{3,2,1,0:T(8,128)(2,1)}, bf16[2,2,256,256]{3,2,1,0:T(8,128)(2,1)}, u32[]{:S(2)}, u32[]{:S(2)}) collective-permute-start(bf16[2,2,256,256]{3,2,1,0:T(8,128)(2,1)} %get-tuple-element.59.refs_1_.refs_2_), channel_id=1, source_target_pairs={{0,1},{1,0},{2,3},{3,2},{4,5},{5,4},{6,7},{7,6},{8,9},{9,8},{10,11... | collective-permute-start | bytes 1572872 | tf_op jit(solution)/shard_map/core_up3/ppermute | solution.py:434
  78.8 3.0 %collective-permute-start.16 = (bf16[2,2,256,256]{3,2,1,0:T(8,128)(2,1)}, bf16[2,2,256,256]{3,2,1,0:T(8,128)(2,1)}, u32[]{:S(2)}, u32[]{:S(2)}) collective-permute-start(bf16[2,2,256,256]{3,2,1,0:T(8,128)(2,1)} %get-tuple-element.60.refs_3_), channel_id=1, source_target_pairs={{0,1},{1,0},{2,3},{3,2},{4,5},{5,4},{6,7},{7,6},{8,9},{9,8},{10,11... | collective-permute-start | bytes 1572872 | tf_op jit(solution)/shard_map/core_down3/ppermute | solution.py:434
  85.4 25.5 %collective-permute-start.19 = (bf16[2,2,2,256,256]{4,3,2,1,0:T(8,128)(2,1)}, bf16[2,2,2,256,256]{4,3,2,1,0:T(8,128)(2,1)}, u32[]{:S(2)}, u32[]{:S(2)}) collective-permute-start(bf16[2,2,2,256,256]{4,3,2,1,0:T(8,128)(2,1)} %late_sum.3.refs_3_), channel_id=1, source_target_pairs={{0,2},{1,3},{2,0},{3,1},{4,6},{5,7},{6,4},{7,5},{8,10},{9,11},{10,... | collective-permute-start | bytes 3145736 | tf_op jit(solution)/shard_map/pair3/ppermute | solution.py:434
  86.9 28.8 %collective-permute-start.17 = (bf16[2,2,256,256]{3,2,1,0:T(8,128)(2,1)}, bf16[2,2,256,256]{3,2,1,0:T(8,128)(2,1)}, u32[]{:S(2)}, u32[]{:S(2)}) collective-permute-start(bf16[2,2,256,256]{3,2,1,0:T(8,128)(2,1)} %get-tuple-element.61), channel_id=1, source_target_pairs={{0,4},{4,8},{8,12},{12,16},{16,20},{20,24},{24,28},{1,5},{5,9},{9,... | collective-permute-start | bytes 1572872 | tf_op jit(solution)/shard_map/up2/ppermute | solution.py:434
  88.8 26.9 %collective-permute-start.18 = (bf16[2,2,256,256]{3,2,1,0:T(8,128)(2,1)}, bf16[2,2,256,256]{3,2,1,0:T(8,128)(2,1)}, u32[]{:S(2)}, u32[]{:S(2)}) collective-permute-start(bf16[2,2,256,256]{3,2,1,0:T(8,128)(2,1)} %get-tuple-element.62), channel_id=1, source_target_pairs={{4,0},{8,4},{12,8},{16,12},{20,16},{24,20},{28,24},{5,1},{9,5},{13... | collective-permute-start | bytes 1572872 | tf_op jit(solution)/shard_map/down2/ppermute | solution.py:434

commit v2 on v1

--- a/solution.py
+++ b/solution.py
@@ -7,11 +7,12 @@
 from jax.experimental.pallas import tpu as pltpu
 from jax.sharding import PartitionSpec as P
 
-CHUNKS = (("early", 0, 2), ("late", 2, 2), ("early", 4, 2), ("late", 6, 2))
+CHUNKS = (("late", 0, 2), ("early", 2, 2), ("late", 4, 2), ("early", 6, 2))
 VMEM = 63 * 2**20
 TILE = 16
 UNROLL = 4
 ANY = pl.BlockSpec(memory_space=pltpu.HBM)
+LOOSE = pl.BlockSpec(memory_space=pl.ANY)
 FACTOR = 100.0
 
 
@@ -23,6 +24,10 @@
 
 F32 = jnp.float32
 BF16 = jnp.bfloat16
+
+
+def unread(values):
+    return [ANY if value.size > 2**16 else LOOSE for value in values]
 
 
 def dot(left, right, transpose=False):
@@ -124,7 +129,7 @@
             pl.BlockSpec((1, 2, energies, width, width), lambda i: (last, 0, 0, 0, 0))
         )
     args.extend(after)
-    in_specs.extend([ANY] * len(after))
+    in_specs.extend(unread(after))
     out_shape = [
         jax.ShapeDtypeStruct((count, 2, energies, width, width), BF16),
         jax.ShapeDtypeStruct((count, 8, width), F32),
@@ -153,23 +158,23 @@
     )(*args)
 
 
-def grid_spec(energies, width):
-    return pl.BlockSpec((1, 2, energies, width, width), lambda i: (i, 0, 0, 0, 0))
-
-
-def edge_spec(width):
-    return pl.BlockSpec((1, 2, width, width), lambda i: (i, 0, 0, 0))
-
-
-def early_members(*blocks):
+def grid_spec(energies, width, base=0):
+    return pl.BlockSpec((1, 2, energies, width, width), lambda i: (base + i, 0, 0, 0, 0))
+
+
+def edge_spec(width, base=0):
+    return pl.BlockSpec((1, 2, width, width), lambda i: (base + i, 0, 0, 0))
+
+
+def early_members(blocks, base=0):
     count, _, energies, width, _ = blocks[0].shape
-    return list(blocks), [grid_spec(energies, width)] * 4
-
-
-def late_members(own, other, *edges):
-    count, _, energies, width, _ = own.shape
-    specs = [grid_spec(energies, width)] * 2 + [edge_spec(width)] * 4
-    return [own, other, *edges], specs
+    return list(blocks), [grid_spec(energies, width, base)] * 4
+
+
+def late_members(blocks, base=0):
+    count, _, energies, width, _ = blocks[0].shape
+    specs = [grid_spec(energies, width, base)] * 2 + [edge_spec(width, base)] * 4
+    return list(blocks), specs
 
 
 def gate_kernel(*refs):
@@ -180,7 +185,7 @@
     count = len(values)
     return pl.pallas_call(
         gate_kernel,
-        in_specs=[ANY] * (count + len(after)),
+        in_specs=[ANY] * count + unread(after),
         out_specs=[ANY] * count,
         out_shape=[jax.ShapeDtypeStruct(value.shape, value.dtype) for value in values],
         input_output_aliases={i: i for i in range(count)},
@@ -227,13 +232,13 @@
 
 
 def early_edges(weights, members, after):
-    args, specs = early_members(*members)
+    args, specs = early_members(members)
     count, _, energies, width, _ = args[0].shape
     edge = jax.ShapeDtypeStruct((count, 2, width, width), BF16)
     return pl.pallas_call(
         early_edges_kernel,
         grid=(count,),
-        in_specs=[pl.BlockSpec(memory_space=pltpu.SMEM)] + specs + [ANY] * len(after),
+        in_specs=[pl.BlockSpec(memory_space=pltpu.SMEM)] + specs + unread(after),
         out_specs=[edge_spec(width)] * 2,
         out_shape=[edge, edge],
         compiler_params=pltpu.CompilerParams(vmem_limit_bytes=VMEM),
@@ -253,43 +258,66 @@
     return lines
 
 
-def late_sum_kernel(w_ref, *refs):
-    members, out_ref = refs[:6], refs[-1]
+def late_sum_kernel(pieces, w_ref, *refs):
+    members, outs = refs[:6], refs[-pieces:]
     energies, width = members[0].shape[2:4]
     w = [[w_ref[1, o, j] for j in range(2)] for o in range(3)]
 
-    @tiles(width)
-    def _(part, rows):
-        line = late_line(members, part, rows)
-        for e in range(energies):
-            terms = [(w[o][j], line[j][e + o]) for j in range(2) for o in range(3)]
-            out_ref[0, part, e, rows, :] = weighted(terms).astype(BF16)
-
-
-def late_sum(weights, members, after):
-    args, specs = late_members(*members)
+    def fill(out_ref):
+        @tiles(width)
+        def _(part, rows):
+            line = late_line(members, part, rows)
+            for e in range(energies):
+                terms = [(w[o][j], line[j][e + o]) for j in range(2) for o in range(3)]
+                out_ref[0, part, e, rows, :] = weighted(terms).astype(BF16)
+
+    if pieces == 1:
+        fill(outs[0])
+    else:
+        for index in range(pieces):
+            pl.when(pl.program_id(0) == index)(functools.partial(fill, outs[index]))
+
+
+def late_sum(weights, members, after, apart=False):
+    args, specs = late_members(members)
     count, _, energies, width, _ = args[0].shape
+    shape = jax.ShapeDtypeStruct(args[0].shape, BF16)
+    out_shape, out_specs = [shape], [grid_spec(energies, width)]
+    if apart:
+        one = pl.BlockSpec((1, 2, energies, width, width), lambda i: (0, 0, 0, 0, 0))
+        out_shape = [jax.ShapeDtypeStruct((1,) + args[0].shape[1:], BF16)] * count
+        out_specs = [one] * count
     return pl.pallas_call(
-        late_sum_kernel,
+        functools.partial(late_sum_kernel, len(out_shape)),
         grid=(count,),
-        in_specs=[pl.BlockSpec(memory_space=pltpu.SMEM)] + specs + [ANY] * len(after),
-        out_specs=grid_spec(energies, width),
-        out_shape=jax.ShapeDtypeStruct(args[0].shape, BF16),
+        in_specs=[pl.BlockSpec(memory_space=pltpu.SMEM)] + specs + unread(after),
+        out_specs=out_specs,
+        out_shape=out_shape,
         compiler_params=pltpu.CompilerParams(vmem_limit_bytes=VMEM),
         cost_estimate=cost(1.8 * count),
         name="late_sum",
     )(weights, *args, *after)
 
 
-def finish_kernel(late, w_ref, across_ref, down_ref, *refs):
-    members, received, out_ref = refs[: 6 if late else 4], refs[6:7] if late else refs[4:6], refs[-1]
+def finish_kernel(late, charged, w_ref, across_ref, *refs):
+    members, received = refs[: 6 if late else 4], refs[6:7] if late else refs[4:6]
+    out_ref, down_ref = refs[-3 if charged else -2], refs[-1]
+    if charged:
+        parts_ref, charge_ref = refs[7 if late else 6], refs[-2]
+
+        @pl.when(pl.program_id(0) == 0)
+        def _():
+            charge_ref[0] = jnp.sum(parts_ref[...])
+
     energies, width = members[0].shape[2:4]
     w = [[w_ref[0, o, j] for j in range(4)] for o in range(3)]
     across = across_ref[0]
+    lanes = down_ref.shape[1]
+    down_ref[...] = jnp.transpose(jnp.broadcast_to(across, (lanes, width)))
 
     @tiles(width)
     def _(part, rows):
-        scale = down_ref[rows, :] * across
+        scale = jnp.concatenate([down_ref[rows, :]] * (width // lanes), axis=1) * across
         if late:
             line = late_line(members, part, rows)
         else:
@@ -313,31 +341,42 @@
             out_ref[part, e, 0, rows, :] = (weighted(terms) * scale).astype(BF16)
 
 
-def finish(sigma, shape, start, weights, across, down, late, members, received, after):
-    args, specs = late_members(*members) if late else early_members(*members)
-    count, _, energies, width, _ = args[0].shape
-    args = [weights, across, down, *args, *received, *after]
+def finish(sigma, shape, start, weights, across, late, members, received, after, base, parts):
+    args, specs = late_members(members, base) if late else early_members(members, base)
+    _, _, energies, width, _ = args[0].shape
+    count = received[0].shape[0]
+    args = [weights, across, *args, *received]
     in_specs = [
         pl.BlockSpec(memory_space=pltpu.SMEM),
-        pl.BlockSpec((1, 1, width), lambda i: (start + i, 0, 0)),
-        pl.BlockSpec((width, 1), lambda i: (start + i, 0)),
+        pl.BlockSpec((1, 1, width), lambda i: (start + base + i, 0, 0)),
     ] + specs
     in_specs += [grid_spec(energies, width)] if late else [edge_spec(width)] * 2
-    in_specs += [ANY] * len(after)
+    out_shape = [jax.ShapeDtypeStruct(shape, BF16)]
+    out_specs = [
+        pl.BlockSpec(
+            (2, energies, 1, width, width), lambda i: (0, 0, 0, start + base + i, 0)
+        )
+    ]
+    if parts is not None:
+        args.append(parts)
+        in_specs.append(pl.BlockSpec(parts.shape, lambda i: (0,) * parts.ndim))
+        out_shape.append(jax.ShapeDtypeStruct((1,), F32))
+        out_specs.append(pl.BlockSpec(memory_space=pltpu.SMEM))
+    args += after
+    in_specs += unread(after)
     aliases = {}
     if sigma is not None:
         aliases = {len(args): 0}
         args.append(sigma)
         in_specs.append(ANY)
     return pl.pallas_call(
-        functools.partial(finish_kernel, late),
+        functools.partial(finish_kernel, late, parts is not None),
         grid=(count,),
         in_specs=in_specs,
-        out_specs=pl.BlockSpec(
-            (2, energies, 1, width, width), lambda i: (0, 0, 0, start + i, 0)
-        ),
-        out_shape=jax.ShapeDtypeStruct(shape, BF16),
+        out_specs=out_specs,
+        out_shape=out_shape,
         input_output_aliases=aliases,
+        scratch_shapes=[pltpu.VMEM((width, 128), F32)],
         compiler_params=pltpu.CompilerParams(vmem_limit_bytes=VMEM),
         cost_estimate=cost(2.2 * count),
         name="finish",
@@ -362,7 +401,7 @@
         for offset, value in pieces:
             inside = (lanes >= begin - offset) & (lanes < end - offset)
             total = total + jnp.where(inside, value, 0.0)
-        out_ref[d] = -total
+        out_ref[d] = -jnp.sum(total, axis=0, keepdims=True)
         return end
 
     lax.fori_loop(0, out_ref.shape[0], one_range, jnp.int32(0))
@@ -374,30 +413,13 @@
         functools.partial(range_parts_kernel, len(densities)),
         in_specs=[pl.BlockSpec(memory_space=pltpu.SMEM)]
         + [pl.BlockSpec(memory_space=pltpu.VMEM)] * len(densities)
-        + [ANY] * len(after),
+        + unread(after),
         out_specs=pl.BlockSpec(memory_space=pltpu.VMEM),
-        out_shape=jax.ShapeDtypeStruct((devices, 8, 128), F32),
+        out_shape=jax.ShapeDtypeStruct((devices, 1, 128), F32),
         compiler_params=pltpu.CompilerParams(vmem_limit_bytes=VMEM),
         cost_estimate=cost(2.2),
         name="range_parts",
     )(range_rows, *densities, *after)
-
-
-def range_total_kernel(parts_ref, *refs):
-    out_ref = refs[-1]
-    out_ref[0] = jnp.sum(parts_ref[...])
-
-
-def range_total(received, after):
-    return pl.pallas_call(
-        range_total_kernel,
-        in_specs=[pl.BlockSpec(memory_space=pltpu.VMEM)] + [ANY] * len(after),
-        out_specs=pl.BlockSpec(memory_space=pltpu.SMEM),
-        out_shape=jax.ShapeDtypeStruct((1,), F32),
-        compiler_params=pltpu.CompilerParams(vmem_limit_bytes=VMEM),
-        cost_estimate=cost(1),
-        name="range_total",
-    )(received, *after)
 
 
 def own_weights(shifts, emission, absorption):
@@ -441,7 +463,6 @@
 
     weights = own_weights(shifts, emission_weight, absorption_weight)
     across_scale = deform_potential.reshape(-1, 1, width)
-    down_scale = deform_potential.reshape(-1, 1)
 
     def run(chunk, previous, after=(), again=False):
         kind, start, count = CHUNKS[chunk]
@@ -455,7 +476,7 @@
     def fall(value, name):
         return send(value, "energy", down, "down" + name)
 
-    def done(sigma, chunk, members, got, after=()):
+    def done(sigma, chunk, members, got, after=(), base=0, parts=None):
         kind, start, _ = CHUNKS[chunk]
         return finish(
             sigma,
@@ -463,65 +484,65 @@
             start,
             weights,
             across_scale,
-            down_scale,
             kind == "late",
             members,
             got,
             after,
+            base,
+            parts,
         )
 
-    g0, n0 = run(0, None)
-    y0, c0 = pair(g0, "pair0"), core(g0, "core0")
-    g1, n1, low1, high1 = run(1, g0)
-    up1, down1, c1 = rise(high1, "1"), fall(low1, "1"), core(g1, "core1")
-    g2, n2, h2 = run(2, g1, (c0,), True)
-    y2 = pair(g2, "pair2")
-    g3, n3, low3, high3, h3 = run(3, g2, (c1,), True)
-
-    (y0,) = gate([y0], (g3,))
-    core_y0 = core(y0, "core_pair0")
-    (c0,) = gate([c0], (y0,))
-    members0 = (g0, c0, y0, core_y0)
-    high0, low0 = early_edges(weights, members0, ())
-
-    low3, high3, h3 = gate([low3, high3, h3], (low0,))
-    up3, down3, c3 = rise(high3, "3"), fall(low3, "3"), core(h3, "core3")
-    (n0,) = gate([n0], (low3,))
-
-    up1, down1 = gate([up1, down1], (n0, c3))
-    core_up1, core_down1 = core(up1, "core_up1"), core(down1, "core_down1")
-    (c1,) = gate([c1], (up1,))
-    members1 = (g1, c1, up1, down1, core_up1, core_down1)
-    total1 = late_sum(weights, members1, ())
-    x1 = pair(total1, "pair1")
-
-    y2, high0, low0, h2 = gate([y2, high0, low0, h2], (total1,))
-    up0, down0, c2 = rise(high0, "0"), fall(low0, "0"), core(h2, "core2")
-
-    (n1,) = gate([n1], (y2,))
-    parts = range_parts(range_rows, [n0, n1, n2, n3], (c2,))
+    g0, n0, low0, high0 = run(0, None)
+    up0, c0, beat0 = rise(high0, "0"), core(g0, "core0"), core(n0, "beat0")
+    g1, n1 = run(1, g0, (beat0,))
+    y1, c1 = pair(g1, "pair1"), core(g1, "core1")
+    (low0,) = gate([low0], (g1,))
+    down0 = fall(low0, "0")
+    g2, n2, low2, high2, h2 = run(2, g1, (c0,), True)
+    g3, n3, h3 = run(3, g2, (c1,), True)
+    y3 = pair(g3, "pair3")
+
+    low2, high2, h2 = gate([low2, high2, h2], (g3,))
+    up2, down2, c2 = rise(high2, "2"), fall(low2, "2"), core(h2, "core2")
+    (n0,) = gate([n0], (low2,))
+
+    up0, down0 = gate([up0, down0], (n0, c2))
+    core_up0, core_down0 = core(up0, "core_up0"), core(down0, "core_down0")
+    (c0,) = gate([c0], (up0,))
+    members0 = (g0, c0, up0, down0, core_up0, core_down0)
+    (total0,) = late_sum(weights, members0, ())
+    x0 = pair(total0, "pair0")
+
+    (y1,) = gate([y1], (total0,))
+    core_y1 = core(y1, "core_pair1")
+    (c1,) = gate([c1], (y1,))
+    members1 = (g1, c1, y1, core_y1)
+    high1, low1 = early_edges(weights, members1, ())
+    high1, low1, h3 = gate([high1, low1, h3], ())
+    up1, down1, c3 = rise(high1, "1"), fall(low1, "1"), core(h3, "core3")
+    (n1,) = gate([n1], (low1,))
+    (n2,) = gate([n2], (n1, c3))
+
+    up2, down2 = gate([up2, down2], (n2,))
+    core_up2, core_down2 = core(up2, "core_up2"), core(down2, "core_down2")
+    (c2,) = gate([c2], (up2,))
+    members2 = (g2, c2, up2, down2, core_up2, core_down2)
+    (total2,) = late_sum(weights, members2, ())
+    x2 = pair(total2, "pair2")
+
+    (y3,) = gate([y3], (total2,))
+    core_y3 = core(y3, "core_pair3")
+    (c3,) = gate([c3], (y3,))
+    members3 = (g3, c3, y3, core_y3)
+    high3, low3 = early_edges(weights, members3, ())
+    up3, down3 = rise(high3, "3"), fall(low3, "3")
+
+    parts = range_parts(range_rows, [n0, n1, n2, n3], (low3,))
     received = lax.all_to_all(parts, ("energy", "mom"), split_axis=0, concat_axis=0, tiled=True)
-
-    (y2,) = gate([y2], (parts,))
-    core_y2 = core(y2, "core_pair2")
-    (c2,) = gate([c2], (y2,))
-    members2 = (g2, c2, y2, core_y2)
-    high2, low2 = early_edges(weights, members2, ())
-
-    up3, down3 = gate([up3, down3], (low2,))
-    core_up3, core_down3 = core(up3, "core_up3"), core(down3, "core_down3")
-    (c3,) = gate([c3], (up3,))
-    members3 = (g3, c3, up3, down3, core_up3, core_down3)
-    total3 = late_sum(weights, members3, ())
-    x3 = pair(total3, "pair3")
-    x1, high2, low2 = gate([x1, high2, low2], (total3,))
-    up2, down2 = rise(high2, "2"), fall(low2, "2")
-
-    sigma = done(None, 1, members1, (x1,))
-    sigma = done(sigma, 0, members0, (up0, down0))
-    charge = range_total(received, (sigma,))
-    sigma = done(sigma, 3, members3, (x3,), (charge,))
-    sigma = done(sigma, 2, members2, (up2, down2))
+    (sigma,) = done(None, 0, members0, (x0,), (parts,))
+    (sigma,) = done(sigma, 1, members1, (up1, down1))
+    (sigma,) = done(sigma, 3, members3, (up3, down3))
+    sigma, charge = done(sigma, 2, members2, (x2,), (), 0, received)
     return sigma, charge
 
 

time: 121 us -> 116 us (0.959)
  starting transfers between devices: 39.5 us -> 36.1 us
    ppermute x22 -> x23, starting transfers between devices: 34 us -> 30.6 us  [send(): return lax.ppermute(value, axis, pairs)]
    reshape x1 -> x0, local copies, waits for them, and re-layouts: 1.37 us -> none  [body(): down_scale = deform_potential.reshape(-1, 1)]
    ppermute x22 -> x23, waiting for transfers between devices: 22.1 us -> 21.1 us  [send(): return lax.ppermute(value, axis, pairs)]
  transfers between devices with their start and end apart: 23 -> 24, of which waited for: 9 -> 10; matrix products, arithmetic and copies ran while one was open for 2% -> 1% of each run, Pallas kernels for 38% -> 39%
where the time goes in v2:
time: 116 us; the launch traced here: 114 us
  Pallas kernels  54.4 us (47%)
  starting transfers between devices  36.1 us (31%)
  waiting for transfers between devices  21.1 us (18%)
    ppermute x23, starting transfers between devices, send(): return lax.ppermute(value, axis, pairs)  30.6 us
    ppermute x23, waiting for transfers between devices, send(): return lax.ppermute(value, axis, pairs)  21.1 us
    pallas_call x4, Pallas kernels, solve(): pl.pallas_call(functools.partial(solve_kernel, first, edges, again), grid...  19.6 us
    pallas_call x4, Pallas kernels, finish(): pl.pallas_call(functools.partial(finish_kernel, late, parts is not None),...  18.4 us
    pallas_call x2, Pallas kernels, late_sum(): pl.pallas_call(functools.partial(late_sum_kernel, len(out_shape)), grid=(...  7.15 us
    pallas_call x2, Pallas kernels, early_edges(): pl.pallas_call(early_edges_kernel, grid=(count,), in_specs=[pl.BlockSpec(...  6.84 us
    all_to_all x1, starting transfers between devices, body(): lax.all_to_all(parts, ('energy', 'mom'), split_axis=0, concat_axis=0, til...  5.45 us
    pallas_call x1, Pallas kernels, range_parts(): pl.pallas_call(functools.partial(range_parts_kernel, len(densities)), in_...  2.37 us
  transfers between devices with their start and end apart: 24, of which 10 were waited for; matrix products, arithmetic and copies ran while one was open for 1% of the time, Pallas kernels for 39%

profile of v2, /device:TPU:24, one launch (start us, length us, event | category | flops | bytes accessed | tf_op | source)
XLA Modules:
  0.0 114.1 jit_solution(7775200835630348368)
XLA Ops:
  0.7 4.8 %solve.4 = (bf16[2,2,2,256,256]{4,3,2,1,0:T(8,128)(2,1)}, f32[2,8,256]{2,1,0:T(8,128)}, bf16[2,2,256,256]{3,2,1,0:T(8,128)(2,1)}, bf16[2,2,256,256]{3,2,1,0:T(8,128)(2,1)}) custom-call(bf16[2,2,1,2048,256]{4,3,2,1,0:T(8,128)(2,1)} %refs_0_.7, bf16[2,1,2048,256]{3,2,1,0:T(8,128)(2,1)} %refs_1_.7), custom_call_target="tpu_custom_call" | custom-call | flops 575000018944 | tf_op jit(solution)/shard_map/solve/pallas_call | solution.py:148
  5.5 0.0 collective-permute-start
  5.5 3.4 %collective-permute-start.7 = (bf16[2,2,256,256]{3,2,1,0:T(8,128)(2,1)}, bf16[2,2,256,256]{3,2,1,0:T(8,128)(2,1)}, u32[]{:S(2)}, u32[]{:S(2)}) collective-permute-start(bf16[2,2,256,256]{3,2,1,0:T(8,128)(2,1)} %get-tuple-element.43), channel_id=1, source_target_pairs={{0,4},{4,8},{8,12},{12,16},{16,20},{20,24},{24,28},{1,5},{5,9},{9,... | collective-permute-start | bytes 1572872 | tf_op jit(solution)/shard_map/up0/ppermute | solution.py:456
  8.9 0.3 collective-permute-start.1
  9.2 0.1 compare_convert_fusion
  9.2 0.1 fusion
  9.3 0.1 add_reduce_fusion.1
  9.4 0.1 broadcast_multiply_fusion
  9.5 0.7 multiply_reduce_fusion.w_ref
  10.2 0.0 collective-permute-done.refs_3_
  10.2 0.6 copy-done.3
  10.8 4.7 %solve.5 = (bf16[2,2,2,256,256]{4,3,2,1,0:T(8,128)(2,1)}, f32[2,8,256]{2,1,0:T(8,128)}) custom-call(bf16[2,2,1,2048,256]{4,3,2,1,0:T(8,128)(2,1)} %refs_0_.7, bf16[2,1,2048,256]{3,2,1,0:T(8,128)(2,1)} %refs_1_.7, bf16[2,2,2,256,256]{4,3,2,1,0:T(8,128)(2,1)} %get-tuple-element.30.refs_2_.refs_0_, f32[2,8,256]{2,1,0:T(8,128)} %copy-done.3), custom_call_target="tpu_custom_call" | custom-call | flops 575000018944 | tf_op jit(solution)/shard_map/solve/pallas_call | solution.py:148
  15.5 1.5 %collective-permute-start.6 = (bf16[2,2,2,256,256]{4,3,2,1,0:T(8,128)(2,1)}, bf16[2,2,2,256,256]{4,3,2,1,0:T(8,128)(2,1)}, u32[]{:S(2)}, u32[]{:S(2)}) collective-permute-start(bf16[2,2,2,256,256]{4,3,2,1,0:T(8,128)(2,1)} %get-tuple-element.32.refs_2_.refs_1_.refs_0_), channel_id=1, source_target_pairs={{0,2},{1,3},{2,0},{3,1},{4,6},{5,7},{6,4},{7,5},{8,10},{9,11},{10,... | collective-permute-start | bytes 3145736 | tf_op jit(solution)/shard_map/pair1/ppermute | solution.py:456
  17.1 0.0 collective-permute-start.2
  17.1 3.3 %collective-permute-start.8 = (bf16[2,2,256,256]{3,2,1,0:T(8,128)(2,1)}, bf16[2,2,256,256]{3,2,1,0:T(8,128)(2,1)}, u32[]{:S(2)}, u32[]{:S(2)}) collective-permute-start(bf16[2,2,256,256]{3,2,1,0:T(8,128)(2,1)} %gate.15), channel_id=1, source_target_pairs={{4,0},{8,4},{12,8},{16,12},{20,16},{24,20},{28,24},{5,1},{9,5},{13... | collective-permute-start | bytes 1572872 | tf_op jit(solution)/shard_map/down0/ppermute | solution.py:456
  20.4 0.0 collective-permute-done.1.refs_3_.refs_0_
  20.4 5.1 %solve.6 = (bf16[2,2,2,256,256]{4,3,2,1,0:T(8,128)(2,1)}, f32[2,8,256]{2,1,0:T(8,128)}, bf16[2,2,256,256]{3,2,1,0:T(8,128)(2,1)}, bf16[2,2,256,256]{3,2,1,0:T(8,128)(2,1)}, bf16[2,2,2,256,256]{4,3,2,1,0:T(8,128)(2,1)}) custom-call(bf16[2,2,1,2048,256]{4,3,2,1,0:T(8,128)(2,1)} %refs_0_.7, bf16[2,1,2048,256]{3,2,1,0:T(8,128)(2,1)} %refs_1_.7, ...), custom_call_target="tpu_custom_call" | custom-call | flops 575000018944 | tf_op jit(solution)/shard_map/solve/pallas_call | solution.py:148
  25.6 0.0 collective-permute-done.2.refs_3_.refs_0_
  25.6 4.9 %solve.7 = (bf16[2,2,2,256,256]{4,3,2,1,0:T(8,128)(2,1)}, f32[2,8,256]{2,1,0:T(8,128)}, bf16[2,2,2,256,256]{4,3,2,1,0:T(8,128)(2,1)}) custom-call(bf16[2,2,1,2048,256]{4,3,2,1,0:T(8,128)(2,1)} %refs_0_.7, bf16[2,1,2048,256]{3,2,1,0:T(8,128)(2,1)} %refs_1_.7, bf16[2,2,2,256,256]{4,3,2,1,0:T(8,128)(2,1)} %get-tuple-element.33.refs_2_.refs_0_, ...), custom_call_target="tpu_custom_call" | custom-call | flops 575000018944 | tf_op jit(solution)/shard_map/solve/pallas_call | solution.py:148
  30.5 0.2 collective-permute-start.3
  30.7 2.4 %collective-permute-start.5 = (bf16[2,2,256,256]{3,2,1,0:T(8,128)(2,1)}, bf16[2,2,256,256]{3,2,1,0:T(8,128)(2,1)}, u32[]{:S(2)}, u32[]{:S(2)}) collective-permute-start(bf16[2,2,256,256]{3,2,1,0:T(8,128)(2,1)} %get-tuple-element.40.refs_1_), channel_id=1, source_target_pairs={{4,0},{8,4},{12,8},{16,12},{20,16},{24,20},{28,24},{5,1},{9,5},{13... | collective-permute-start | bytes 1572872 | tf_op jit(solution)/shard_map/down2/ppermute | solution.py:456
  33.1 0.0 collective-permute-done.7.refs_0_
  33.1 0.6 collective-permute-start.16
  33.7 0.4 collective-permute-done.8.refs_1_
  34.1 0.0 collective-permute-done.3.refs_3_.refs_0_
  34.1 0.1 collective-permute-start.10
  34.2 0.4 collective-permute-start.9
  34.7 1.7 %collective-permute-done.10.refs_5_ = bf16[2,2,256,256]{3,2,1,0:T(8,128)(2,1)} collective-permute-done((bf16[2,2,256,256]{3,2,1,0:T(8,128)(2,1)}, bf16[2,2,256,256]{3,2,1,0:T(8,128)(2,1)}, u32[]{:S(2)}, u32[]{:S(2)}) %collective-permute-start.10) | collective-permute-done | bytes 524320 | tf_op jit(solution)/shard_map/core_down0/ppermute | solution.py:456
  36.4 3.7 %collective-permute-start.4 = (bf16[2,2,256,256]{3,2,1,0:T(8,128)(2,1)}, bf16[2,2,256,256]{3,2,1,0:T(8,128)(2,1)}, u32[]{:S(2)}, u32[]{:S(2)}) collective-permute-start(bf16[2,2,256,256]{3,2,1,0:T(8,128)(2,1)} %get-tuple-element.39), channel_id=1, source_target_pairs={{0,4},{4,8},{8,12},{12,16},{16,20},{20,24},{24,28},{1,5},{5,9},{9,... | collective-permute-start | bytes 1572872 | tf_op jit(solution)/shard_map/up2/ppermute | solution.py:456
  40.1 0.0 collective-permute-done.9.refs_4_
  40.1 3.6 %late_sum.2.refs_1_ = bf16[2,2,2,256,256]{4,3,2,1,0:T(8,128)(2,1)} custom-call(f32[2,3,4]{2,1,0:T(4,128)} %multiply_reduce_fusion.w_ref, bf16[2,2,2,256,256]{4,3,2,1,0:T(8,128)(2,1)} %get-tuple-element.30.refs_2_.refs_0_, bf16[2,2,2,256,256]{4,3,2,1,0:T(8,128)(2,1)} %gate.18.refs_1_, bf16[2,2,256,256]{3,2,1,0:T(8,128)(2,1)} %get-tuple-element.45.refs_1_.refs_2_, ...), custom_call_target="tpu_custom_call" | custom-call | flops 413999988736 | tf_op jit(solution)/shard_map/late_sum/pallas_call | solution.py:290
  43.7 1.5 %collective-permute-start.22 = (bf16[2,2,2,256,256]{4,3,2,1,0:T(8,128)(2,1)}, bf16[2,2,2,256,256]{4,3,2,1,0:T(8,128)(2,1)}, u32[]{:S(2)}, u32[]{:S(2)}) collective-permute-start(bf16[2,2,2,256,256]{4,3,2,1,0:T(8,128)(2,1)} %late_sum.2.refs_1_), channel_id=1, source_target_pairs={{0,2},{1,3},{2,0},{3,1},{4,6},{5,7},{6,4},{7,5},{8,10},{9,11},{10,... | collective-permute-start | bytes 3145736 | tf_op jit(solution)/shard_map/pair0/ppermute | solution.py:456
  45.2 0.0 collective-permute-done.6.refs_0_
  45.2 0.0 collective-permute-start.11
  45.2 3.0 %collective-permute-done.11.refs_3_ = bf16[2,2,2,256,256]{4,3,2,1,0:T(8,128)(2,1)} collective-permute-done((bf16[2,2,2,256,256]{4,3,2,1,0:T(8,128)(2,1)}, bf16[2,2,2,256,256]{4,3,2,1,0:T(8,128)(2,1)}, u32[]{:S(2)}, u32[]{:S(2)}) %collective-permute-start.11) | collective-permute-done | bytes 1048608 | tf_op jit(solution)/shard_map/core_pair1/ppermute | solution.py:456
  48.2 3.4 %early_edges.2 = (bf16[2,2,256,256]{3,2,1,0:T(8,128)(2,1)}, bf16[2,2,256,256]{3,2,1,0:T(8,128)(2,1)}) custom-call(f32[2,3,4]{2,1,0:T(4,128)} %multiply_reduce_fusion.w_ref, bf16[2,2,2,256,256]{4,3,2,1,0:T(8,128)(2,1)} %get-tuple-element.32.refs_2_.refs_1_.refs_0_, bf16[2,2,2,256,256]{4,3,2,1,0:T(8,128)(2,1)} %gate.20.refs_1_, ...), custom_call_target="tpu_custom_call" | custom-call | flops 390999998464 | tf_op jit(solution)/shard_map/early_edges/pallas_call | solution.py:238
  51.6 0.1 collective-permute-start.12
  51.7 2.9 %collective-permute-done.12.refs_2_.refs_0_ = bf16[2,2,2,256,256]{4,3,2,1,0:T(8,128)(2,1)} collective-permute-done((bf16[2,2,2,256,256]{4,3,2,1,0:T(8,128)(2,1)}, bf16[2,2,2,256,256]{4,3,2,1,0:T(8,128)(2,1)}, u32[]{:S(2)}, u32[]{:S(2)}) %collective-permute-start.12) | collective-permute-done | bytes 1048608 | tf_op jit(solution)/shard_map/core3/ppermute | solution.py:456
  54.6 3.0 %collective-permute-start.21 = (bf16[2,2,256,256]{3,2,1,0:T(8,128)(2,1)}, bf16[2,2,256,256]{3,2,1,0:T(8,128)(2,1)}, u32[]{:S(2)}, u32[]{:S(2)}) collective-permute-start(bf16[2,2,256,256]{3,2,1,0:T(8,128)(2,1)} %get-tuple-element.50.refs_1_), channel_id=1, source_target_pairs={{4,0},{8,4},{12,8},{16,12},{20,16},{24,20},{28,24},{5,1},{9,5},{13... | collective-permute-start | bytes 1572872 | tf_op jit(solution)/shard_map/down1/ppermute | solution.py:456
  57.6 0.0 collective-permute-done.4.refs_0_
  57.6 0.6 collective-permute-done.5.refs_1_
  58.3 0.0 collective-permute-start.14
  58.3 0.5 collective-permute-start.13
  58.8 1.7 %collective-permute-done.14.refs_5_ = bf16[2,2,256,256]{3,2,1,0:T(8,128)(2,1)} collective-permute-done((bf16[2,2,256,256]{3,2,1,0:T(8,128)(2,1)}, bf16[2,2,256,256]{3,2,1,0:T(8,128)(2,1)}, u32[]{:S(2)}, u32[]{:S(2)}) %collective-permute-start.14) | collective-permute-done | bytes 524320 | tf_op jit(solution)/shard_map/core_down2/ppermute | solution.py:456
  60.5 3.0 %collective-permute-start.20 = (bf16[2,2,256,256]{3,2,1,0:T(8,128)(2,1)}, bf16[2,2,256,256]{3,2,1,0:T(8,128)(2,1)}, u32[]{:S(2)}, u32[]{:S(2)}) collective-permute-start(bf16[2,2,256,256]{3,2,1,0:T(8,128)(2,1)} %get-tuple-element.57), channel_id=1, source_target_pairs={{0,4},{4,8},{8,12},{12,16},{16,20},{20,24},{24,28},{1,5},{5,9},{9,... | collective-permute-start | bytes 1572872 | tf_op jit(solution)/shard_map/up1/ppermute | solution.py:456
  63.6 3.6 %late_sum.3.refs_1_ = bf16[2,2,2,256,256]{4,3,2,1,0:T(8,128)(2,1)} custom-call(f32[2,3,4]{2,1,0:T(4,128)} %multiply_reduce_fusion.w_ref, bf16[2,2,2,256,256]{4,3,2,1,0:T(8,128)(2,1)} %get-tuple-element.33.refs_2_.refs_0_, bf16[2,2,2,256,256]{4,3,2,1,0:T(8,128)(2,1)} %gate.25.refs_1_, bf16[2,2,256,256]{3,2,1,0:T(8,128)(2,1)} %get-tuple-element.52.refs_1_.refs_2_, ...), custom_call_target="tpu_custom_call" | custom-call | flops 413999988736 | tf_op jit(solution)/shard_map/late_sum/pallas_call | solution.py:290
  67.2 0.5 collective-permute-start.15
  67.7 0.0 collective-permute-done.16.refs_0_
  67.7 0.0 collective-permute-start.17
  67.7 3.0 %collective-permute-done.17.refs_3_ = bf16[2,2,2,256,256]{4,3,2,1,0:T(8,128)(2,1)} collective-permute-done((bf16[2,2,2,256,256]{4,3,2,1,0:T(8,128)(2,1)}, bf16[2,2,2,256,256]{4,3,2,1,0:T(8,128)(2,1)}, u32[]{:S(2)}, u32[]{:S(2)}) %collective-permute-start.17) | collective-permute-done | bytes 1048608 | tf_op jit(solution)/shard_map/core_pair3/ppermute | solution.py:456
  70.7 3.4 %early_edges.3 = (bf16[2,2,256,256]{3,2,1,0:T(8,128)(2,1)}, bf16[2,2,256,256]{3,2,1,0:T(8,128)(2,1)}) custom-call(f32[2,3,4]{2,1,0:T(4,128)} %multiply_reduce_fusion.w_ref, bf16[2,2,2,256,256]{4,3,2,1,0:T(8,128)(2,1)} %get-tuple-element.37.refs_3_.refs_0_, bf16[2,2,2,256,256]{4,3,2,1,0:T(8,128)(2,1)} %gate.27.refs_1_, ...), custom_call_target="tpu_custom_call" | custom-call | flops 390999998464 | tf_op jit(solution)/shard_map/early_edges/pallas_call | solution.py:238
  74.1 3.7 %collective-permute-start.19 = (bf16[2,2,256,256]{3,2,1,0:T(8,128)(2,1)}, bf16[2,2,256,256]{3,2,1,0:T(8,128)(2,1)}, u32[]{:S(2)}, u32[]{:S(2)}) collective-permute-start(bf16[2,2,256,256]{3,2,1,0:T(8,128)(2,1)} %get-tuple-element.55.refs_4_), channel_id=1, source_target_pairs={{4,0},{8,4},{12,8},{16,12},{20,16},{24,20},{28,24},{5,1},{9,5},{13... | collective-permute-start | bytes 1572872 | tf_op jit(solution)/shard_map/down3/ppermute | solution.py:456
  77.9 2.4 %range_parts.1.refs_7_ = f32[32,1,128]{2,1,0:T(1,128)} custom-call(s32[32]{0:T(128)} %range_ref.1, f32[2,8,256]{2,1,0:T(8,128)} %gate.16.refs_2_.refs_0_, f32[2,8,256]{2,1,0:T(8,128)} %gate.22.refs_1_, f32[2,8,256]{2,1,0:T(8,128)} %gate.23.refs_2_, f32[2,8,256]{2,1,0:T(8,128)} %get-tuple-element.54.refs_3_, bf16[2,2,256,256]{3,2,1,0:T(8,128)(2,1)} %get-tuple-element.55.refs_4_), custom_call_target="tpu_custom_call" | custom-call | flops 253000007680 | tf_op jit(solution)/shard_map/range_parts/pallas_call | solution.py:412
  80.2 5.4 %all-to-all-start = ((f32[32,1,128]{2,1,0:T(1,128)}), f32[32,1,128]{2,1,0:T(1,128)}, u32[]{:S(2)}, u32[]{:S(2)}) async-start(f32[32,1,128]{2,1,0:T(1,128)} %range_parts.1.refs_7_), calls=%async_computation | async-start | bytes 32768 | tf_op jit(solution)/shard_map/all_to_all | solution.py:541
  85.7 1.1 collective-permute-done.22.refs_6_
  86.8 2.3 %collective-permute-start.18 = (bf16[2,2,256,256]{3,2,1,0:T(8,128)(2,1)}, bf16[2,2,256,256]{3,2,1,0:T(8,128)(2,1)}, u32[]{:S(2)}, u32[]{:S(2)}) collective-permute-start(bf16[2,2,256,256]{3,2,1,0:T(8,128)(2,1)} %get-tuple-element.56), channel_id=1, source_target_pairs={{0,4},{4,8},{8,12},{12,16},{16,20},{20,24},{24,28},{1,5},{5,9},{9,... | collective-permute-start | bytes 1572872 | tf_op jit(solution)/shard_map/up3/ppermute | solution.py:456
  89.1 4.3 %finish.4.refs_6_ = bf16[2,2,1,2048,256]{4,3,2,1,0:T(8,128)(2,1)} custom-call(f32[2,3,4]{2,1,0:T(4,128)} %multiply_reduce_fusion.w_ref, f32[8,1,256]{2,1,0:T(1,128)} %bitcast.7, bf16[2,2,2,256,256]{4,3,2,1,0:T(8,128)(2,1)} %get-tuple-element.30.refs_2_.refs_0_, bf16[2,2,2,256,256]{4,3,2,1,0:T(8,128)(2,1)} %gate.18.refs_1_, ...), custom_call_target="tpu_custom_call" | custom-call | flops 506000015360 | tf_op jit(solution)/shard_map/finish/pallas_call | solution.py:372
  93.4 0.0 collective-permute-done.20.refs_4_
  93.4 4.8 %finish.5.refs_6_ = bf16[2,2,1,2048,256]{4,3,2,1,0:T(8,128)(2,1)} custom-call(f32[2,3,4]{2,1,0:T(4,128)} %multiply_reduce_fusion.w_ref, f32[8,1,256]{2,1,0:T(1,128)} %bitcast.8, bf16[2,2,2,256,256]{4,3,2,1,0:T(8,128)(2,1)} %get-tuple-element.32.refs_2_.refs_1_.refs_0_, bf16[2,2,2,256,256]{4,3,2,1,0:T(8,128)(2,1)} %gate.20.refs_1_, ...), custom_call_target="tpu_custom_call", output_to_operand_aliasing={{}: (8, {})} | custom-call | flops 506000015360 | tf_op jit(solution)/shard_map/finish/pallas_call | solution.py:372
  98.1 4.8 %collective-permute-done.18.refs_4_ = bf16[2,2,256,256]{3,2,1,0:T(8,128)(2,1)} collective-permute-done((bf16[2,2,256,256]{3,2,1,0:T(8,128)(2,1)}, bf16[2,2,256,256]{3,2,1,0:T(8,128)(2,1)}, u32[]{:S(2)}, u32[]{:S(2)}) %collective-permute-start.18) | collective-permute-done | bytes 524320 | tf_op jit(solution)/shard_map/up3/ppermute | solution.py:456
  102.9 1.7 %collective-permute-done.19.refs_5_ = bf16[2,2,256,256]{3,2,1,0:T(8,128)(2,1)} collective-permute-done((bf16[2,2,256,256]{3,2,1,0:T(8,128)(2,1)}, bf16[2,2,256,256]{3,2,1,0:T(8,128)(2,1)}, u32[]{:S(2)}, u32[]{:S(2)}) %collective-permute-start.19) | collective-permute-done | bytes 524320 | tf_op jit(solution)/shard_map/down3/ppermute | solution.py:456
  104.6 4.7 %finish.6.refs_8_ = bf16[2,2,1,2048,256]{4,3,2,1,0:T(8,128)(2,1)} custom-call(f32[2,3,4]{2,1,0:T(4,128)} %multiply_reduce_fusion.w_ref, f32[8,1,256]{2,1,0:T(1,128)} %bitcast.9, bf16[2,2,2,256,256]{4,3,2,1,0:T(8,128)(2,1)} %get-tuple-element.37.refs_3_.refs_0_, bf16[2,2,2,256,256]{4,3,2,1,0:T(8,128)(2,1)} %gate.27.refs_1_, ...), custom_call_target="tpu_custom_call", output_to_operand_aliasing={{}: (8, {})} | custom-call | flops 506000015360 | tf_op jit(solution)/shard_map/finish/pallas_call | solution.py:372
  109.4 0.0 all-to-all-done.refs_7_
  109.4 4.7 %finish.7 = (bf16[2,2,1,2048,256]{4,3,2,1,0:T(8,128)(2,1)}, f32[1]{0:T(128)}) custom-call(f32[2,3,4]{2,1,0:T(4,128)} %multiply_reduce_fusion.w_ref, f32[8,1,256]{2,1,0:T(1,128)} %bitcast.10, bf16[2,2,2,256,256]{4,3,2,1,0:T(8,128)(2,1)} %get-tuple-element.33.refs_2_.refs_0_, ...), custom_call_target="tpu_custom_call", output_to_operand_aliasing={{0}: (10, {})} | custom-call | flops 506000015360 | tf_op jit(solution)/shard_map/finish/pallas_call | solution.py:372
  (28 shorter events, 0.0 us)
Async XLA Ops:
  0.6 8.7 %copy-start.2 = (s32[4]{0:T(128)S(1)}, s32[4]{0:T(128)}, u32[]{:S(2)}) copy-start(s32[4]{0:T(128)} %param.10) | copy-start | bytes 52
  0.6 8.7 %copy-start = (f32[4,4,4]{2,1,0:T(4,128)S(1)}, f32[4,4,4]{2,1,0:T(4,128)}, u32[]{:S(2)}) copy-start(f32[4,4,4]{2,1,0:T(4,128)} %param.12) | copy-start | bytes 772
  0.7 8.7 %copy-start.1 = (f32[4,4,4]{2,1,0:T(4,128)S(1)}, f32[4,4,4]{2,1,0:T(4,128)}, u32[]{:S(2)}) copy-start(f32[4,4,4]{2,1,0:T(4,128)} %param.11) | copy-start | bytes 772
  5.5 4.8 %collective-permute-start = (f32[2,8,256]{2,1,0:T(8,128)}, f32[2,8,256]{2,1,0:T(8,128)S(1)}, u32[]{:S(2)}, u32[]{:S(2)}) collective-permute-start(f32[2,8,256]{2,1,0:T(8,128)} %get-tuple-element.31.refs_0_), channel_id=1, source_target_pairs={{0,1},{1,0},{2,3},{3,2},{4,5},{5,4},{6,7},{7,6},{8,9},{9,8},{10,11... | collective-permute-start | bytes 49160 | tf_op jit(solution)/shard_map/beat0/ppermute | solution.py:456
  5.5 27.6 %collective-permute-start.7 = (bf16[2,2,256,256]{3,2,1,0:T(8,128)(2,1)}, bf16[2,2,256,256]{3,2,1,0:T(8,128)(2,1)}, u32[]{:S(2)}, u32[]{:S(2)}) collective-permute-start(bf16[2,2,256,256]{3,2,1,0:T(8,128)(2,1)} %get-tuple-element.43), channel_id=1, source_target_pairs={{0,4},{4,8},{8,12},{12,16},{16,20},{20,24},{24,28},{1,5},{5,9},{9,... | collective-permute-start | bytes 1572872 | tf_op jit(solution)/shard_map/up0/ppermute | solution.py:456
  8.9 11.5 %collective-permute-start.1 = (bf16[2,2,2,256,256]{4,3,2,1,0:T(8,128)(2,1)}, bf16[2,2,2,256,256]{4,3,2,1,0:T(8,128)(2,1)}, u32[]{:S(2)}, u32[]{:S(2)}) collective-permute-start(bf16[2,2,2,256,256]{4,3,2,1,0:T(8,128)(2,1)} %get-tuple-element.30.refs_2_.refs_0_), channel_id=1, source_target_pairs={{0,1},{1,0},{2,3},{3,2},{4,5},{5,4},{6,7},{7,6},{8,9},{9,8},{10,11... | collective-permute-start | bytes 3145736 | tf_op jit(solution)/shard_map/core0/ppermute | solution.py:456
  10.2 0.6 copy-start.3
  15.5 29.7 %collective-permute-start.6 = (bf16[2,2,2,256,256]{4,3,2,1,0:T(8,128)(2,1)}, bf16[2,2,2,256,256]{4,3,2,1,0:T(8,128)(2,1)}, u32[]{:S(2)}, u32[]{:S(2)}) collective-permute-start(bf16[2,2,2,256,256]{4,3,2,1,0:T(8,128)(2,1)} %get-tuple-element.32.refs_2_.refs_1_.refs_0_), channel_id=1, source_target_pairs={{0,2},{1,3},{2,0},{3,1},{4,6},{5,7},{6,4},{7,5},{8,10},{9,11},{10,... | collective-permute-start | bytes 3145736 | tf_op jit(solution)/shard_map/pair1/ppermute | solution.py:456
  17.1 8.5 %collective-permute-start.2 = (bf16[2,2,2,256,256]{4,3,2,1,0:T(8,128)(2,1)}, bf16[2,2,2,256,256]{4,3,2,1,0:T(8,128)(2,1)}, u32[]{:S(2)}, u32[]{:S(2)}) collective-permute-start(bf16[2,2,2,256,256]{4,3,2,1,0:T(8,128)(2,1)} %get-tuple-element.32.refs_2_.refs_1_.refs_0_), channel_id=1, source_target_pairs={{0,1},{1,0},{2,3},{3,2},{4,5},{5,4},{6,7},{7,6},{8,9},{9,8},{10,11... | collective-permute-start | bytes 3145736 | tf_op jit(solution)/shard_map/core1/ppermute | solution.py:456
  17.1 17.1 %collective-permute-start.8 = (bf16[2,2,256,256]{3,2,1,0:T(8,128)(2,1)}, bf16[2,2,256,256]{3,2,1,0:T(8,128)(2,1)}, u32[]{:S(2)}, u32[]{:S(2)}) collective-permute-start(bf16[2,2,256,256]{3,2,1,0:T(8,128)(2,1)} %gate.15), channel_id=1, source_target_pairs={{4,0},{8,4},{12,8},{16,12},{20,16},{24,20},{28,24},{5,1},{9,5},{13... | collective-permute-start | bytes 1572872 | tf_op jit(solution)/shard_map/down0/ppermute | solution.py:456
  30.5 3.6 %collective-permute-start.3 = (bf16[2,2,2,256,256]{4,3,2,1,0:T(8,128)(2,1)}, bf16[2,2,2,256,256]{4,3,2,1,0:T(8,128)(2,1)}, u32[]{:S(2)}, u32[]{:S(2)}) collective-permute-start(bf16[2,2,2,256,256]{4,3,2,1,0:T(8,128)(2,1)} %get-tuple-element.38), channel_id=1, source_target_pairs={{0,1},{1,0},{2,3},{3,2},{4,5},{5,4},{6,7},{7,6},{8,9},{9,8},{10,11... | collective-permute-start | bytes 3145736 | tf_op jit(solution)/shard_map/core2/ppermute | solution.py:456
  30.7 27.6 %collective-permute-start.5 = (bf16[2,2,256,256]{3,2,1,0:T(8,128)(2,1)}, bf16[2,2,256,256]{3,2,1,0:T(8,128)(2,1)}, u32[]{:S(2)}, u32[]{:S(2)}) collective-permute-start(bf16[2,2,256,256]{3,2,1,0:T(8,128)(2,1)} %get-tuple-element.40.refs_1_), channel_id=1, source_target_pairs={{4,0},{8,4},{12,8},{16,12},{20,16},{24,20},{28,24},{5,1},{9,5},{13... | collective-permute-start | bytes 1572872 | tf_op jit(solution)/shard_map/down2/ppermute | solution.py:456
  33.1 34.6 %collective-permute-start.16 = (bf16[2,2,2,256,256]{4,3,2,1,0:T(8,128)(2,1)}, bf16[2,2,2,256,256]{4,3,2,1,0:T(8,128)(2,1)}, u32[]{:S(2)}, u32[]{:S(2)}) collective-permute-start(bf16[2,2,2,256,256]{4,3,2,1,0:T(8,128)(2,1)} %get-tuple-element.37.refs_3_.refs_0_), channel_id=1, source_target_pairs={{0,2},{1,3},{2,0},{3,1},{4,6},{5,7},{6,4},{7,5},{8,10},{9,11},{10,... | collective-permute-start | bytes 3145736 | tf_op jit(solution)/shard_map/pair3/ppermute | solution.py:456
  34.1 2.3 %collective-permute-start.10 = (bf16[2,2,256,256]{3,2,1,0:T(8,128)(2,1)}, bf16[2,2,256,256]{3,2,1,0:T(8,128)(2,1)}, u32[]{:S(2)}, u32[]{:S(2)}) collective-permute-start(bf16[2,2,256,256]{3,2,1,0:T(8,128)(2,1)} %get-tuple-element.46.refs_3_), channel_id=1, source_target_pairs={{0,1},{1,0},{2,3},{3,2},{4,5},{5,4},{6,7},{7,6},{8,9},{9,8},{10,11... | collective-permute-start | bytes 1572872 | tf_op jit(solution)/shard_map/core_down0/ppermute | solution.py:456
  34.2 5.9 %collective-permute-start.9 = (bf16[2,2,256,256]{3,2,1,0:T(8,128)(2,1)}, bf16[2,2,256,256]{3,2,1,0:T(8,128)(2,1)}, u32[]{:S(2)}, u32[]{:S(2)}) collective-permute-start(bf16[2,2,256,256]{3,2,1,0:T(8,128)(2,1)} %get-tuple-element.45.refs_1_.refs_2_), channel_id=1, source_target_pairs={{0,1},{1,0},{2,3},{3,2},{4,5},{5,4},{6,7},{7,6},{8,9},{9,8},{10,11... | collective-permute-start | bytes 1572872 | tf_op jit(solution)/shard_map/core_up0/ppermute | solution.py:456
  36.4 21.2 %collective-permute-start.4 = (bf16[2,2,256,256]{3,2,1,0:T(8,128)(2,1)}, bf16[2,2,256,256]{3,2,1,0:T(8,128)(2,1)}, u32[]{:S(2)}, u32[]{:S(2)}) collective-permute-start(bf16[2,2,256,256]{3,2,1,0:T(8,128)(2,1)} %get-tuple-element.39), channel_id=1, source_target_pairs={{0,4},{4,8},{8,12},{12,16},{16,20},{20,24},{24,28},{1,5},{5,9},{9,... | collective-permute-start | bytes 1572872 | tf_op jit(solution)/shard_map/up2/ppermute | solution.py:456
  43.7 43.1 %collective-permute-start.22 = (bf16[2,2,2,256,256]{4,3,2,1,0:T(8,128)(2,1)}, bf16[2,2,2,256,256]{4,3,2,1,0:T(8,128)(2,1)}, u32[]{:S(2)}, u32[]{:S(2)}) collective-permute-start(bf16[2,2,2,256,256]{4,3,2,1,0:T(8,128)(2,1)} %late_sum.2.refs_1_), channel_id=1, source_target_pairs={{0,2},{1,3},{2,0},{3,1},{4,6},{5,7},{6,4},{7,5},{8,10},{9,11},{10,... | collective-permute-start | bytes 3145736 | tf_op jit(solution)/shard_map/pair0/ppermute | solution.py:456
  45.2 3.0 %collective-permute-start.11 = (bf16[2,2,2,256,256]{4,3,2,1,0:T(8,128)(2,1)}, bf16[2,2,2,256,256]{4,3,2,1,0:T(8,128)(2,1)}, u32[]{:S(2)}, u32[]{:S(2)}) collective-permute-start(bf16[2,2,2,256,256]{4,3,2,1,0:T(8,128)(2,1)} %gate.19.refs_1_.refs_2_), channel_id=1, source_target_pairs={{0,1},{1,0},{2,3},{3,2},{4,5},{5,4},{6,7},{7,6},{8,9},{9,8},{10,11... | collective-permute-start | bytes 3145736 | tf_op jit(solution)/shard_map/core_pair1/ppermute | solution.py:456
  51.6 3.0 %collective-permute-start.12 = (bf16[2,2,2,256,256]{4,3,2,1,0:T(8,128)(2,1)}, bf16[2,2,2,256,256]{4,3,2,1,0:T(8,128)(2,1)}, u32[]{:S(2)}, u32[]{:S(2)}) collective-permute-start(bf16[2,2,2,256,256]{4,3,2,1,0:T(8,128)(2,1)} %get-tuple-element.51), channel_id=1, source_target_pairs={{0,1},{1,0},{2,3},{3,2},{4,5},{5,4},{6,7},{7,6},{8,9},{9,8},{10,11... | collective-permute-start | bytes 3145736 | tf_op jit(solution)/shard_map/core3/ppermute | solution.py:456
  54.6 38.8 %collective-permute-start.21 = (bf16[2,2,256,256]{3,2,1,0:T(8,128)(2,1)}, bf16[2,2,256,256]{3,2,1,0:T(8,128)(2,1)}, u32[]{:S(2)}, u32[]{:S(2)}) collective-permute-start(bf16[2,2,256,256]{3,2,1,0:T(8,128)(2,1)} %get-tuple-element.50.refs_1_), channel_id=1, source_target_pairs={{4,0},{8,4},{12,8},{16,12},{20,16},{24,20},{28,24},{5,1},{9,5},{13... | collective-permute-start | bytes 1572872 | tf_op jit(solution)/shard_map/down1/ppermute | solution.py:456
  58.3 2.3 %collective-permute-start.14 = (bf16[2,2,256,256]{3,2,1,0:T(8,128)(2,1)}, bf16[2,2,256,256]{3,2,1,0:T(8,128)(2,1)}, u32[]{:S(2)}, u32[]{:S(2)}) collective-permute-start(bf16[2,2,256,256]{3,2,1,0:T(8,128)(2,1)} %get-tuple-element.53.refs_3_), channel_id=1, source_target_pairs={{0,1},{1,0},{2,3},{3,2},{4,5},{5,4},{6,7},{7,6},{8,9},{9,8},{10,11... | collective-permute-start | bytes 1572872 | tf_op jit(solution)/shard_map/core_down2/ppermute | solution.py:456
  58.3 5.3 %collective-permute-start.13 = (bf16[2,2,256,256]{3,2,1,0:T(8,128)(2,1)}, bf16[2,2,256,256]{3,2,1,0:T(8,128)(2,1)}, u32[]{:S(2)}, u32[]{:S(2)}) collective-permute-start(bf16[2,2,256,256]{3,2,1,0:T(8,128)(2,1)} %get-tuple-element.52.refs_1_.refs_2_), channel_id=1, source_target_pairs={{0,1},{1,0},{2,3},{3,2},{4,5},{5,4},{6,7},{7,6},{8,9},{9,8},{10,11... | collective-permute-start | bytes 1572872 | tf_op jit(solution)/shard_map/core_up2/ppermute | solution.py:456
  60.5 32.8 %collective-permute-start.20 = (bf16[2,2,256,256]{3,2,1,0:T(8,128)(2,1)}, bf16[2,2,256,256]{3,2,1,0:T(8,128)(2,1)}, u32[]{:S(2)}, u32[]{:S(2)}) collective-permute-start(bf16[2,2,256,256]{3,2,1,0:T(8,128)(2,1)} %get-tuple-element.57), channel_id=1, source_target_pairs={{0,4},{4,8},{8,12},{12,16},{16,20},{20,24},{24,28},{1,5},{5,9},{9,... | collective-permute-start | bytes 1572872 | tf_op jit(solution)/shard_map/up1/ppermute | solution.py:456
  67.2 42.2 %collective-permute-start.15 = (bf16[2,2,2,256,256]{4,3,2,1,0:T(8,128)(2,1)}, bf16[2,2,2,256,256]{4,3,2,1,0:T(8,128)(2,1)}, u32[]{:S(2)}, u32[]{:S(2)}) collective-permute-start(bf16[2,2,2,256,256]{4,3,2,1,0:T(8,128)(2,1)} %late_sum.3.refs_1_), channel_id=1, source_target_pairs={{0,2},{1,3},{2,0},{3,1},{4,6},{5,7},{6,4},{7,5},{8,10},{9,11},{10,... | collective-permute-start | bytes 3145736 | tf_op jit(solution)/shard_map/pair2/ppermute | solution.py:456
  67.7 3.0 %collective-permute-start.17 = (bf16[2,2,2,256,256]{4,3,2,1,0:T(8,128)(2,1)}, bf16[2,2,2,256,256]{4,3,2,1,0:T(8,128)(2,1)}, u32[]{:S(2)}, u32[]{:S(2)}) collective-permute-start(bf16[2,2,2,256,256]{4,3,2,1,0:T(8,128)(2,1)} %gate.26.refs_1_.refs_2_), channel_id=1, source_target_pairs={{0,1},{1,0},{2,3},{3,2},{4,5},{5,4},{6,7},{7,6},{8,9},{9,8},{10,11... | collective-permute-start | bytes 3145736 | tf_op jit(solution)/shard_map/core_pair3/ppermute | solution.py:456
  74.1 30.5 %collective-permute-start.19 = (bf16[2,2,256,256]{3,2,1,0:T(8,128)(2,1)}, bf16[2,2,256,256]{3,2,1,0:T(8,128)(2,1)}, u32[]{:S(2)}, u32[]{:S(2)}) collective-permute-start(bf16[2,2,256,256]{3,2,1,0:T(8,128)(2,1)} %get-tuple-element.55.refs_4_), channel_id=1, source_target_pairs={{4,0},{8,4},{12,8},{16,12},{20,16},{24,20},{28,24},{5,1},{9,5},{13... | collective-permute-start | bytes 1572872 | tf_op jit(solution)/shard_map/down3/ppermute | solution.py:456
  80.2 29.1 %all-to-all-start = ((f32[32,1,128]{2,1,0:T(1,128)}), f32[32,1,128]{2,1,0:T(1,128)}, u32[]{:S(2)}, u32[]{:S(2)}) async-start(f32[32,1,128]{2,1,0:T(1,128)} %range_parts.1.refs_7_), calls=%async_computation | async-start | bytes 32768 | tf_op jit(solution)/shard_map/all_to_all | solution.py:541
  86.8 16.1 %collective-permute-start.18 = (bf16[2,2,256,256]{3,2,1,0:T(8,128)(2,1)}, bf16[2,2,256,256]{3,2,1,0:T(8,128)(2,1)}, u32[]{:S(2)}, u32[]{:S(2)}) collective-permute-start(bf16[2,2,256,256]{3,2,1,0:T(8,128)(2,1)} %get-tuple-element.56), channel_id=1, source_target_pairs={{0,4},{4,8},{8,12},{12,16},{16,20},{20,24},{24,28},{1,5},{5,9},{9,... | collective-permute-start | bytes 1572872 | tf_op jit(solution)/shard_map/up3/ppermute | solution.py:456

commit v3 on v2

--- a/solution.py
+++ b/solution.py
@@ -7,12 +7,11 @@
 from jax.experimental.pallas import tpu as pltpu
 from jax.sharding import PartitionSpec as P
 
-CHUNKS = (("late", 0, 2), ("early", 2, 2), ("late", 4, 2), ("early", 6, 2))
+CHUNKS = (("late", 0, 2), ("early", 2, 2), ("late", 6, 2), ("early", 4, 2))
 VMEM = 63 * 2**20
 TILE = 16
 UNROLL = 4
 ANY = pl.BlockSpec(memory_space=pltpu.HBM)
-LOOSE = pl.BlockSpec(memory_space=pl.ANY)
 FACTOR = 100.0
 
 
@@ -27,7 +26,7 @@
 
 
 def unread(values):
-    return [ANY if value.size > 2**16 else LOOSE for value in values]
+    return [ANY] * len(values)
 
 
 def dot(left, right, transpose=False):
@@ -158,23 +157,12 @@
     )(*args)
 
 
-def grid_spec(energies, width, base=0):
-    return pl.BlockSpec((1, 2, energies, width, width), lambda i: (base + i, 0, 0, 0, 0))
-
-
-def edge_spec(width, base=0):
-    return pl.BlockSpec((1, 2, width, width), lambda i: (base + i, 0, 0, 0))
-
-
-def early_members(blocks, base=0):
-    count, _, energies, width, _ = blocks[0].shape
-    return list(blocks), [grid_spec(energies, width, base)] * 4
-
-
-def late_members(blocks, base=0):
-    count, _, energies, width, _ = blocks[0].shape
-    specs = [grid_spec(energies, width, base)] * 2 + [edge_spec(width, base)] * 4
-    return list(blocks), specs
+def grid_spec(energies, width):
+    return pl.BlockSpec((1, 2, energies, width, width), lambda i: (i, 0, 0, 0, 0))
+
+
+def edge_spec(width):
+    return pl.BlockSpec((1, 2, width, width), lambda i: (i, 0, 0, 0))
 
 
 def gate_kernel(*refs):
@@ -217,34 +205,43 @@
 
 
 def early_edges_kernel(w_ref, *refs):
-    grids, (high_ref, low_ref) = refs[:4], refs[-2:]
-    last = grids[0].shape[2] - 1
-    width = grids[0].shape[-1]
-    above = [w_ref[0, 0, j] for j in range(4)]
-    below = [w_ref[0, 2, j] for j in range(4)]
+    grids, (high_ref, low_ref, local_ref) = refs[:4], refs[-3:]
+    energies, width = grids[0].shape[2:4]
+    w = [[w_ref[0, o, j] for j in range(4)] for o in range(3)]
 
     @tiles(width)
     def _(part, rows):
-        high = [(above[j], grids[j][0, part, last, rows, :].astype(F32)) for j in range(4)]
-        low = [(below[j], grids[j][0, part, 0, rows, :].astype(F32)) for j in range(4)]
+        line = [
+            [ref[0, part, e, rows, :].astype(F32) for e in range(energies)] for ref in grids
+        ]
+        high = [(w[0][j], line[j][energies - 1]) for j in range(4)]
+        low = [(w[2][j], line[j][0]) for j in range(4)]
         high_ref[0, part, rows, :] = weighted(high).astype(BF16)
         low_ref[0, part, rows, :] = weighted(low).astype(BF16)
+        for e in range(energies):
+            terms = [
+                (w[o][j], line[j][e + o - 1])
+                for j in range(4)
+                for o in range(3)
+                if 0 <= e + o - 1 < energies
+            ]
+            local_ref[0, part, e, rows, :] = weighted(terms).astype(BF16)
 
 
 def early_edges(weights, members, after):
-    args, specs = early_members(members)
-    count, _, energies, width, _ = args[0].shape
+    count, _, energies, width, _ = members[0].shape
     edge = jax.ShapeDtypeStruct((count, 2, width, width), BF16)
+    spec = grid_spec(energies, width)
     return pl.pallas_call(
         early_edges_kernel,
         grid=(count,),
-        in_specs=[pl.BlockSpec(memory_space=pltpu.SMEM)] + specs + unread(after),
-        out_specs=[edge_spec(width)] * 2,
-        out_shape=[edge, edge],
+        in_specs=[pl.BlockSpec(memory_space=pltpu.SMEM)] + [spec] * 4 + unread(after),
+        out_specs=[edge_spec(width)] * 2 + [spec],
+        out_shape=[edge, edge, jax.ShapeDtypeStruct(members[0].shape, BF16)],
         compiler_params=pltpu.CompilerParams(vmem_limit_bytes=VMEM),
         cost_estimate=cost(1.7 * count),
         name="early_edges",
-    )(weights, *args, *after)
+    )(weights, *members, *after)
 
 
 def late_line(refs, part, rows):
@@ -258,59 +255,49 @@
     return lines
 
 
-def late_sum_kernel(pieces, w_ref, *refs):
-    members, outs = refs[:6], refs[-pieces:]
+def late_sum_kernel(w_ref, *refs):
+    members, outs = refs[:6], refs[-2:]
     energies, width = members[0].shape[2:4]
-    w = [[w_ref[1, o, j] for j in range(2)] for o in range(3)]
-
-    def fill(out_ref):
-        @tiles(width)
-        def _(part, rows):
-            line = late_line(members, part, rows)
+    w = [[[w_ref[t, o, j] for j in range(2)] for o in range(3)] for t in range(2)]
+
+    @tiles(width)
+    def _(part, rows):
+        line = late_line(members, part, rows)
+        for target, out_ref in zip((1, 0), outs):
             for e in range(energies):
-                terms = [(w[o][j], line[j][e + o]) for j in range(2) for o in range(3)]
+                terms = [(w[target][o][j], line[j][e + o]) for j in range(2) for o in range(3)]
                 out_ref[0, part, e, rows, :] = weighted(terms).astype(BF16)
 
-    if pieces == 1:
-        fill(outs[0])
-    else:
-        for index in range(pieces):
-            pl.when(pl.program_id(0) == index)(functools.partial(fill, outs[index]))
-
-
-def late_sum(weights, members, after, apart=False):
-    args, specs = late_members(members)
-    count, _, energies, width, _ = args[0].shape
-    shape = jax.ShapeDtypeStruct(args[0].shape, BF16)
-    out_shape, out_specs = [shape], [grid_spec(energies, width)]
-    if apart:
-        one = pl.BlockSpec((1, 2, energies, width, width), lambda i: (0, 0, 0, 0, 0))
-        out_shape = [jax.ShapeDtypeStruct((1,) + args[0].shape[1:], BF16)] * count
-        out_specs = [one] * count
-    return pl.pallas_call(
-        functools.partial(late_sum_kernel, len(out_shape)),
+
+def late_sum(weights, members, after):
+    count, _, energies, width, _ = members[0].shape
+    spec = grid_spec(energies, width)
+    return pl.pallas_call(
+        late_sum_kernel,
         grid=(count,),
-        in_specs=[pl.BlockSpec(memory_space=pltpu.SMEM)] + specs + unread(after),
-        out_specs=out_specs,
-        out_shape=out_shape,
+        in_specs=[pl.BlockSpec(memory_space=pltpu.SMEM)]
+        + [spec] * 2
+        + [edge_spec(width)] * 4
+        + unread(after),
+        out_specs=[spec, spec],
+        out_shape=[jax.ShapeDtypeStruct(members[0].shape, BF16)] * 2,
         compiler_params=pltpu.CompilerParams(vmem_limit_bytes=VMEM),
         cost_estimate=cost(1.8 * count),
         name="late_sum",
-    )(weights, *args, *after)
-
-
-def finish_kernel(late, charged, w_ref, across_ref, *refs):
-    members, received = refs[: 6 if late else 4], refs[6:7] if late else refs[4:6]
+    )(weights, *members, *after)
+
+
+def finish_kernel(late, charged, across_ref, local_ref, *refs):
+    received = refs[:1] if late else refs[:2]
     out_ref, down_ref = refs[-3 if charged else -2], refs[-1]
     if charged:
-        parts_ref, charge_ref = refs[7 if late else 6], refs[-2]
+        parts_ref, charge_ref = refs[len(received)], refs[-2]
 
         @pl.when(pl.program_id(0) == 0)
         def _():
             charge_ref[0] = jnp.sum(parts_ref[...])
 
-    energies, width = members[0].shape[2:4]
-    w = [[w_ref[0, o, j] for j in range(4)] for o in range(3)]
+    energies, width = local_ref.shape[2:4]
     across = across_ref[0]
     lanes = down_ref.shape[1]
     down_ref[...] = jnp.transpose(jnp.broadcast_to(across, (lanes, width)))
@@ -318,44 +305,28 @@
     @tiles(width)
     def _(part, rows):
         scale = jnp.concatenate([down_ref[rows, :]] * (width // lanes), axis=1) * across
-        if late:
-            line = late_line(members, part, rows)
-        else:
-            line = [
-                [None] + [ref[0, part, e, rows, :].astype(F32) for e in range(energies)] + [None]
-                for ref in members
-            ]
         for e in range(energies):
-            terms = [
-                (w[o][j], line[j][e + o])
-                for j in range(len(line))
-                for o in range(3)
-                if line[j][e + o] is not None
-            ]
+            total = local_ref[0, part, e, rows, :].astype(F32)
             if late:
-                terms.append((None, received[0][0, part, e, rows, :].astype(F32)))
+                total = total + received[0][0, part, e, rows, :].astype(F32)
             if not late and e == 0:
-                terms.append((None, received[0][0, part, rows, :].astype(F32)))
+                total = total + received[0][0, part, rows, :].astype(F32)
             if not late and e == energies - 1:
-                terms.append((None, received[1][0, part, rows, :].astype(F32)))
-            out_ref[part, e, 0, rows, :] = (weighted(terms) * scale).astype(BF16)
-
-
-def finish(sigma, shape, start, weights, across, late, members, received, after, base, parts):
-    args, specs = late_members(members, base) if late else early_members(members, base)
-    _, _, energies, width, _ = args[0].shape
-    count = received[0].shape[0]
-    args = [weights, across, *args, *received]
+                total = total + received[1][0, part, rows, :].astype(F32)
+            out_ref[part, e, 0, rows, :] = (total * scale).astype(BF16)
+
+
+def finish(sigma, shape, start, across, late, local, received, after, parts):
+    count, _, energies, width, _ = local.shape
+    args = [across, local, *received]
     in_specs = [
-        pl.BlockSpec(memory_space=pltpu.SMEM),
-        pl.BlockSpec((1, 1, width), lambda i: (start + base + i, 0, 0)),
-    ] + specs
+        pl.BlockSpec((1, 1, width), lambda i: (start + i, 0, 0)),
+        grid_spec(energies, width),
+    ]
     in_specs += [grid_spec(energies, width)] if late else [edge_spec(width)] * 2
     out_shape = [jax.ShapeDtypeStruct(shape, BF16)]
     out_specs = [
-        pl.BlockSpec(
-            (2, energies, 1, width, width), lambda i: (0, 0, 0, start + base + i, 0)
-        )
+        pl.BlockSpec((2, energies, 1, width, width), lambda i: (0, 0, 0, start + i, 0))
     ]
     if parts is not None:
         args.append(parts)
@@ -404,7 +375,7 @@
         out_ref[d] = -jnp.sum(total, axis=0, keepdims=True)
         return end
 
-    lax.fori_loop(0, out_ref.shape[0], one_range, jnp.int32(0))
+    lax.fori_loop(0, out_ref.shape[0], one_range, jnp.int32(0), unroll=4)
 
 
 def range_parts(range_rows, densities, after):
@@ -422,19 +393,33 @@
     )(range_rows, *densities, *after)
 
 
-def own_weights(shifts, emission, absorption):
+def own_weights_kernel(shift_ref, emission_ref, absorption_ref, *refs):
+    out_ref = refs[-1]
     me = lax.axis_index("mom")
-    folded = []
-    for offset in (-1, 0, 1):
-        lower = (shifts == -offset).astype(F32)[:, None, None]
-        upper = (shifts == offset).astype(F32)[:, None, None]
-        folded.append(jnp.sum(lower * emission + upper * absorption, axis=0))
-    folded = jnp.stack(folded)
-    momenta = jnp.arange(4, dtype=jnp.int32)
-    targets = ((me ^ jnp.array([0, 2], jnp.int32))[:, None] == momenta[None]).astype(F32)
-    sources = ((me ^ momenta)[:, None] == momenta[None]).astype(F32)
-    picked = folded[None, :, None] * targets[:, None, None, :, None] * sources[None, None, :, None, :]
-    return jnp.sum(picked, axis=(3, 4))
+    zero = jnp.float32(0)
+    for target in range(2):
+        for offset in (-1, 0, 1):
+            for j in range(4):
+                total = zero
+                for p in range(shift_ref.shape[0]):
+                    emitted = emission_ref[p, me ^ (2 * target), me ^ j]
+                    absorbed = absorption_ref[p, me ^ (2 * target), me ^ j]
+                    total = total + jnp.where(shift_ref[p] == -offset, emitted, zero)
+                    total = total + jnp.where(shift_ref[p] == offset, absorbed, zero)
+                out_ref[target, offset + 1, j] = total
+
+
+def own_weights(shifts, emission, absorption, after):
+    smem = pl.BlockSpec(memory_space=pltpu.SMEM)
+    return pl.pallas_call(
+        own_weights_kernel,
+        in_specs=[smem] * 3 + unread(after),
+        out_specs=smem,
+        out_shape=jax.ShapeDtypeStruct((2, 3, 4), F32),
+        compiler_params=pltpu.CompilerParams(vmem_limit_bytes=VMEM),
+        cost_estimate=cost(0.5),
+        name="own_weights",
+    )(shifts, emission, absorption, *after)
 
 
 def body(
@@ -461,7 +446,6 @@
     def pair(value, name):
         return send(value, "mom", [(i, i ^ 2) for i in range(4)], name)
 
-    weights = own_weights(shifts, emission_weight, absorption_weight)
     across_scale = deform_potential.reshape(-1, 1, width)
 
     def run(chunk, previous, after=(), again=False):
@@ -476,33 +460,32 @@
     def fall(value, name):
         return send(value, "energy", down, "down" + name)
 
-    def done(sigma, chunk, members, got, after=(), base=0, parts=None):
+    def done(sigma, chunk, local, got, after=(), parts=None):
         kind, start, _ = CHUNKS[chunk]
         return finish(
             sigma,
             inverse_blocks.shape,
             start,
-            weights,
             across_scale,
             kind == "late",
-            members,
+            local,
             got,
             after,
-            base,
             parts,
         )
 
     g0, n0, low0, high0 = run(0, None)
-    up0, c0, beat0 = rise(high0, "0"), core(g0, "core0"), core(n0, "beat0")
-    g1, n1 = run(1, g0, (beat0,))
+    up0, c0 = rise(high0, "0"), core(g0, "core0")
+    g1, n1 = run(1, g0, (c0,))
     y1, c1 = pair(g1, "pair1"), core(g1, "core1")
     (low0,) = gate([low0], (g1,))
     down0 = fall(low0, "0")
-    g2, n2, low2, high2, h2 = run(2, g1, (c0,), True)
-    g3, n3, h3 = run(3, g2, (c1,), True)
+    g3, n3, h3 = run(3, g1, (c1,), True)
     y3 = pair(g3, "pair3")
-
-    low2, high2, h2 = gate([low2, high2, h2], (g3,))
+    g2, n2, low2, high2, h2 = run(2, g3, (), True)
+    weights = own_weights(shifts, emission_weight, absorption_weight, (n2,))
+
+    low2, high2, h2 = gate([low2, high2, h2], (weights,))
     up2, down2, c2 = rise(high2, "2"), fall(low2, "2"), core(h2, "core2")
     (n0,) = gate([n0], (low2,))
 
@@ -510,39 +493,38 @@
     core_up0, core_down0 = core(up0, "core_up0"), core(down0, "core_down0")
     (c0,) = gate([c0], (up0,))
     members0 = (g0, c0, up0, down0, core_up0, core_down0)
-    (total0,) = late_sum(weights, members0, ())
+    total0, local0 = late_sum(weights, members0, ())
     x0 = pair(total0, "pair0")
-
-    (y1,) = gate([y1], (total0,))
-    core_y1 = core(y1, "core_pair1")
+    y1, h3 = gate([y1, h3], (total0,))
+    core_y1, c3 = core(y1, "core_pair1"), core(h3, "core3")
     (c1,) = gate([c1], (y1,))
+
     members1 = (g1, c1, y1, core_y1)
-    high1, low1 = early_edges(weights, members1, ())
-    high1, low1, h3 = gate([high1, low1, h3], ())
-    up1, down1, c3 = rise(high1, "1"), fall(low1, "1"), core(h3, "core3")
-    (n1,) = gate([n1], (low1,))
-    (n2,) = gate([n2], (n1, c3))
-
-    up2, down2 = gate([up2, down2], (n2,))
+    high1, low1, local1 = early_edges(weights, members1, (c3,))
+    high1, low1, n1 = gate([high1, low1, n1], ())
+    up1, down1, beat1 = rise(high1, "1"), fall(low1, "1"), core(n1, "beat1")
+    (n2,) = gate([n2], (n1,))
+    (n3,) = gate([n3], (n2, beat1))
+
+    up2, down2 = gate([up2, down2], (n3,))
     core_up2, core_down2 = core(up2, "core_up2"), core(down2, "core_down2")
     (c2,) = gate([c2], (up2,))
+    (y3,) = gate([y3], (c2, core_up2, core_down2))
+    core_y3 = core(y3, "core_pair3")
     members2 = (g2, c2, up2, down2, core_up2, core_down2)
-    (total2,) = late_sum(weights, members2, ())
+    total2, local2 = late_sum(weights, members2, (y3,))
     x2 = pair(total2, "pair2")
 
-    (y3,) = gate([y3], (total2,))
-    core_y3 = core(y3, "core_pair3")
-    (c3,) = gate([c3], (y3,))
     members3 = (g3, c3, y3, core_y3)
-    high3, low3 = early_edges(weights, members3, ())
+    high3, low3, local3 = early_edges(weights, members3, (total2,))
     up3, down3 = rise(high3, "3"), fall(low3, "3")
 
-    parts = range_parts(range_rows, [n0, n1, n2, n3], (low3,))
+    parts = range_parts(range_rows, [n0, n1, n3, n2], (low3,))
     received = lax.all_to_all(parts, ("energy", "mom"), split_axis=0, concat_axis=0, tiled=True)
-    (sigma,) = done(None, 0, members0, (x0,), (parts,))
-    (sigma,) = done(sigma, 1, members1, (up1, down1))
-    (sigma,) = done(sigma, 3, members3, (up3, down3))
-    sigma, charge = done(sigma, 2, members2, (x2,), (), 0, received)
+    (sigma,) = done(None, 0, local0, (x0,), (parts,))
+    (sigma,) = done(sigma, 1, local1, (up1, down1))
+    (sigma,) = done(sigma, 3, local3, (up3, down3))
+    sigma, charge = done(sigma, 2, local2, (x2,), (), received)
     return sigma, charge
 
 

time: 116 us -> 113 us (0.974)
  Pallas kernels: 54.4 us -> 52.4 us
    pallas_call x4, Pallas kernels: 18.4 us -> 10.9 us  [finish(): pl.pallas_call(functools.partial(finish_kernel, late, parts is not None),...]
    pallas_call x2 -> x3, Pallas kernels: 7.15 us -> 10.9 us  [the longest x2 9.21 us: late_sum(): pl.pallas_call(late_sum_kernel, grid=(count,), in_specs=[pl.BlockSpec(mem...]
    pallas_call x2, Pallas kernels: 6.84 us -> 8.98 us  [early_edges(): pl.pallas_call(early_edges_kernel, grid=(count,), in_specs=[pl.BlockSpec(...]
  transfers between devices with their start and end apart: 24 -> 24, of which waited for: 10 -> 8; matrix products, arithmetic and copies ran while one was open for 1% -> 0% of each run, Pallas kernels for 39% -> 40%
where the time goes in v3:
time: 113 us; the launch traced here: 112 us
  Pallas kernels  52.4 us (46%)
  starting transfers between devices  36.8 us (33%)
  waiting for transfers between devices  21.6 us (19%)
    ppermute x23, starting transfers between devices, send(): return lax.ppermute(value, axis, pairs)  31 us
    ppermute x23, waiting for transfers between devices, send(): return lax.ppermute(value, axis, pairs)  21.6 us
    pallas_call x4, Pallas kernels, solve(): pl.pallas_call(functools.partial(solve_kernel, first, edges, again), grid...  19.6 us
    pallas_call x4, Pallas kernels, finish(): pl.pallas_call(functools.partial(finish_kernel, late, parts is not None),...  10.9 us
    pallas_call x2, Pallas kernels, late_sum(): pl.pallas_call(late_sum_kernel, grid=(count,), in_specs=[pl.BlockSpec(mem...  9.21 us
    pallas_call x2, Pallas kernels, early_edges(): pl.pallas_call(early_edges_kernel, grid=(count,), in_specs=[pl.BlockSpec(...  8.98 us
    all_to_all x1, starting transfers between devices, body(): lax.all_to_all(parts, ('energy', 'mom'), split_axis=0, concat_axis=0, til...  5.82 us
  transfers between devices with their start and end apart: 24, of which 8 were waited for; matrix products, arithmetic and copies ran while one was open for 0% of the time, Pallas kernels for 40%

profile of v3, /device:TPU:24, one launch (start us, length us, event | category | flops | bytes accessed | tf_op | source)
XLA Modules:
  0.0 111.7 jit_solution(2506973902788023252)
XLA Ops:
  0.6 4.8 %solve.4 = (bf16[2,2,2,256,256]{4,3,2,1,0:T(8,128)(2,1)}, f32[2,8,256]{2,1,0:T(8,128)}, bf16[2,2,256,256]{3,2,1,0:T(8,128)(2,1)}, bf16[2,2,256,256]{3,2,1,0:T(8,128)(2,1)}) custom-call(bf16[2,2,1,2048,256]{4,3,2,1,0:T(8,128)(2,1)} %refs_0_.7, bf16[2,1,2048,256]{3,2,1,0:T(8,128)(2,1)} %refs_1_.7), custom_call_target="tpu_custom_call" | custom-call | flops 575000018944 | tf_op jit(solution)/shard_map/solve/pallas_call | solution.py:147
  5.4 0.0 collective-permute-start
  5.4 3.4 %collective-permute-start.6 = (bf16[2,2,256,256]{3,2,1,0:T(8,128)(2,1)}, bf16[2,2,256,256]{3,2,1,0:T(8,128)(2,1)}, u32[]{:S(2)}, u32[]{:S(2)}) collective-permute-start(bf16[2,2,256,256]{3,2,1,0:T(8,128)(2,1)} %get-tuple-element.51), channel_id=1, source_target_pairs={{0,4},{4,8},{8,12},{12,16},{16,20},{20,24},{24,28},{1,5},{5,9},{9,... | collective-permute-start | bytes 1572872 | tf_op jit(solution)/shard_map/up0/ppermute | solution.py:441
  8.8 0.0 collective-permute-done.refs_3_.refs_0_
  8.8 4.8 %solve.5 = (bf16[2,2,2,256,256]{4,3,2,1,0:T(8,128)(2,1)}, f32[2,8,256]{2,1,0:T(8,128)}) custom-call(bf16[2,2,1,2048,256]{4,3,2,1,0:T(8,128)(2,1)} %refs_0_.7, bf16[2,1,2048,256]{3,2,1,0:T(8,128)(2,1)} %refs_1_.7, bf16[2,2,2,256,256]{4,3,2,1,0:T(8,128)(2,1)} %get-tuple-element.38.refs_2_.refs_0_, bf16[2,2,2,256,256]{4,3,2,1,0:T(8,128)(2,1)} %collective-permute-done.refs_3_.refs_0_), custom_call_target="tpu_custom_call" | custom-call | flops 575000018944 | tf_op jit(solution)/shard_map/solve/pallas_call | solution.py:147
  13.6 0.2 collective-permute-start.1
  13.8 1.5 %collective-permute-start.5 = (bf16[2,2,2,256,256]{4,3,2,1,0:T(8,128)(2,1)}, bf16[2,2,2,256,256]{4,3,2,1,0:T(8,128)(2,1)}, u32[]{:S(2)}, u32[]{:S(2)}) collective-permute-start(bf16[2,2,2,256,256]{4,3,2,1,0:T(8,128)(2,1)} %get-tuple-element.39.refs_2_.refs_1_.refs_0_), channel_id=1, source_target_pairs={{0,2},{1,3},{2,0},{3,1},{4,6},{5,7},{6,4},{7,5},{8,10},{9,11},{10,... | collective-permute-start | bytes 3145736 | tf_op jit(solution)/shard_map/pair1/ppermute | solution.py:441
  15.3 3.3 %collective-permute-start.7 = (bf16[2,2,256,256]{3,2,1,0:T(8,128)(2,1)}, bf16[2,2,256,256]{3,2,1,0:T(8,128)(2,1)}, u32[]{:S(2)}, u32[]{:S(2)}) collective-permute-start(bf16[2,2,256,256]{3,2,1,0:T(8,128)(2,1)} %gate.14), channel_id=1, source_target_pairs={{4,0},{8,4},{12,8},{16,12},{20,16},{24,20},{28,24},{5,1},{9,5},{13... | collective-permute-start | bytes 1572872 | tf_op jit(solution)/shard_map/down0/ppermute | solution.py:441
  18.7 0.0 collective-permute-done.1.refs_3_.refs_0_
  18.7 4.9 %solve.6 = (bf16[2,2,2,256,256]{4,3,2,1,0:T(8,128)(2,1)}, f32[2,8,256]{2,1,0:T(8,128)}, bf16[2,2,2,256,256]{4,3,2,1,0:T(8,128)(2,1)}) custom-call(bf16[2,2,1,2048,256]{4,3,2,1,0:T(8,128)(2,1)} %refs_0_.7, bf16[2,1,2048,256]{3,2,1,0:T(8,128)(2,1)} %refs_1_.7, bf16[2,2,2,256,256]{4,3,2,1,0:T(8,128)(2,1)} %get-tuple-element.39.refs_2_.refs_1_.refs_0_, ...), custom_call_target="tpu_custom_call" | custom-call | flops 575000018944 | tf_op jit(solution)/shard_map/solve/pallas_call | solution.py:147
  23.6 5.1 %solve.7 = (bf16[2,2,2,256,256]{4,3,2,1,0:T(8,128)(2,1)}, f32[2,8,256]{2,1,0:T(8,128)}, bf16[2,2,256,256]{3,2,1,0:T(8,128)(2,1)}, bf16[2,2,256,256]{3,2,1,0:T(8,128)(2,1)}, bf16[2,2,2,256,256]{4,3,2,1,0:T(8,128)(2,1)}) custom-call(bf16[2,2,1,2048,256]{4,3,2,1,0:T(8,128)(2,1)} %refs_0_.7, bf16[2,1,2048,256]{3,2,1,0:T(8,128)(2,1)} %refs_1_.7, ...), custom_call_target="tpu_custom_call" | custom-call | flops 575000018944 | tf_op jit(solution)/shard_map/solve/pallas_call | solution.py:147
  28.7 1.7 %own_weights.1.refs_3_.w_ref = f32[2,3,4]{2,1,0:T(4,128)} custom-call(s32[4]{0:T(128)} %shift_ref.1, f32[4,4,4]{2,1,0:T(4,128)} %emission_ref.1, f32[4,4,4]{2,1,0:T(4,128)} %absorption_ref.1, f32[2,8,256]{2,1,0:T(8,128)} %get-tuple-element.41.refs_0_), custom_call_target="tpu_custom_call" | custom-call | flops 57500000256 | tf_op jit(solution)/shard_map/own_weights/pallas_call | solution.py:414
  30.5 0.1 collective-permute-start.2
  30.6 2.4 %collective-permute-start.4 = (bf16[2,2,256,256]{3,2,1,0:T(8,128)(2,1)}, bf16[2,2,256,256]{3,2,1,0:T(8,128)(2,1)}, u32[]{:S(2)}, u32[]{:S(2)}) collective-permute-start(bf16[2,2,256,256]{3,2,1,0:T(8,128)(2,1)} %get-tuple-element.48.refs_1_), channel_id=1, source_target_pairs={{4,0},{8,4},{12,8},{16,12},{20,16},{24,20},{28,24},{5,1},{9,5},{13... | collective-permute-start | bytes 1572872 | tf_op jit(solution)/shard_map/down2/ppermute | solution.py:441
  33.0 0.0 collective-permute-done.6.refs_0_
  33.0 0.6 collective-permute-start.15
  33.6 0.5 collective-permute-done.7.refs_1_
  34.1 0.0 collective-permute-done.2.refs_3_.refs_0_
  34.1 0.0 collective-permute-start.8
  34.1 0.5 collective-permute-start.9
  34.6 1.7 %collective-permute-done.8.refs_4_ = bf16[2,2,256,256]{3,2,1,0:T(8,128)(2,1)} collective-permute-done((bf16[2,2,256,256]{3,2,1,0:T(8,128)(2,1)}, bf16[2,2,256,256]{3,2,1,0:T(8,128)(2,1)}, u32[]{:S(2)}, u32[]{:S(2)}) %collective-permute-start.8) | collective-permute-done | bytes 524320 | tf_op jit(solution)/shard_map/core_up0/ppermute | solution.py:441
  36.3 3.6 %collective-permute-start.3 = (bf16[2,2,256,256]{3,2,1,0:T(8,128)(2,1)}, bf16[2,2,256,256]{3,2,1,0:T(8,128)(2,1)}, u32[]{:S(2)}, u32[]{:S(2)}) collective-permute-start(bf16[2,2,256,256]{3,2,1,0:T(8,128)(2,1)} %get-tuple-element.47), channel_id=1, source_target_pairs={{0,4},{4,8},{8,12},{12,16},{16,20},{20,24},{24,28},{1,5},{5,9},{9,... | collective-permute-start | bytes 1572872 | tf_op jit(solution)/shard_map/up2/ppermute | solution.py:441
  40.0 0.0 collective-permute-done.9.refs_5_
  40.0 4.6 %late_sum.2 = (bf16[2,2,2,256,256]{4,3,2,1,0:T(8,128)(2,1)}, bf16[2,2,2,256,256]{4,3,2,1,0:T(8,128)(2,1)}) custom-call(f32[2,3,4]{2,1,0:T(4,128)} %own_weights.1.refs_3_.w_ref, bf16[2,2,2,256,256]{4,3,2,1,0:T(8,128)(2,1)} %get-tuple-element.38.refs_2_.refs_0_, bf16[2,2,2,256,256]{4,3,2,1,0:T(8,128)(2,1)} %gate.17.refs_1_, ...), custom_call_target="tpu_custom_call" | custom-call | flops 413999988736 | tf_op jit(solution)/shard_map/late_sum/pallas_call | solution.py:275
  44.6 0.0 collective-permute-done.5.refs_0_
  44.6 0.1 collective-permute-start.10
  44.7 0.5 collective-permute-start.11
  45.2 2.5 %collective-permute-done.10.refs_3_ = bf16[2,2,2,256,256]{4,3,2,1,0:T(8,128)(2,1)} collective-permute-done((bf16[2,2,2,256,256]{4,3,2,1,0:T(8,128)(2,1)}, bf16[2,2,2,256,256]{4,3,2,1,0:T(8,128)(2,1)}, u32[]{:S(2)}, u32[]{:S(2)}) %collective-permute-start.10) | collective-permute-done | bytes 1048608 | tf_op jit(solution)/shard_map/core_pair1/ppermute | solution.py:441
  47.7 1.5 %collective-permute-start.22 = (bf16[2,2,2,256,256]{4,3,2,1,0:T(8,128)(2,1)}, bf16[2,2,2,256,256]{4,3,2,1,0:T(8,128)(2,1)}, u32[]{:S(2)}, u32[]{:S(2)}) collective-permute-start(bf16[2,2,2,256,256]{4,3,2,1,0:T(8,128)(2,1)} %get-tuple-element.56.refs_2_), channel_id=1, source_target_pairs={{0,2},{1,3},{2,0},{3,1},{4,6},{5,7},{6,4},{7,5},{8,10},{9,11},{10,... | collective-permute-start | bytes 3145736 | tf_op jit(solution)/shard_map/pair0/ppermute | solution.py:441
  49.2 0.0 collective-permute-done.11.refs_4_.refs_1_
  49.2 4.5 %early_edges.2 = (bf16[2,2,256,256]{3,2,1,0:T(8,128)(2,1)}, bf16[2,2,256,256]{3,2,1,0:T(8,128)(2,1)}, bf16[2,2,2,256,256]{4,3,2,1,0:T(8,128)(2,1)}) custom-call(f32[2,3,4]{2,1,0:T(4,128)} %own_weights.1.refs_3_.w_ref, bf16[2,2,2,256,256]{4,3,2,1,0:T(8,128)(2,1)} %get-tuple-element.39.refs_2_.refs_1_.refs_0_, bf16[2,2,2,256,256]{4,3,2,1,0:T(8,128)(2,1)} %gate.19.refs_1_, ...), custom_call_target="tpu_custom_call" | custom-call | flops 390999998464 | tf_op jit(solution)/shard_map/early_edges/pallas_call | solution.py:235
  53.7 0.1 collective-permute-start.12
  53.8 1.4 %collective-permute-done.12.refs_2_ = f32[2,8,256]{2,1,0:T(8,128)} collective-permute-done((f32[2,8,256]{2,1,0:T(8,128)}, f32[2,8,256]{2,1,0:T(8,128)}, u32[]{:S(2)}, u32[]{:S(2)}) %collective-permute-start.12) | collective-permute-done | bytes 16416 | tf_op jit(solution)/shard_map/beat1/ppermute | solution.py:441
  55.2 1.9 %collective-permute-start.20 = (bf16[2,2,256,256]{3,2,1,0:T(8,128)(2,1)}, bf16[2,2,256,256]{3,2,1,0:T(8,128)(2,1)}, u32[]{:S(2)}, u32[]{:S(2)}) collective-permute-start(bf16[2,2,256,256]{3,2,1,0:T(8,128)(2,1)} %get-tuple-element.71), channel_id=1, source_target_pairs={{0,4},{4,8},{8,12},{12,16},{16,20},{20,24},{24,28},{1,5},{5,9},{9,... | collective-permute-start | bytes 1572872 | tf_op jit(solution)/shard_map/up1/ppermute | solution.py:441
  57.1 0.0 collective-permute-done.3.refs_0_
  57.1 1.2 %collective-permute-done.4.refs_1_ = bf16[2,2,256,256]{3,2,1,0:T(8,128)(2,1)} collective-permute-done((bf16[2,2,256,256]{3,2,1,0:T(8,128)(2,1)}, bf16[2,2,256,256]{3,2,1,0:T(8,128)(2,1)}, u32[]{:S(2)}, u32[]{:S(2)}) %collective-permute-start.4) | collective-permute-done | bytes 524320 | tf_op jit(solution)/shard_map/down2/ppermute | solution.py:441
  58.3 0.0 collective-permute-start.13
  58.3 0.5 collective-permute-start.14
  58.8 3.7 %collective-permute-done.15.refs_0_ = bf16[2,2,2,256,256]{4,3,2,1,0:T(8,128)(2,1)} collective-permute-done((bf16[2,2,2,256,256]{4,3,2,1,0:T(8,128)(2,1)}, bf16[2,2,2,256,256]{4,3,2,1,0:T(8,128)(2,1)}, u32[]{:S(2)}, u32[]{:S(2)}) %collective-permute-start.15) | collective-permute-done | bytes 1048608 | tf_op jit(solution)/shard_map/pair3/ppermute | solution.py:441
  62.6 3.3 %collective-permute-start.21 = (bf16[2,2,256,256]{3,2,1,0:T(8,128)(2,1)}, bf16[2,2,256,256]{3,2,1,0:T(8,128)(2,1)}, u32[]{:S(2)}, u32[]{:S(2)}) collective-permute-start(bf16[2,2,256,256]{3,2,1,0:T(8,128)(2,1)} %get-tuple-element.72), channel_id=1, source_target_pairs={{4,0},{8,4},{12,8},{16,12},{20,16},{24,20},{28,24},{5,1},{9,5},{13... | collective-permute-start | bytes 1572872 | tf_op jit(solution)/shard_map/down1/ppermute | solution.py:441
  65.9 0.0 collective-permute-done.13.refs_2_.refs_4_
  65.9 0.0 collective-permute-done.14.refs_3_.refs_5_
  66.0 0.1 collective-permute-start.17
  66.0 4.6 %late_sum.3 = (bf16[2,2,2,256,256]{4,3,2,1,0:T(8,128)(2,1)}, bf16[2,2,2,256,256]{4,3,2,1,0:T(8,128)(2,1)}) custom-call(f32[2,3,4]{2,1,0:T(4,128)} %own_weights.1.refs_3_.w_ref, bf16[2,2,2,256,256]{4,3,2,1,0:T(8,128)(2,1)} %get-tuple-element.42.refs_0_, bf16[2,2,2,256,256]{4,3,2,1,0:T(8,128)(2,1)} %gate.24.refs_1_, ...), custom_call_target="tpu_custom_call" | custom-call | flops 413999988736 | tf_op jit(solution)/shard_map/late_sum/pallas_call | solution.py:275
  70.7 1.5 %collective-permute-start.16 = (bf16[2,2,2,256,256]{4,3,2,1,0:T(8,128)(2,1)}, bf16[2,2,2,256,256]{4,3,2,1,0:T(8,128)(2,1)}, u32[]{:S(2)}, u32[]{:S(2)}) collective-permute-start(bf16[2,2,2,256,256]{4,3,2,1,0:T(8,128)(2,1)} %get-tuple-element.66.refs_4_), channel_id=1, source_target_pairs={{0,2},{1,3},{2,0},{3,1},{4,6},{5,7},{6,4},{7,5},{8,10},{9,11},{10,... | collective-permute-start | bytes 3145736 | tf_op jit(solution)/shard_map/pair2/ppermute | solution.py:441
  72.2 0.0 collective-permute-done.17.refs_3_
  72.2 4.5 %early_edges.3 = (bf16[2,2,256,256]{3,2,1,0:T(8,128)(2,1)}, bf16[2,2,256,256]{3,2,1,0:T(8,128)(2,1)}, bf16[2,2,2,256,256]{4,3,2,1,0:T(8,128)(2,1)}) custom-call(f32[2,3,4]{2,1,0:T(4,128)} %own_weights.1.refs_3_.w_ref, bf16[2,2,2,256,256]{4,3,2,1,0:T(8,128)(2,1)} %get-tuple-element.40.refs_2_.refs_0_, ...), custom_call_target="tpu_custom_call" | custom-call | flops 390999998464 | tf_op jit(solution)/shard_map/early_edges/pallas_call | solution.py:235
  76.7 2.4 %collective-permute-start.19 = (bf16[2,2,256,256]{3,2,1,0:T(8,128)(2,1)}, bf16[2,2,256,256]{3,2,1,0:T(8,128)(2,1)}, u32[]{:S(2)}, u32[]{:S(2)}) collective-permute-start(bf16[2,2,256,256]{3,2,1,0:T(8,128)(2,1)} %get-tuple-element.67.refs_4_), channel_id=1, source_target_pairs={{4,0},{8,4},{12,8},{16,12},{20,16},{24,20},{28,24},{5,1},{9,5},{13... | collective-permute-start | bytes 1572872 | tf_op jit(solution)/shard_map/down3/ppermute | solution.py:441
  79.1 1.9 %range_parts.1.refs_1_ = f32[32,1,128]{2,1,0:T(1,128)} custom-call(s32[32]{0:T(128)} %range_ref.1, f32[2,8,256]{2,1,0:T(8,128)} %gate.15.refs_2_.refs_0_, f32[2,8,256]{2,1,0:T(8,128)} %get-tuple-element.62.refs_1_, f32[2,8,256]{2,1,0:T(8,128)} %gate.22.refs_2_, f32[2,8,256]{2,1,0:T(8,128)} %gate.21.refs_1_.refs_3_, ...), custom_call_target="tpu_custom_call" | custom-call | flops 253000007680 | tf_op jit(solution)/shard_map/range_parts/pallas_call | solution.py:383
  81.0 5.8 %all-to-all-start = ((f32[32,1,128]{2,1,0:T(1,128)}), f32[32,1,128]{2,1,0:T(1,128)}, u32[]{:S(2)}, u32[]{:S(2)}) async-start(f32[32,1,128]{2,1,0:T(1,128)} %range_parts.1.refs_1_), calls=%async_computation | async-start | bytes 32768 | tf_op jit(solution)/shard_map/all_to_all | solution.py:523
  86.8 0.0 collective-permute-done.22.refs_0_
  86.9 3.4 %collective-permute-start.18 = (bf16[2,2,256,256]{3,2,1,0:T(8,128)(2,1)}, bf16[2,2,256,256]{3,2,1,0:T(8,128)(2,1)}, u32[]{:S(2)}, u32[]{:S(2)}) collective-permute-start(bf16[2,2,256,256]{3,2,1,0:T(8,128)(2,1)} %get-tuple-element.69), channel_id=1, source_target_pairs={{0,4},{4,8},{8,12},{12,16},{16,20},{20,24},{24,28},{1,5},{5,9},{9,... | collective-permute-start | bytes 1572872 | tf_op jit(solution)/shard_map/up3/ppermute | solution.py:441
  90.3 2.7 %finish.4.refs_2_ = bf16[2,2,1,2048,256]{4,3,2,1,0:T(8,128)(2,1)} custom-call(f32[8,1,256]{2,1,0:T(1,128)} %bitcast.1, bf16[2,2,2,256,256]{4,3,2,1,0:T(8,128)(2,1)} %get-tuple-element.73.local_ref, bf16[2,2,2,256,256]{4,3,2,1,0:T(8,128)(2,1)} %collective-permute-done.22.refs_0_, f32[32,1,128]{2,1,0:T(1,128)} %range_parts.1.refs_1_), custom_call_target="tpu_custom_call" | custom-call | flops 506000015360 | tf_op jit(solution)/shard_map/finish/pallas_call | solution.py:343
  92.9 0.0 collective-permute-done.20.refs_0_
  92.9 0.0 collective-permute-done.21.refs_1_
  92.9 2.7 %finish.5.refs_2_ = bf16[2,2,1,2048,256]{4,3,2,1,0:T(8,128)(2,1)} custom-call(f32[8,1,256]{2,1,0:T(1,128)} %bitcast.2, bf16[2,2,2,256,256]{4,3,2,1,0:T(8,128)(2,1)} %get-tuple-element.70.local_ref, bf16[2,2,256,256]{3,2,1,0:T(8,128)(2,1)} %collective-permute-done.20.refs_0_, ...), custom_call_target="tpu_custom_call", output_to_operand_aliasing={{}: (4, {})} | custom-call | flops 506000015360 | tf_op jit(solution)/shard_map/finish/pallas_call | solution.py:343
  95.6 8.4 %collective-permute-done.18.refs_0_ = bf16[2,2,256,256]{3,2,1,0:T(8,128)(2,1)} collective-permute-done((bf16[2,2,256,256]{3,2,1,0:T(8,128)(2,1)}, bf16[2,2,256,256]{3,2,1,0:T(8,128)(2,1)}, u32[]{:S(2)}, u32[]{:S(2)}) %collective-permute-start.18) | collective-permute-done | bytes 524320 | tf_op jit(solution)/shard_map/up3/ppermute | solution.py:441
  104.0 2.1 %collective-permute-done.19.refs_1_ = bf16[2,2,256,256]{3,2,1,0:T(8,128)(2,1)} collective-permute-done((bf16[2,2,256,256]{3,2,1,0:T(8,128)(2,1)}, bf16[2,2,256,256]{3,2,1,0:T(8,128)(2,1)}, u32[]{:S(2)}, u32[]{:S(2)}) %collective-permute-start.19) | collective-permute-done | bytes 524320 | tf_op jit(solution)/shard_map/down3/ppermute | solution.py:441
  106.2 2.7 %finish.6.refs_2_ = bf16[2,2,1,2048,256]{4,3,2,1,0:T(8,128)(2,1)} custom-call(f32[8,1,256]{2,1,0:T(1,128)} %bitcast.3, bf16[2,2,2,256,256]{4,3,2,1,0:T(8,128)(2,1)} %get-tuple-element.68.local_ref, bf16[2,2,256,256]{3,2,1,0:T(8,128)(2,1)} %collective-permute-done.18.refs_0_, ...), custom_call_target="tpu_custom_call", output_to_operand_aliasing={{}: (4, {})} | custom-call | flops 506000015360 | tf_op jit(solution)/shard_map/finish/pallas_call | solution.py:343
  108.8 0.0 collective-permute-done.16.refs_0_
  108.8 0.0 all-to-all-done.refs_1_
  108.8 2.8 %finish.7 = (bf16[2,2,1,2048,256]{4,3,2,1,0:T(8,128)(2,1)}, f32[1]{0:T(128)}) custom-call(f32[8,1,256]{2,1,0:T(1,128)} %bitcast.4, bf16[2,2,2,256,256]{4,3,2,1,0:T(8,128)(2,1)} %get-tuple-element.65.local_ref, bf16[2,2,2,256,256]{4,3,2,1,0:T(8,128)(2,1)} %collective-permute-done.16.refs_0_, ...), custom_call_target="tpu_custom_call", output_to_operand_aliasing={{0}: (4, {})} | custom-call | flops 506000015360 | tf_op jit(solution)/shard_map/finish/pallas_call | solution.py:343
  (13 shorter events, 0.0 us)
Async XLA Ops:
  5.4 3.4 %collective-permute-start = (bf16[2,2,2,256,256]{4,3,2,1,0:T(8,128)(2,1)}, bf16[2,2,2,256,256]{4,3,2,1,0:T(8,128)(2,1)}, u32[]{:S(2)}, u32[]{:S(2)}) collective-permute-start(bf16[2,2,2,256,256]{4,3,2,1,0:T(8,128)(2,1)} %get-tuple-element.38.refs_2_.refs_0_), channel_id=1, source_target_pairs={{0,1},{1,0},{2,3},{3,2},{4,5},{5,4},{6,7},{7,6},{8,9},{9,8},{10,11... | collective-permute-start | bytes 3145736 | tf_op jit(solution)/shard_map/core0/ppermute | solution.py:441
  5.4 27.6 %collective-permute-start.6 = (bf16[2,2,256,256]{3,2,1,0:T(8,128)(2,1)}, bf16[2,2,256,256]{3,2,1,0:T(8,128)(2,1)}, u32[]{:S(2)}, u32[]{:S(2)}) collective-permute-start(bf16[2,2,256,256]{3,2,1,0:T(8,128)(2,1)} %get-tuple-element.51), channel_id=1, source_target_pairs={{0,4},{4,8},{8,12},{12,16},{16,20},{20,24},{24,28},{1,5},{5,9},{9,... | collective-permute-start | bytes 1572872 | tf_op jit(solution)/shard_map/up0/ppermute | solution.py:441
  13.6 5.1 %collective-permute-start.1 = (bf16[2,2,2,256,256]{4,3,2,1,0:T(8,128)(2,1)}, bf16[2,2,2,256,256]{4,3,2,1,0:T(8,128)(2,1)}, u32[]{:S(2)}, u32[]{:S(2)}) collective-permute-start(bf16[2,2,2,256,256]{4,3,2,1,0:T(8,128)(2,1)} %get-tuple-element.39.refs_2_.refs_1_.refs_0_), channel_id=1, source_target_pairs={{0,1},{1,0},{2,3},{3,2},{4,5},{5,4},{6,7},{7,6},{8,9},{9,8},{10,11... | collective-permute-start | bytes 3145736 | tf_op jit(solution)/shard_map/core1/ppermute | solution.py:441
  13.8 30.8 %collective-permute-start.5 = (bf16[2,2,2,256,256]{4,3,2,1,0:T(8,128)(2,1)}, bf16[2,2,2,256,256]{4,3,2,1,0:T(8,128)(2,1)}, u32[]{:S(2)}, u32[]{:S(2)}) collective-permute-start(bf16[2,2,2,256,256]{4,3,2,1,0:T(8,128)(2,1)} %get-tuple-element.39.refs_2_.refs_1_.refs_0_), channel_id=1, source_target_pairs={{0,2},{1,3},{2,0},{3,1},{4,6},{5,7},{6,4},{7,5},{8,10},{9,11},{10,... | collective-permute-start | bytes 3145736 | tf_op jit(solution)/shard_map/pair1/ppermute | solution.py:441
  15.3 18.8 %collective-permute-start.7 = (bf16[2,2,256,256]{3,2,1,0:T(8,128)(2,1)}, bf16[2,2,256,256]{3,2,1,0:T(8,128)(2,1)}, u32[]{:S(2)}, u32[]{:S(2)}) collective-permute-start(bf16[2,2,256,256]{3,2,1,0:T(8,128)(2,1)} %gate.14), channel_id=1, source_target_pairs={{4,0},{8,4},{12,8},{16,12},{20,16},{24,20},{28,24},{5,1},{9,5},{13... | collective-permute-start | bytes 1572872 | tf_op jit(solution)/shard_map/down0/ppermute | solution.py:441
  30.5 3.6 %collective-permute-start.2 = (bf16[2,2,2,256,256]{4,3,2,1,0:T(8,128)(2,1)}, bf16[2,2,2,256,256]{4,3,2,1,0:T(8,128)(2,1)}, u32[]{:S(2)}, u32[]{:S(2)}) collective-permute-start(bf16[2,2,2,256,256]{4,3,2,1,0:T(8,128)(2,1)} %get-tuple-element.46), channel_id=1, source_target_pairs={{0,1},{1,0},{2,3},{3,2},{4,5},{5,4},{6,7},{7,6},{8,9},{9,8},{10,11... | collective-permute-start | bytes 3145736 | tf_op jit(solution)/shard_map/core2/ppermute | solution.py:441
  30.6 27.8 %collective-permute-start.4 = (bf16[2,2,256,256]{3,2,1,0:T(8,128)(2,1)}, bf16[2,2,256,256]{3,2,1,0:T(8,128)(2,1)}, u32[]{:S(2)}, u32[]{:S(2)}) collective-permute-start(bf16[2,2,256,256]{3,2,1,0:T(8,128)(2,1)} %get-tuple-element.48.refs_1_), channel_id=1, source_target_pairs={{4,0},{8,4},{12,8},{16,12},{20,16},{24,20},{28,24},{5,1},{9,5},{13... | collective-permute-start | bytes 1572872 | tf_op jit(solution)/shard_map/down2/ppermute | solution.py:441
  33.0 29.6 %collective-permute-start.15 = (bf16[2,2,2,256,256]{4,3,2,1,0:T(8,128)(2,1)}, bf16[2,2,2,256,256]{4,3,2,1,0:T(8,128)(2,1)}, u32[]{:S(2)}, u32[]{:S(2)}) collective-permute-start(bf16[2,2,2,256,256]{4,3,2,1,0:T(8,128)(2,1)} %get-tuple-element.40.refs_2_.refs_0_), channel_id=1, source_target_pairs={{0,2},{1,3},{2,0},{3,1},{4,6},{5,7},{6,4},{7,5},{8,10},{9,11},{10,... | collective-permute-start | bytes 3145736 | tf_op jit(solution)/shard_map/pair3/ppermute | solution.py:441
  34.1 2.3 %collective-permute-start.8 = (bf16[2,2,256,256]{3,2,1,0:T(8,128)(2,1)}, bf16[2,2,256,256]{3,2,1,0:T(8,128)(2,1)}, u32[]{:S(2)}, u32[]{:S(2)}) collective-permute-start(bf16[2,2,256,256]{3,2,1,0:T(8,128)(2,1)} %get-tuple-element.54.refs_1_.refs_2_), channel_id=1, source_target_pairs={{0,1},{1,0},{2,3},{3,2},{4,5},{5,4},{6,7},{7,6},{8,9},{9,8},{10,11... | collective-permute-start | bytes 1572872 | tf_op jit(solution)/shard_map/core_up0/ppermute | solution.py:441
  34.1 5.9 %collective-permute-start.9 = (bf16[2,2,256,256]{3,2,1,0:T(8,128)(2,1)}, bf16[2,2,256,256]{3,2,1,0:T(8,128)(2,1)}, u32[]{:S(2)}, u32[]{:S(2)}) collective-permute-start(bf16[2,2,256,256]{3,2,1,0:T(8,128)(2,1)} %get-tuple-element.55.refs_3_), channel_id=1, source_target_pairs={{0,1},{1,0},{2,3},{3,2},{4,5},{5,4},{6,7},{7,6},{8,9},{9,8},{10,11... | collective-permute-start | bytes 1572872 | tf_op jit(solution)/shard_map/core_down0/ppermute | solution.py:441
  36.3 20.8 %collective-permute-start.3 = (bf16[2,2,256,256]{3,2,1,0:T(8,128)(2,1)}, bf16[2,2,256,256]{3,2,1,0:T(8,128)(2,1)}, u32[]{:S(2)}, u32[]{:S(2)}) collective-permute-start(bf16[2,2,256,256]{3,2,1,0:T(8,128)(2,1)} %get-tuple-element.47), channel_id=1, source_target_pairs={{0,4},{4,8},{8,12},{12,16},{16,20},{20,24},{24,28},{1,5},{5,9},{9,... | collective-permute-start | bytes 1572872 | tf_op jit(solution)/shard_map/up2/ppermute | solution.py:441
  44.6 3.1 %collective-permute-start.10 = (bf16[2,2,2,256,256]{4,3,2,1,0:T(8,128)(2,1)}, bf16[2,2,2,256,256]{4,3,2,1,0:T(8,128)(2,1)}, u32[]{:S(2)}, u32[]{:S(2)}) collective-permute-start(bf16[2,2,2,256,256]{4,3,2,1,0:T(8,128)(2,1)} %get-tuple-element.57.refs_1_.refs_2_), channel_id=1, source_target_pairs={{0,1},{1,0},{2,3},{3,2},{4,5},{5,4},{6,7},{7,6},{8,9},{9,8},{10,11... | collective-permute-start | bytes 3145736 | tf_op jit(solution)/shard_map/core_pair1/ppermute | solution.py:441
  44.7 4.5 %collective-permute-start.11 = (bf16[2,2,2,256,256]{4,3,2,1,0:T(8,128)(2,1)}, bf16[2,2,2,256,256]{4,3,2,1,0:T(8,128)(2,1)}, u32[]{:S(2)}, u32[]{:S(2)}) collective-permute-start(bf16[2,2,2,256,256]{4,3,2,1,0:T(8,128)(2,1)} %get-tuple-element.58), channel_id=1, source_target_pairs={{0,1},{1,0},{2,3},{3,2},{4,5},{5,4},{6,7},{7,6},{8,9},{9,8},{10,11... | collective-permute-start | bytes 3145736 | tf_op jit(solution)/shard_map/core3/ppermute | solution.py:441
  47.7 39.2 %collective-permute-start.22 = (bf16[2,2,2,256,256]{4,3,2,1,0:T(8,128)(2,1)}, bf16[2,2,2,256,256]{4,3,2,1,0:T(8,128)(2,1)}, u32[]{:S(2)}, u32[]{:S(2)}) collective-permute-start(bf16[2,2,2,256,256]{4,3,2,1,0:T(8,128)(2,1)} %get-tuple-element.56.refs_2_), channel_id=1, source_target_pairs={{0,2},{1,3},{2,0},{3,1},{4,6},{5,7},{6,4},{7,5},{8,10},{9,11},{10,... | collective-permute-start | bytes 3145736 | tf_op jit(solution)/shard_map/pair0/ppermute | solution.py:441
  53.7 1.5 %collective-permute-start.12 = (f32[2,8,256]{2,1,0:T(8,128)}, f32[2,8,256]{2,1,0:T(8,128)}, u32[]{:S(2)}, u32[]{:S(2)}) collective-permute-start(f32[2,8,256]{2,1,0:T(8,128)} %get-tuple-element.62.refs_1_), channel_id=1, source_target_pairs={{0,1},{1,0},{2,3},{3,2},{4,5},{5,4},{6,7},{7,6},{8,9},{9,8},{10,11... | collective-permute-start | bytes 49160 | tf_op jit(solution)/shard_map/beat1/ppermute | solution.py:441
  55.2 37.7 %collective-permute-start.20 = (bf16[2,2,256,256]{3,2,1,0:T(8,128)(2,1)}, bf16[2,2,256,256]{3,2,1,0:T(8,128)(2,1)}, u32[]{:S(2)}, u32[]{:S(2)}) collective-permute-start(bf16[2,2,256,256]{3,2,1,0:T(8,128)(2,1)} %get-tuple-element.71), channel_id=1, source_target_pairs={{0,4},{4,8},{8,12},{12,16},{16,20},{20,24},{24,28},{1,5},{5,9},{9,... | collective-permute-start | bytes 1572872 | tf_op jit(solution)/shard_map/up1/ppermute | solution.py:441
  58.3 7.6 %collective-permute-start.13 = (bf16[2,2,256,256]{3,2,1,0:T(8,128)(2,1)}, bf16[2,2,256,256]{3,2,1,0:T(8,128)(2,1)}, u32[]{:S(2)}, u32[]{:S(2)}) collective-permute-start(bf16[2,2,256,256]{3,2,1,0:T(8,128)(2,1)} %get-tuple-element.63.refs_1_.refs_2_), channel_id=1, source_target_pairs={{0,1},{1,0},{2,3},{3,2},{4,5},{5,4},{6,7},{7,6},{8,9},{9,8},{10,11... | collective-permute-start | bytes 1572872 | tf_op jit(solution)/shard_map/core_up2/ppermute | solution.py:441
  58.3 7.6 %collective-permute-start.14 = (bf16[2,2,256,256]{3,2,1,0:T(8,128)(2,1)}, bf16[2,2,256,256]{3,2,1,0:T(8,128)(2,1)}, u32[]{:S(2)}, u32[]{:S(2)}) collective-permute-start(bf16[2,2,256,256]{3,2,1,0:T(8,128)(2,1)} %get-tuple-element.64.refs_3_), channel_id=1, source_target_pairs={{0,1},{1,0},{2,3},{3,2},{4,5},{5,4},{6,7},{7,6},{8,9},{9,8},{10,11... | collective-permute-start | bytes 1572872 | tf_op jit(solution)/shard_map/core_down2/ppermute | solution.py:441
  62.6 30.4 %collective-permute-start.21 = (bf16[2,2,256,256]{3,2,1,0:T(8,128)(2,1)}, bf16[2,2,256,256]{3,2,1,0:T(8,128)(2,1)}, u32[]{:S(2)}, u32[]{:S(2)}) collective-permute-start(bf16[2,2,256,256]{3,2,1,0:T(8,128)(2,1)} %get-tuple-element.72), channel_id=1, source_target_pairs={{4,0},{8,4},{12,8},{16,12},{20,16},{24,20},{28,24},{5,1},{9,5},{13... | collective-permute-start | bytes 1572872 | tf_op jit(solution)/shard_map/down1/ppermute | solution.py:441
  66.0 6.2 %collective-permute-start.17 = (bf16[2,2,2,256,256]{4,3,2,1,0:T(8,128)(2,1)}, bf16[2,2,2,256,256]{4,3,2,1,0:T(8,128)(2,1)}, u32[]{:S(2)}, u32[]{:S(2)}) collective-permute-start(bf16[2,2,2,256,256]{4,3,2,1,0:T(8,128)(2,1)} %gate.25.refs_6_.refs_2_), channel_id=1, source_target_pairs={{0,1},{1,0},{2,3},{3,2},{4,5},{5,4},{6,7},{7,6},{8,9},{9,8},{10,11... | collective-permute-start | bytes 3145736 | tf_op jit(solution)/shard_map/core_pair3/ppermute | solution.py:441
  70.7 38.2 %collective-permute-start.16 = (bf16[2,2,2,256,256]{4,3,2,1,0:T(8,128)(2,1)}, bf16[2,2,2,256,256]{4,3,2,1,0:T(8,128)(2,1)}, u32[]{:S(2)}, u32[]{:S(2)}) collective-permute-start(bf16[2,2,2,256,256]{4,3,2,1,0:T(8,128)(2,1)} %get-tuple-element.66.refs_4_), channel_id=1, source_target_pairs={{0,2},{1,3},{2,0},{3,1},{4,6},{5,7},{6,4},{7,5},{8,10},{9,11},{10,... | collective-permute-start | bytes 3145736 | tf_op jit(solution)/shard_map/pair2/ppermute | solution.py:441
  76.7 29.5 %collective-permute-start.19 = (bf16[2,2,256,256]{3,2,1,0:T(8,128)(2,1)}, bf16[2,2,256,256]{3,2,1,0:T(8,128)(2,1)}, u32[]{:S(2)}, u32[]{:S(2)}) collective-permute-start(bf16[2,2,256,256]{3,2,1,0:T(8,128)(2,1)} %get-tuple-element.67.refs_4_), channel_id=1, source_target_pairs={{4,0},{8,4},{12,8},{16,12},{20,16},{24,20},{28,24},{5,1},{9,5},{13... | collective-permute-start | bytes 1572872 | tf_op jit(solution)/shard_map/down3/ppermute | solution.py:441
  81.0 27.8 %all-to-all-start = ((f32[32,1,128]{2,1,0:T(1,128)}), f32[32,1,128]{2,1,0:T(1,128)}, u32[]{:S(2)}, u32[]{:S(2)}) async-start(f32[32,1,128]{2,1,0:T(1,128)} %range_parts.1.refs_1_), calls=%async_computation | async-start | bytes 32768 | tf_op jit(solution)/shard_map/all_to_all | solution.py:523
  86.9 17.2 %collective-permute-start.18 = (bf16[2,2,256,256]{3,2,1,0:T(8,128)(2,1)}, bf16[2,2,256,256]{3,2,1,0:T(8,128)(2,1)}, u32[]{:S(2)}, u32[]{:S(2)}) collective-permute-start(bf16[2,2,256,256]{3,2,1,0:T(8,128)(2,1)} %get-tuple-element.69), channel_id=1, source_target_pairs={{0,4},{4,8},{8,12},{12,16},{16,20},{20,24},{24,28},{1,5},{5,9},{9,... | collective-permute-start | bytes 1572872 | tf_op jit(solution)/shard_map/up3/ppermute | solution.py:441

commit v4 on v3

--- a/solution.py
+++ b/solution.py
@@ -10,7 +10,7 @@
 CHUNKS = (("late", 0, 2), ("early", 2, 2), ("late", 6, 2), ("early", 4, 2))
 VMEM = 63 * 2**20
 TILE = 16
-UNROLL = 4
+UNROLL = 16
 ANY = pl.BlockSpec(memory_space=pltpu.HBM)
 FACTOR = 100.0
 
@@ -492,19 +492,19 @@
     up0, down0 = gate([up0, down0], (n0, c2))
     core_up0, core_down0 = core(up0, "core_up0"), core(down0, "core_down0")
     (c0,) = gate([c0], (up0,))
-    members0 = (g0, c0, up0, down0, core_up0, core_down0)
-    total0, local0 = late_sum(weights, members0, ())
-    x0 = pair(total0, "pair0")
-    y1, h3 = gate([y1, h3], (total0,))
+    y1, h3 = gate([y1, h3], (c0,))
     core_y1, c3 = core(y1, "core_pair1"), core(h3, "core3")
     (c1,) = gate([c1], (y1,))
-
     members1 = (g1, c1, y1, core_y1)
     high1, low1, local1 = early_edges(weights, members1, (c3,))
     high1, low1, n1 = gate([high1, low1, n1], ())
     up1, down1, beat1 = rise(high1, "1"), fall(low1, "1"), core(n1, "beat1")
     (n2,) = gate([n2], (n1,))
-    (n3,) = gate([n3], (n2, beat1))
+
+    members0 = (g0, c0, up0, down0, core_up0, core_down0)
+    total0, local0 = late_sum(weights, members0, (n2,))
+    x0 = pair(total0, "pair0")
+    (n3,) = gate([n3], (total0, beat1))
 
     up2, down2 = gate([up2, down2], (n3,))
     core_up2, core_down2 = core(up2, "core_up2"), core(down2, "core_down2")

time: 113 us -> 112 us (level)
  Pallas kernels: 52.4 us -> 50.9 us
  transfers between devices with their start and end apart: 24 -> 24, of which waited for: 8 -> 7; matrix products, arithmetic and copies ran while one was open for 0% -> 0% of each run, Pallas kernels for 40% -> 39%
where the time goes in v4:
time: 112 us; the launch traced here: 111 us
  Pallas kernels  50.9 us (45%)
  starting transfers between devices  37.9 us (34%)
  waiting for transfers between devices  21.5 us (19%)
    ppermute x23, starting transfers between devices, send(): return lax.ppermute(value, axis, pairs)  32 us
    ppermute x23, waiting for transfers between devices, send(): return lax.ppermute(value, axis, pairs)  21.5 us
    pallas_call x4, Pallas kernels, solve(): pl.pallas_call(functools.partial(solve_kernel, first, edges, again), grid...  19.6 us
    pallas_call x4, Pallas kernels, finish(): pl.pallas_call(functools.partial(finish_kernel, late, parts is not None),...  10.1 us
    pallas_call x2, Pallas kernels, late_sum(): pl.pallas_call(late_sum_kernel, grid=(count,), in_specs=[pl.BlockSpec(mem...  8.92 us
    pallas_call x2, Pallas kernels, early_edges(): pl.pallas_call(early_edges_kernel, grid=(count,), in_specs=[pl.BlockSpec(...  8.57 us
    all_to_all x1, starting transfers between devices, body(): lax.all_to_all(parts, ('energy', 'mom'), split_axis=0, concat_axis=0, til...  5.8 us
  transfers between devices with their start and end apart: 24, of which 7 were waited for; matrix products, arithmetic and copies ran while one was open for 0% of the time, Pallas kernels for 39%

profile of v4, /device:TPU:24, one launch (start us, length us, event | category | flops | bytes accessed | tf_op | source)
XLA Modules:
  0.0 111.1 jit_solution(18327095647682944446)
XLA Ops:
  0.6 4.8 %solve.4 = (bf16[2,2,2,256,256]{4,3,2,1,0:T(8,128)(2,1)}, f32[2,8,256]{2,1,0:T(8,128)}, bf16[2,2,256,256]{3,2,1,0:T(8,128)(2,1)}, bf16[2,2,256,256]{3,2,1,0:T(8,128)(2,1)}) custom-call(bf16[2,2,1,2048,256]{4,3,2,1,0:T(8,128)(2,1)} %refs_0_.7, bf16[2,1,2048,256]{3,2,1,0:T(8,128)(2,1)} %refs_1_.7), custom_call_target="tpu_custom_call" | custom-call | flops 575000018944 | tf_op jit(solution)/shard_map/solve/pallas_call | solution.py:147
  5.4 0.0 collective-permute-start
  5.4 3.4 %collective-permute-start.5 = (bf16[2,2,256,256]{3,2,1,0:T(8,128)(2,1)}, bf16[2,2,256,256]{3,2,1,0:T(8,128)(2,1)}, u32[]{:S(2)}, u32[]{:S(2)}) collective-permute-start(bf16[2,2,256,256]{3,2,1,0:T(8,128)(2,1)} %get-tuple-element.50), channel_id=1, source_target_pairs={{0,4},{4,8},{8,12},{12,16},{16,20},{20,24},{24,28},{1,5},{5,9},{9,... | collective-permute-start | bytes 1572872 | tf_op jit(solution)/shard_map/up0/ppermute | solution.py:441
  8.8 0.0 collective-permute-done.refs_3_.refs_0_
  8.8 4.7 %solve.5 = (bf16[2,2,2,256,256]{4,3,2,1,0:T(8,128)(2,1)}, f32[2,8,256]{2,1,0:T(8,128)}) custom-call(bf16[2,2,1,2048,256]{4,3,2,1,0:T(8,128)(2,1)} %refs_0_.7, bf16[2,1,2048,256]{3,2,1,0:T(8,128)(2,1)} %refs_1_.7, bf16[2,2,2,256,256]{4,3,2,1,0:T(8,128)(2,1)} %get-tuple-element.38.refs_2_.refs_0_, bf16[2,2,2,256,256]{4,3,2,1,0:T(8,128)(2,1)} %collective-permute-done.refs_3_.refs_0_), custom_call_target="tpu_custom_call" | custom-call | flops 575000018944 | tf_op jit(solution)/shard_map/solve/pallas_call | solution.py:147
  13.5 0.2 collective-permute-start.1
  13.8 1.5 %collective-permute-start.9 = (bf16[2,2,2,256,256]{4,3,2,1,0:T(8,128)(2,1)}, bf16[2,2,2,256,256]{4,3,2,1,0:T(8,128)(2,1)}, u32[]{:S(2)}, u32[]{:S(2)}) collective-permute-start(bf16[2,2,2,256,256]{4,3,2,1,0:T(8,128)(2,1)} %get-tuple-element.39.refs_2_.refs_1_.refs_0_), channel_id=1, source_target_pairs={{0,2},{1,3},{2,0},{3,1},{4,6},{5,7},{6,4},{7,5},{8,10},{9,11},{10,... | collective-permute-start | bytes 3145736 | tf_op jit(solution)/shard_map/pair1/ppermute | solution.py:441
  15.3 3.3 %collective-permute-start.6 = (bf16[2,2,256,256]{3,2,1,0:T(8,128)(2,1)}, bf16[2,2,256,256]{3,2,1,0:T(8,128)(2,1)}, u32[]{:S(2)}, u32[]{:S(2)}) collective-permute-start(bf16[2,2,256,256]{3,2,1,0:T(8,128)(2,1)} %gate.14), channel_id=1, source_target_pairs={{4,0},{8,4},{12,8},{16,12},{20,16},{24,20},{28,24},{5,1},{9,5},{13... | collective-permute-start | bytes 1572872 | tf_op jit(solution)/shard_map/down0/ppermute | solution.py:441
  18.6 0.0 collective-permute-done.1.refs_3_.refs_0_
  18.6 4.9 %solve.6 = (bf16[2,2,2,256,256]{4,3,2,1,0:T(8,128)(2,1)}, f32[2,8,256]{2,1,0:T(8,128)}, bf16[2,2,2,256,256]{4,3,2,1,0:T(8,128)(2,1)}) custom-call(bf16[2,2,1,2048,256]{4,3,2,1,0:T(8,128)(2,1)} %refs_0_.7, bf16[2,1,2048,256]{3,2,1,0:T(8,128)(2,1)} %refs_1_.7, bf16[2,2,2,256,256]{4,3,2,1,0:T(8,128)(2,1)} %get-tuple-element.39.refs_2_.refs_1_.refs_0_, ...), custom_call_target="tpu_custom_call" | custom-call | flops 575000018944 | tf_op jit(solution)/shard_map/solve/pallas_call | solution.py:147
  23.5 5.2 %solve.7 = (bf16[2,2,2,256,256]{4,3,2,1,0:T(8,128)(2,1)}, f32[2,8,256]{2,1,0:T(8,128)}, bf16[2,2,256,256]{3,2,1,0:T(8,128)(2,1)}, bf16[2,2,256,256]{3,2,1,0:T(8,128)(2,1)}, bf16[2,2,2,256,256]{4,3,2,1,0:T(8,128)(2,1)}) custom-call(bf16[2,2,1,2048,256]{4,3,2,1,0:T(8,128)(2,1)} %refs_0_.7, bf16[2,1,2048,256]{3,2,1,0:T(8,128)(2,1)} %refs_1_.7, ...), custom_call_target="tpu_custom_call" | custom-call | flops 575000018944 | tf_op jit(solution)/shard_map/solve/pallas_call | solution.py:147
  28.7 1.7 %own_weights.1.refs_3_.w_ref = f32[2,3,4]{2,1,0:T(4,128)} custom-call(s32[4]{0:T(128)} %shift_ref.1, f32[4,4,4]{2,1,0:T(4,128)} %emission_ref.1, f32[4,4,4]{2,1,0:T(4,128)} %absorption_ref.1, f32[2,8,256]{2,1,0:T(8,128)} %get-tuple-element.41.refs_0_), custom_call_target="tpu_custom_call" | custom-call | flops 57500000256 | tf_op jit(solution)/shard_map/own_weights/pallas_call | solution.py:414
  30.5 0.1 collective-permute-start.2
  30.5 2.4 %collective-permute-start.4 = (bf16[2,2,256,256]{3,2,1,0:T(8,128)(2,1)}, bf16[2,2,256,256]{3,2,1,0:T(8,128)(2,1)}, u32[]{:S(2)}, u32[]{:S(2)}) collective-permute-start(bf16[2,2,256,256]{3,2,1,0:T(8,128)(2,1)} %get-tuple-element.48.refs_1_), channel_id=1, source_target_pairs={{4,0},{8,4},{12,8},{16,12},{20,16},{24,20},{28,24},{5,1},{9,5},{13... | collective-permute-start | bytes 1572872 | tf_op jit(solution)/shard_map/down2/ppermute | solution.py:441
  32.9 0.0 collective-permute-done.5.refs_0_
  33.0 0.6 collective-permute-start.15
  33.6 0.5 collective-permute-done.6.refs_1_
  34.1 3.6 %collective-permute-start.3 = (bf16[2,2,256,256]{3,2,1,0:T(8,128)(2,1)}, bf16[2,2,256,256]{3,2,1,0:T(8,128)(2,1)}, u32[]{:S(2)}, u32[]{:S(2)}) collective-permute-start(bf16[2,2,256,256]{3,2,1,0:T(8,128)(2,1)} %get-tuple-element.47), channel_id=1, source_target_pairs={{0,4},{4,8},{8,12},{12,16},{16,20},{20,24},{24,28},{1,5},{5,9},{9,... | collective-permute-start | bytes 1572872 | tf_op jit(solution)/shard_map/up2/ppermute | solution.py:441
  37.7 0.0 collective-permute-done.2.refs_3_.refs_0_
  37.8 2.3 %collective-permute-done.9.refs_0_ = bf16[2,2,2,256,256]{4,3,2,1,0:T(8,128)(2,1)} collective-permute-done((bf16[2,2,2,256,256]{4,3,2,1,0:T(8,128)(2,1)}, bf16[2,2,2,256,256]{4,3,2,1,0:T(8,128)(2,1)}, u32[]{:S(2)}, u32[]{:S(2)}) %collective-permute-start.9) | collective-permute-done | bytes 1048608 | tf_op jit(solution)/shard_map/pair1/ppermute | solution.py:441
  40.1 0.0 collective-permute-start.10
  40.1 0.5 collective-permute-start.11
  40.6 2.5 %collective-permute-done.10.refs_3_ = bf16[2,2,2,256,256]{4,3,2,1,0:T(8,128)(2,1)} collective-permute-done((bf16[2,2,2,256,256]{4,3,2,1,0:T(8,128)(2,1)}, bf16[2,2,2,256,256]{4,3,2,1,0:T(8,128)(2,1)}, u32[]{:S(2)}, u32[]{:S(2)}) %collective-permute-start.10) | collective-permute-done | bytes 1048608 | tf_op jit(solution)/shard_map/core_pair1/ppermute | solution.py:441
  43.1 0.1 collective-permute-start.7
  43.2 1.4 %collective-permute-done.11.refs_4_.refs_1_ = bf16[2,2,2,256,256]{4,3,2,1,0:T(8,128)(2,1)} collective-permute-done((bf16[2,2,2,256,256]{4,3,2,1,0:T(8,128)(2,1)}, bf16[2,2,2,256,256]{4,3,2,1,0:T(8,128)(2,1)}, u32[]{:S(2)}, u32[]{:S(2)}) %collective-permute-start.11) | collective-permute-done | bytes 1048608 | tf_op jit(solution)/shard_map/core3/ppermute | solution.py:441
  44.6 0.1 collective-permute-start.8
  44.7 4.3 %early_edges.2 = (bf16[2,2,256,256]{3,2,1,0:T(8,128)(2,1)}, bf16[2,2,256,256]{3,2,1,0:T(8,128)(2,1)}, bf16[2,2,2,256,256]{4,3,2,1,0:T(8,128)(2,1)}) custom-call(f32[2,3,4]{2,1,0:T(4,128)} %own_weights.1.refs_3_.w_ref, bf16[2,2,2,256,256]{4,3,2,1,0:T(8,128)(2,1)} %get-tuple-element.39.refs_2_.refs_1_.refs_0_, bf16[2,2,2,256,256]{4,3,2,1,0:T(8,128)(2,1)} %gate.19.refs_1_, ...), custom_call_target="tpu_custom_call" | custom-call | flops 390999998464 | tf_op jit(solution)/shard_map/early_edges/pallas_call | solution.py:235
  49.0 0.0 collective-permute-done.7.refs_4_
  49.0 0.4 collective-permute-start.12
  49.4 0.0 collective-permute-done.8.refs_5_
  49.4 4.5 %late_sum.2 = (bf16[2,2,2,256,256]{4,3,2,1,0:T(8,128)(2,1)}, bf16[2,2,2,256,256]{4,3,2,1,0:T(8,128)(2,1)}) custom-call(f32[2,3,4]{2,1,0:T(4,128)} %own_weights.1.refs_3_.w_ref, bf16[2,2,2,256,256]{4,3,2,1,0:T(8,128)(2,1)} %get-tuple-element.38.refs_2_.refs_0_, bf16[2,2,2,256,256]{4,3,2,1,0:T(8,128)(2,1)} %gate.17.refs_2_.refs_1_, ...), custom_call_target="tpu_custom_call" | custom-call | flops 413999988736 | tf_op jit(solution)/shard_map/late_sum/pallas_call | solution.py:275
  53.9 1.5 %collective-permute-start.22 = (bf16[2,2,2,256,256]{4,3,2,1,0:T(8,128)(2,1)}, bf16[2,2,2,256,256]{4,3,2,1,0:T(8,128)(2,1)}, u32[]{:S(2)}, u32[]{:S(2)}) collective-permute-start(bf16[2,2,2,256,256]{4,3,2,1,0:T(8,128)(2,1)} %get-tuple-element.62.refs_1_), channel_id=1, source_target_pairs={{0,2},{1,3},{2,0},{3,1},{4,6},{5,7},{6,4},{7,5},{8,10},{9,11},{10,... | collective-permute-start | bytes 3145736 | tf_op jit(solution)/shard_map/pair0/ppermute | solution.py:441
  55.4 0.0 collective-permute-done.12.refs_2_
  55.4 2.9 %collective-permute-start.20 = (bf16[2,2,256,256]{3,2,1,0:T(8,128)(2,1)}, bf16[2,2,256,256]{3,2,1,0:T(8,128)(2,1)}, u32[]{:S(2)}, u32[]{:S(2)}) collective-permute-start(bf16[2,2,256,256]{3,2,1,0:T(8,128)(2,1)} %get-tuple-element.71), channel_id=1, source_target_pairs={{0,4},{4,8},{8,12},{12,16},{16,20},{20,24},{24,28},{1,5},{5,9},{9,... | collective-permute-start | bytes 1572872 | tf_op jit(solution)/shard_map/up1/ppermute | solution.py:441
  58.3 0.0 collective-permute-done.3.refs_0_
  58.3 0.0 collective-permute-done.4.refs_1_
  58.3 0.1 collective-permute-start.13
  58.4 0.5 collective-permute-start.14
  58.9 3.6 %collective-permute-done.15.refs_0_ = bf16[2,2,2,256,256]{4,3,2,1,0:T(8,128)(2,1)} collective-permute-done((bf16[2,2,2,256,256]{4,3,2,1,0:T(8,128)(2,1)}, bf16[2,2,2,256,256]{4,3,2,1,0:T(8,128)(2,1)}, u32[]{:S(2)}, u32[]{:S(2)}) %collective-permute-start.15) | collective-permute-done | bytes 1048608 | tf_op jit(solution)/shard_map/pair3/ppermute | solution.py:441
  62.5 3.3 %collective-permute-start.21 = (bf16[2,2,256,256]{3,2,1,0:T(8,128)(2,1)}, bf16[2,2,256,256]{3,2,1,0:T(8,128)(2,1)}, u32[]{:S(2)}, u32[]{:S(2)}) collective-permute-start(bf16[2,2,256,256]{3,2,1,0:T(8,128)(2,1)} %get-tuple-element.72), channel_id=1, source_target_pairs={{4,0},{8,4},{12,8},{16,12},{20,16},{24,20},{28,24},{5,1},{9,5},{13... | collective-permute-start | bytes 1572872 | tf_op jit(solution)/shard_map/down1/ppermute | solution.py:441
  65.9 0.0 collective-permute-done.13.refs_2_.refs_4_
  65.9 0.0 collective-permute-done.14.refs_3_.refs_5_
  65.9 0.1 collective-permute-start.17
  66.0 4.5 %late_sum.3 = (bf16[2,2,2,256,256]{4,3,2,1,0:T(8,128)(2,1)}, bf16[2,2,2,256,256]{4,3,2,1,0:T(8,128)(2,1)}) custom-call(f32[2,3,4]{2,1,0:T(4,128)} %own_weights.1.refs_3_.w_ref, bf16[2,2,2,256,256]{4,3,2,1,0:T(8,128)(2,1)} %get-tuple-element.42.refs_0_, bf16[2,2,2,256,256]{4,3,2,1,0:T(8,128)(2,1)} %gate.24.refs_1_, ...), custom_call_target="tpu_custom_call" | custom-call | flops 413999988736 | tf_op jit(solution)/shard_map/late_sum/pallas_call | solution.py:275
  70.4 1.5 %collective-permute-start.16 = (bf16[2,2,2,256,256]{4,3,2,1,0:T(8,128)(2,1)}, bf16[2,2,2,256,256]{4,3,2,1,0:T(8,128)(2,1)}, u32[]{:S(2)}, u32[]{:S(2)}) collective-permute-start(bf16[2,2,2,256,256]{4,3,2,1,0:T(8,128)(2,1)} %get-tuple-element.66.refs_4_), channel_id=1, source_target_pairs={{0,2},{1,3},{2,0},{3,1},{4,6},{5,7},{6,4},{7,5},{8,10},{9,11},{10,... | collective-permute-start | bytes 3145736 | tf_op jit(solution)/shard_map/pair2/ppermute | solution.py:441
  72.0 0.0 collective-permute-done.17.refs_3_
  72.0 4.3 %early_edges.3 = (bf16[2,2,256,256]{3,2,1,0:T(8,128)(2,1)}, bf16[2,2,256,256]{3,2,1,0:T(8,128)(2,1)}, bf16[2,2,2,256,256]{4,3,2,1,0:T(8,128)(2,1)}) custom-call(f32[2,3,4]{2,1,0:T(4,128)} %own_weights.1.refs_3_.w_ref, bf16[2,2,2,256,256]{4,3,2,1,0:T(8,128)(2,1)} %get-tuple-element.40.refs_2_.refs_0_, ...), custom_call_target="tpu_custom_call" | custom-call | flops 390999998464 | tf_op jit(solution)/shard_map/early_edges/pallas_call | solution.py:235
  76.3 2.4 %collective-permute-start.19 = (bf16[2,2,256,256]{3,2,1,0:T(8,128)(2,1)}, bf16[2,2,256,256]{3,2,1,0:T(8,128)(2,1)}, u32[]{:S(2)}, u32[]{:S(2)}) collective-permute-start(bf16[2,2,256,256]{3,2,1,0:T(8,128)(2,1)} %get-tuple-element.67.refs_4_), channel_id=1, source_target_pairs={{4,0},{8,4},{12,8},{16,12},{20,16},{24,20},{28,24},{5,1},{9,5},{13... | collective-permute-start | bytes 1572872 | tf_op jit(solution)/shard_map/down3/ppermute | solution.py:441
  78.7 2.0 %range_parts.1.refs_1_ = f32[32,1,128]{2,1,0:T(1,128)} custom-call(s32[32]{0:T(128)} %range_ref.1, f32[2,8,256]{2,1,0:T(8,128)} %gate.15.refs_2_.refs_0_, f32[2,8,256]{2,1,0:T(8,128)} %get-tuple-element.61.refs_1_, f32[2,8,256]{2,1,0:T(8,128)} %gate.22.refs_2_, f32[2,8,256]{2,1,0:T(8,128)} %gate.21.refs_6_.refs_3_, ...), custom_call_target="tpu_custom_call" | custom-call | flops 253000007680 | tf_op jit(solution)/shard_map/range_parts/pallas_call | solution.py:383
  80.6 5.8 %all-to-all-start = ((f32[32,1,128]{2,1,0:T(1,128)}), f32[32,1,128]{2,1,0:T(1,128)}, u32[]{:S(2)}, u32[]{:S(2)}) async-start(f32[32,1,128]{2,1,0:T(1,128)} %range_parts.1.refs_1_), calls=%async_computation | async-start | bytes 32768 | tf_op jit(solution)/shard_map/all_to_all | solution.py:523
  86.4 0.0 collective-permute-done.22.refs_0_
  86.4 3.4 %collective-permute-start.18 = (bf16[2,2,256,256]{3,2,1,0:T(8,128)(2,1)}, bf16[2,2,256,256]{3,2,1,0:T(8,128)(2,1)}, u32[]{:S(2)}, u32[]{:S(2)}) collective-permute-start(bf16[2,2,256,256]{3,2,1,0:T(8,128)(2,1)} %get-tuple-element.69), channel_id=1, source_target_pairs={{0,4},{4,8},{8,12},{12,16},{16,20},{20,24},{24,28},{1,5},{5,9},{9,... | collective-permute-start | bytes 1572872 | tf_op jit(solution)/shard_map/up3/ppermute | solution.py:441
  89.8 2.5 %finish.4.refs_2_ = bf16[2,2,1,2048,256]{4,3,2,1,0:T(8,128)(2,1)} custom-call(f32[8,1,256]{2,1,0:T(1,128)} %bitcast.1, bf16[2,2,2,256,256]{4,3,2,1,0:T(8,128)(2,1)} %get-tuple-element.73.local_ref, bf16[2,2,2,256,256]{4,3,2,1,0:T(8,128)(2,1)} %collective-permute-done.22.refs_0_, f32[32,1,128]{2,1,0:T(1,128)} %range_parts.1.refs_1_), custom_call_target="tpu_custom_call" | custom-call | flops 506000015360 | tf_op jit(solution)/shard_map/finish/pallas_call | solution.py:343
  92.4 0.0 collective-permute-done.20.refs_0_
  92.4 0.0 collective-permute-done.21.refs_1_
  92.4 2.5 %finish.5.refs_2_ = bf16[2,2,1,2048,256]{4,3,2,1,0:T(8,128)(2,1)} custom-call(f32[8,1,256]{2,1,0:T(1,128)} %bitcast.2, bf16[2,2,2,256,256]{4,3,2,1,0:T(8,128)(2,1)} %get-tuple-element.70.local_ref, bf16[2,2,256,256]{3,2,1,0:T(8,128)(2,1)} %collective-permute-done.20.refs_0_, ...), custom_call_target="tpu_custom_call", output_to_operand_aliasing={{}: (4, {})} | custom-call | flops 506000015360 | tf_op jit(solution)/shard_map/finish/pallas_call | solution.py:343
  94.9 8.7 %collective-permute-done.18.refs_0_ = bf16[2,2,256,256]{3,2,1,0:T(8,128)(2,1)} collective-permute-done((bf16[2,2,256,256]{3,2,1,0:T(8,128)(2,1)}, bf16[2,2,256,256]{3,2,1,0:T(8,128)(2,1)}, u32[]{:S(2)}, u32[]{:S(2)}) %collective-permute-start.18) | collective-permute-done | bytes 524320 | tf_op jit(solution)/shard_map/up3/ppermute | solution.py:441
  103.6 2.4 %collective-permute-done.19.refs_1_ = bf16[2,2,256,256]{3,2,1,0:T(8,128)(2,1)} collective-permute-done((bf16[2,2,256,256]{3,2,1,0:T(8,128)(2,1)}, bf16[2,2,256,256]{3,2,1,0:T(8,128)(2,1)}, u32[]{:S(2)}, u32[]{:S(2)}) %collective-permute-start.19) | collective-permute-done | bytes 524320 | tf_op jit(solution)/shard_map/down3/ppermute | solution.py:441
  106.0 2.5 %finish.6.refs_2_ = bf16[2,2,1,2048,256]{4,3,2,1,0:T(8,128)(2,1)} custom-call(f32[8,1,256]{2,1,0:T(1,128)} %bitcast.3, bf16[2,2,2,256,256]{4,3,2,1,0:T(8,128)(2,1)} %get-tuple-element.68.local_ref, bf16[2,2,256,256]{3,2,1,0:T(8,128)(2,1)} %collective-permute-done.18.refs_0_, ...), custom_call_target="tpu_custom_call", output_to_operand_aliasing={{}: (4, {})} | custom-call | flops 506000015360 | tf_op jit(solution)/shard_map/finish/pallas_call | solution.py:343
  108.6 0.0 collective-permute-done.16.refs_0_
  108.6 0.0 all-to-all-done.refs_1_
  108.6 2.6 %finish.7 = (bf16[2,2,1,2048,256]{4,3,2,1,0:T(8,128)(2,1)}, f32[1]{0:T(128)}) custom-call(f32[8,1,256]{2,1,0:T(1,128)} %bitcast.4, bf16[2,2,2,256,256]{4,3,2,1,0:T(8,128)(2,1)} %get-tuple-element.65.local_ref, bf16[2,2,2,256,256]{4,3,2,1,0:T(8,128)(2,1)} %collective-permute-done.16.refs_0_, ...), custom_call_target="tpu_custom_call", output_to_operand_aliasing={{0}: (4, {})} | custom-call | flops 506000015360 | tf_op jit(solution)/shard_map/finish/pallas_call | solution.py:343
  (13 shorter events, 0.0 us)
Async XLA Ops:
  5.4 3.4 %collective-permute-start = (bf16[2,2,2,256,256]{4,3,2,1,0:T(8,128)(2,1)}, bf16[2,2,2,256,256]{4,3,2,1,0:T(8,128)(2,1)}, u32[]{:S(2)}, u32[]{:S(2)}) collective-permute-start(bf16[2,2,2,256,256]{4,3,2,1,0:T(8,128)(2,1)} %get-tuple-element.38.refs_2_.refs_0_), channel_id=1, source_target_pairs={{0,1},{1,0},{2,3},{3,2},{4,5},{5,4},{6,7},{7,6},{8,9},{9,8},{10,11... | collective-permute-start | bytes 3145736 | tf_op jit(solution)/shard_map/core0/ppermute | solution.py:441
  5.4 27.5 %collective-permute-start.5 = (bf16[2,2,256,256]{3,2,1,0:T(8,128)(2,1)}, bf16[2,2,256,256]{3,2,1,0:T(8,128)(2,1)}, u32[]{:S(2)}, u32[]{:S(2)}) collective-permute-start(bf16[2,2,256,256]{3,2,1,0:T(8,128)(2,1)} %get-tuple-element.50), channel_id=1, source_target_pairs={{0,4},{4,8},{8,12},{12,16},{16,20},{20,24},{24,28},{1,5},{5,9},{9,... | collective-permute-start | bytes 1572872 | tf_op jit(solution)/shard_map/up0/ppermute | solution.py:441
  13.5 5.1 %collective-permute-start.1 = (bf16[2,2,2,256,256]{4,3,2,1,0:T(8,128)(2,1)}, bf16[2,2,2,256,256]{4,3,2,1,0:T(8,128)(2,1)}, u32[]{:S(2)}, u32[]{:S(2)}) collective-permute-start(bf16[2,2,2,256,256]{4,3,2,1,0:T(8,128)(2,1)} %get-tuple-element.39.refs_2_.refs_1_.refs_0_), channel_id=1, source_target_pairs={{0,1},{1,0},{2,3},{3,2},{4,5},{5,4},{6,7},{7,6},{8,9},{9,8},{10,11... | collective-permute-start | bytes 3145736 | tf_op jit(solution)/shard_map/core1/ppermute | solution.py:441
  13.8 26.3 %collective-permute-start.9 = (bf16[2,2,2,256,256]{4,3,2,1,0:T(8,128)(2,1)}, bf16[2,2,2,256,256]{4,3,2,1,0:T(8,128)(2,1)}, u32[]{:S(2)}, u32[]{:S(2)}) collective-permute-start(bf16[2,2,2,256,256]{4,3,2,1,0:T(8,128)(2,1)} %get-tuple-element.39.refs_2_.refs_1_.refs_0_), channel_id=1, source_target_pairs={{0,2},{1,3},{2,0},{3,1},{4,6},{5,7},{6,4},{7,5},{8,10},{9,11},{10,... | collective-permute-start | bytes 3145736 | tf_op jit(solution)/shard_map/pair1/ppermute | solution.py:441
  15.3 18.8 %collective-permute-start.6 = (bf16[2,2,256,256]{3,2,1,0:T(8,128)(2,1)}, bf16[2,2,256,256]{3,2,1,0:T(8,128)(2,1)}, u32[]{:S(2)}, u32[]{:S(2)}) collective-permute-start(bf16[2,2,256,256]{3,2,1,0:T(8,128)(2,1)} %gate.14), channel_id=1, source_target_pairs={{4,0},{8,4},{12,8},{16,12},{20,16},{24,20},{28,24},{5,1},{9,5},{13... | collective-permute-start | bytes 1572872 | tf_op jit(solution)/shard_map/down0/ppermute | solution.py:441
  30.5 7.3 %collective-permute-start.2 = (bf16[2,2,2,256,256]{4,3,2,1,0:T(8,128)(2,1)}, bf16[2,2,2,256,256]{4,3,2,1,0:T(8,128)(2,1)}, u32[]{:S(2)}, u32[]{:S(2)}) collective-permute-start(bf16[2,2,2,256,256]{4,3,2,1,0:T(8,128)(2,1)} %get-tuple-element.46), channel_id=1, source_target_pairs={{0,1},{1,0},{2,3},{3,2},{4,5},{5,4},{6,7},{7,6},{8,9},{9,8},{10,11... | collective-permute-start | bytes 3145736 | tf_op jit(solution)/shard_map/core2/ppermute | solution.py:441
  30.5 27.8 %collective-permute-start.4 = (bf16[2,2,256,256]{3,2,1,0:T(8,128)(2,1)}, bf16[2,2,256,256]{3,2,1,0:T(8,128)(2,1)}, u32[]{:S(2)}, u32[]{:S(2)}) collective-permute-start(bf16[2,2,256,256]{3,2,1,0:T(8,128)(2,1)} %get-tuple-element.48.refs_1_), channel_id=1, source_target_pairs={{4,0},{8,4},{12,8},{16,12},{20,16},{24,20},{28,24},{5,1},{9,5},{13... | collective-permute-start | bytes 1572872 | tf_op jit(solution)/shard_map/down2/ppermute | solution.py:441
  33.0 29.6 %collective-permute-start.15 = (bf16[2,2,2,256,256]{4,3,2,1,0:T(8,128)(2,1)}, bf16[2,2,2,256,256]{4,3,2,1,0:T(8,128)(2,1)}, u32[]{:S(2)}, u32[]{:S(2)}) collective-permute-start(bf16[2,2,2,256,256]{4,3,2,1,0:T(8,128)(2,1)} %get-tuple-element.40.refs_2_.refs_0_), channel_id=1, source_target_pairs={{0,2},{1,3},{2,0},{3,1},{4,6},{5,7},{6,4},{7,5},{8,10},{9,11},{10,... | collective-permute-start | bytes 3145736 | tf_op jit(solution)/shard_map/pair3/ppermute | solution.py:441
  34.1 24.2 %collective-permute-start.3 = (bf16[2,2,256,256]{3,2,1,0:T(8,128)(2,1)}, bf16[2,2,256,256]{3,2,1,0:T(8,128)(2,1)}, u32[]{:S(2)}, u32[]{:S(2)}) collective-permute-start(bf16[2,2,256,256]{3,2,1,0:T(8,128)(2,1)} %get-tuple-element.47), channel_id=1, source_target_pairs={{0,4},{4,8},{8,12},{12,16},{16,20},{20,24},{24,28},{1,5},{5,9},{9,... | collective-permute-start | bytes 1572872 | tf_op jit(solution)/shard_map/up2/ppermute | solution.py:441
  40.1 3.0 %collective-permute-start.10 = (bf16[2,2,2,256,256]{4,3,2,1,0:T(8,128)(2,1)}, bf16[2,2,2,256,256]{4,3,2,1,0:T(8,128)(2,1)}, u32[]{:S(2)}, u32[]{:S(2)}) collective-permute-start(bf16[2,2,2,256,256]{4,3,2,1,0:T(8,128)(2,1)} %get-tuple-element.56.refs_1_.refs_2_), channel_id=1, source_target_pairs={{0,1},{1,0},{2,3},{3,2},{4,5},{5,4},{6,7},{7,6},{8,9},{9,8},{10,11... | collective-permute-start | bytes 3145736 | tf_op jit(solution)/shard_map/core_pair1/ppermute | solution.py:441
  40.1 4.5 %collective-permute-start.11 = (bf16[2,2,2,256,256]{4,3,2,1,0:T(8,128)(2,1)}, bf16[2,2,2,256,256]{4,3,2,1,0:T(8,128)(2,1)}, u32[]{:S(2)}, u32[]{:S(2)}) collective-permute-start(bf16[2,2,2,256,256]{4,3,2,1,0:T(8,128)(2,1)} %get-tuple-element.57), channel_id=1, source_target_pairs={{0,1},{1,0},{2,3},{3,2},{4,5},{5,4},{6,7},{7,6},{8,9},{9,8},{10,11... | collective-permute-start | bytes 3145736 | tf_op jit(solution)/shard_map/core3/ppermute | solution.py:441
  43.1 5.9 %collective-permute-start.7 = (bf16[2,2,256,256]{3,2,1,0:T(8,128)(2,1)}, bf16[2,2,256,256]{3,2,1,0:T(8,128)(2,1)}, u32[]{:S(2)}, u32[]{:S(2)}) collective-permute-start(bf16[2,2,256,256]{3,2,1,0:T(8,128)(2,1)} %get-tuple-element.53.refs_1_.refs_2_), channel_id=1, source_target_pairs={{0,1},{1,0},{2,3},{3,2},{4,5},{5,4},{6,7},{7,6},{8,9},{9,8},{10,11... | collective-permute-start | bytes 1572872 | tf_op jit(solution)/shard_map/core_up0/ppermute | solution.py:441
  44.6 4.9 %collective-permute-start.8 = (bf16[2,2,256,256]{3,2,1,0:T(8,128)(2,1)}, bf16[2,2,256,256]{3,2,1,0:T(8,128)(2,1)}, u32[]{:S(2)}, u32[]{:S(2)}) collective-permute-start(bf16[2,2,256,256]{3,2,1,0:T(8,128)(2,1)} %get-tuple-element.54.refs_3_), channel_id=1, source_target_pairs={{0,1},{1,0},{2,3},{3,2},{4,5},{5,4},{6,7},{7,6},{8,9},{9,8},{10,11... | collective-permute-start | bytes 1572872 | tf_op jit(solution)/shard_map/core_down0/ppermute | solution.py:441
  49.0 6.4 %collective-permute-start.12 = (f32[2,8,256]{2,1,0:T(8,128)}, f32[2,8,256]{2,1,0:T(8,128)}, u32[]{:S(2)}, u32[]{:S(2)}) collective-permute-start(f32[2,8,256]{2,1,0:T(8,128)} %get-tuple-element.61.refs_1_), channel_id=1, source_target_pairs={{0,1},{1,0},{2,3},{3,2},{4,5},{5,4},{6,7},{7,6},{8,9},{9,8},{10,11... | collective-permute-start | bytes 49160 | tf_op jit(solution)/shard_map/beat1/ppermute | solution.py:441
  53.9 32.5 %collective-permute-start.22 = (bf16[2,2,2,256,256]{4,3,2,1,0:T(8,128)(2,1)}, bf16[2,2,2,256,256]{4,3,2,1,0:T(8,128)(2,1)}, u32[]{:S(2)}, u32[]{:S(2)}) collective-permute-start(bf16[2,2,2,256,256]{4,3,2,1,0:T(8,128)(2,1)} %get-tuple-element.62.refs_1_), channel_id=1, source_target_pairs={{0,2},{1,3},{2,0},{3,1},{4,6},{5,7},{6,4},{7,5},{8,10},{9,11},{10,... | collective-permute-start | bytes 3145736 | tf_op jit(solution)/shard_map/pair0/ppermute | solution.py:441
  55.4 37.0 %collective-permute-start.20 = (bf16[2,2,256,256]{3,2,1,0:T(8,128)(2,1)}, bf16[2,2,256,256]{3,2,1,0:T(8,128)(2,1)}, u32[]{:S(2)}, u32[]{:S(2)}) collective-permute-start(bf16[2,2,256,256]{3,2,1,0:T(8,128)(2,1)} %get-tuple-element.71), channel_id=1, source_target_pairs={{0,4},{4,8},{8,12},{12,16},{16,20},{20,24},{24,28},{1,5},{5,9},{9,... | collective-permute-start | bytes 1572872 | tf_op jit(solution)/shard_map/up1/ppermute | solution.py:441
  58.3 7.5 %collective-permute-start.13 = (bf16[2,2,256,256]{3,2,1,0:T(8,128)(2,1)}, bf16[2,2,256,256]{3,2,1,0:T(8,128)(2,1)}, u32[]{:S(2)}, u32[]{:S(2)}) collective-permute-start(bf16[2,2,256,256]{3,2,1,0:T(8,128)(2,1)} %get-tuple-element.63.refs_1_.refs_2_), channel_id=1, source_target_pairs={{0,1},{1,0},{2,3},{3,2},{4,5},{5,4},{6,7},{7,6},{8,9},{9,8},{10,11... | collective-permute-start | bytes 1572872 | tf_op jit(solution)/shard_map/core_up2/ppermute | solution.py:441
  58.4 7.5 %collective-permute-start.14 = (bf16[2,2,256,256]{3,2,1,0:T(8,128)(2,1)}, bf16[2,2,256,256]{3,2,1,0:T(8,128)(2,1)}, u32[]{:S(2)}, u32[]{:S(2)}) collective-permute-start(bf16[2,2,256,256]{3,2,1,0:T(8,128)(2,1)} %get-tuple-element.64.refs_3_), channel_id=1, source_target_pairs={{0,1},{1,0},{2,3},{3,2},{4,5},{5,4},{6,7},{7,6},{8,9},{9,8},{10,11... | collective-permute-start | bytes 1572872 | tf_op jit(solution)/shard_map/core_down2/ppermute | solution.py:441
  62.5 29.8 %collective-permute-start.21 = (bf16[2,2,256,256]{3,2,1,0:T(8,128)(2,1)}, bf16[2,2,256,256]{3,2,1,0:T(8,128)(2,1)}, u32[]{:S(2)}, u32[]{:S(2)}) collective-permute-start(bf16[2,2,256,256]{3,2,1,0:T(8,128)(2,1)} %get-tuple-element.72), channel_id=1, source_target_pairs={{4,0},{8,4},{12,8},{16,12},{20,16},{24,20},{28,24},{5,1},{9,5},{13... | collective-permute-start | bytes 1572872 | tf_op jit(solution)/shard_map/down1/ppermute | solution.py:441
  65.9 6.1 %collective-permute-start.17 = (bf16[2,2,2,256,256]{4,3,2,1,0:T(8,128)(2,1)}, bf16[2,2,2,256,256]{4,3,2,1,0:T(8,128)(2,1)}, u32[]{:S(2)}, u32[]{:S(2)}) collective-permute-start(bf16[2,2,2,256,256]{4,3,2,1,0:T(8,128)(2,1)} %gate.25.refs_6_.refs_2_), channel_id=1, source_target_pairs={{0,1},{1,0},{2,3},{3,2},{4,5},{5,4},{6,7},{7,6},{8,9},{9,8},{10,11... | collective-permute-start | bytes 3145736 | tf_op jit(solution)/shard_map/core_pair3/ppermute | solution.py:441
  70.4 38.1 %collective-permute-start.16 = (bf16[2,2,2,256,256]{4,3,2,1,0:T(8,128)(2,1)}, bf16[2,2,2,256,256]{4,3,2,1,0:T(8,128)(2,1)}, u32[]{:S(2)}, u32[]{:S(2)}) collective-permute-start(bf16[2,2,2,256,256]{4,3,2,1,0:T(8,128)(2,1)} %get-tuple-element.66.refs_4_), channel_id=1, source_target_pairs={{0,2},{1,3},{2,0},{3,1},{4,6},{5,7},{6,4},{7,5},{8,10},{9,11},{10,... | collective-permute-start | bytes 3145736 | tf_op jit(solution)/shard_map/pair2/ppermute | solution.py:441
  76.3 29.8 %collective-permute-start.19 = (bf16[2,2,256,256]{3,2,1,0:T(8,128)(2,1)}, bf16[2,2,256,256]{3,2,1,0:T(8,128)(2,1)}, u32[]{:S(2)}, u32[]{:S(2)}) collective-permute-start(bf16[2,2,256,256]{3,2,1,0:T(8,128)(2,1)} %get-tuple-element.67.refs_4_), channel_id=1, source_target_pairs={{4,0},{8,4},{12,8},{16,12},{20,16},{24,20},{28,24},{5,1},{9,5},{13... | collective-permute-start | bytes 1572872 | tf_op jit(solution)/shard_map/down3/ppermute | solution.py:441
  80.6 27.9 %all-to-all-start = ((f32[32,1,128]{2,1,0:T(1,128)}), f32[32,1,128]{2,1,0:T(1,128)}, u32[]{:S(2)}, u32[]{:S(2)}) async-start(f32[32,1,128]{2,1,0:T(1,128)} %range_parts.1.refs_1_), calls=%async_computation | async-start | bytes 32768 | tf_op jit(solution)/shard_map/all_to_all | solution.py:523
  86.4 17.2 %collective-permute-start.18 = (bf16[2,2,256,256]{3,2,1,0:T(8,128)(2,1)}, bf16[2,2,256,256]{3,2,1,0:T(8,128)(2,1)}, u32[]{:S(2)}, u32[]{:S(2)}) collective-permute-start(bf16[2,2,256,256]{3,2,1,0:T(8,128)(2,1)} %get-tuple-element.69), channel_id=1, source_target_pairs={{0,4},{4,8},{8,12},{12,16},{16,20},{20,24},{24,28},{1,5},{5,9},{9,... | collective-permute-start | bytes 1572872 | tf_op jit(solution)/shard_map/up3/ppermute | solution.py:441

commit v5 on v4

--- a/solution.py
+++ b/solution.py
@@ -60,6 +60,7 @@
     energies = a_ref.shape[1]
     width = a_ref.shape[-1]
     t = (t_ref[0, 0], t_ref[1, 0])
+    odd = lax.rem(lax.axis_index("energy"), 2)
     if not first:
 
         @pl.when(pl.program_id(0) == 0)
@@ -102,12 +103,13 @@
         if again:
             again_ref[0, 0, e] = re
             again_ref[0, 1, e] = im
-        if edges and e == 0:
-            low_ref[0, 0] = re
-            low_ref[0, 1] = im
-        if edges and e == energies - 1:
-            high_ref[0, 0] = re
-            high_ref[0, 1] = im
+        for low in [edge for edge, at in ((True, 0), (False, energies - 1)) if edges and e == at]:
+            for parity, target in ((1, low_ref if low else high_ref), (0, high_ref if low else low_ref)):
+
+                @pl.when(odd == parity)
+                def _(target=target, re=re, im=im):
+                    target[0, 0] = re
+                    target[0, 1] = im
         diagonal = jnp.where(rows == columns, im.astype(F32), 0.0)
         total = total + jnp.sum(diagonal.reshape(width // 8, 8, width), axis=0)
     density_ref[0] = total
@@ -207,6 +209,7 @@
 def early_edges_kernel(w_ref, *refs):
     grids, (high_ref, low_ref, local_ref) = refs[:4], refs[-3:]
     energies, width = grids[0].shape[2:4]
+    odd = lax.rem(lax.axis_index("energy"), 2) == 1
     w = [[w_ref[0, o, j] for j in range(4)] for o in range(3)]
 
     @tiles(width)
@@ -216,8 +219,9 @@
         ]
         high = [(w[0][j], line[j][energies - 1]) for j in range(4)]
         low = [(w[2][j], line[j][0]) for j in range(4)]
-        high_ref[0, part, rows, :] = weighted(high).astype(BF16)
-        low_ref[0, part, rows, :] = weighted(low).astype(BF16)
+        high, low = weighted(high), weighted(low)
+        high_ref[0, part, rows, :] = jnp.where(odd, high, low).astype(BF16)
+        low_ref[0, part, rows, :] = jnp.where(odd, low, high).astype(BF16)
         for e in range(energies):
             terms = [
                 (w[o][j], line[j][e + o - 1])
@@ -247,11 +251,16 @@
 def late_line(refs, part, rows):
     grids, edges = refs[:2], refs[2:]
     lines = []
+    odd = lax.rem(lax.axis_index("energy"), 2) == 1
     for j in range(2):
-        line = [edges[2 * j][0, part, rows, :]]
-        line += [grids[j][0, part, e, rows, :] for e in range(grids[j].shape[2])]
-        line += [edges[2 * j + 1][0, part, rows, :]]
-        lines.append([value.astype(F32) for value in line])
+        near = edges[2 * j + 1][0, part, rows, :].astype(F32)
+        far = edges[2 * j][0, part, rows, :].astype(F32)
+        line = [jnp.where(odd, near, far)]
+        line += [
+            grids[j][0, part, e, rows, :].astype(F32) for e in range(grids[j].shape[2])
+        ]
+        line += [jnp.where(odd, far, near)]
+        lines.append(line)
     return lines
 
 
@@ -300,19 +309,23 @@
     energies, width = local_ref.shape[2:4]
     across = across_ref[0]
     lanes = down_ref.shape[1]
+    odd = lax.rem(lax.axis_index("energy"), 2) == 1
     down_ref[...] = jnp.transpose(jnp.broadcast_to(across, (lanes, width)))
 
     @tiles(width)
     def _(part, rows):
+        if not late:
+            far, near = [ref[0, part, rows, :].astype(F32) for ref in received]
+            before, behind = jnp.where(odd, near, far), jnp.where(odd, far, near)
         scale = jnp.concatenate([down_ref[rows, :]] * (width // lanes), axis=1) * across
         for e in range(energies):
             total = local_ref[0, part, e, rows, :].astype(F32)
             if late:
                 total = total + received[0][0, part, e, rows, :].astype(F32)
             if not late and e == 0:
-                total = total + received[0][0, part, rows, :].astype(F32)
+                total = total + before
             if not late and e == energies - 1:
-                total = total + received[1][0, part, rows, :].astype(F32)
+                total = total + behind
             out_ref[part, e, 0, rows, :] = (total * scale).astype(BF16)
 
 
@@ -433,8 +446,9 @@
 ):
     n_energy = lax.axis_size("energy")
     width = inverse_blocks.shape[-1]
-    up = [(i, i + 1) for i in range(n_energy - 1)]
-    down = [(i + 1, i) for i in range(n_energy - 1)]
+    between = [(i, i + 1) for i in range(1, n_energy - 1, 2)]
+    up = between + [(j, i) for i, j in between]
+    down = [(i, i ^ 1) for i in range(n_energy)]
 
     def send(value, axis, pairs, name):
         with jax.named_scope(name):
@@ -475,17 +489,17 @@
         )
 
     g0, n0, low0, high0 = run(0, None)
-    up0, c0 = rise(high0, "0"), core(g0, "core0")
+    down0, c0 = fall(low0, "0"), core(g0, "core0")
     g1, n1 = run(1, g0, (c0,))
     y1, c1 = pair(g1, "pair1"), core(g1, "core1")
-    (low0,) = gate([low0], (g1,))
-    down0 = fall(low0, "0")
+    (high0,) = gate([high0], (g1,))
+    up0 = rise(high0, "0")
     g3, n3, h3 = run(3, g1, (c1,), True)
     y3 = pair(g3, "pair3")
     g2, n2, low2, high2, h2 = run(2, g3, (), True)
     weights = own_weights(shifts, emission_weight, absorption_weight, (n2,))
 
-    low2, high2, h2 = gate([low2, high2, h2], (weights,))
+    low2, high2, h2 = gate([low2, high2, h2], (n2,))
     up2, down2, c2 = rise(high2, "2"), fall(low2, "2"), core(h2, "core2")
     (n0,) = gate([n0], (low2,))
 

time: 112 us -> 112 us (level)
  starting transfers between devices: 37.9 us -> 31.1 us
  waiting for transfers between devices: 21.5 us -> 27.1 us
  Pallas kernels: 50.9 us -> 52.4 us
    ppermute x23, starting transfers between devices: 32 us -> 26.1 us  [send(): return lax.ppermute(value, axis, pairs)]
    ppermute x23, waiting for transfers between devices: 21.5 us -> 27.1 us  [send(): return lax.ppermute(value, axis, pairs)]
  transfers between devices with their start and end apart: 24 -> 24, of which waited for: 7 -> 8; matrix products, arithmetic and copies ran while one was open for 0% -> 0% of each run, Pallas kernels for 39% -> 40%
where the time goes in v5:
time: 112 us; the launch traced here: 111 us
  Pallas kernels  52.4 us (47%)
  starting transfers between devices  31.1 us (28%)
  waiting for transfers between devices  27.1 us (24%)
    ppermute x23, waiting for transfers between devices, send(): return lax.ppermute(value, axis, pairs)  27.1 us
    ppermute x23, starting transfers between devices, send(): return lax.ppermute(value, axis, pairs)  26.1 us
    pallas_call x4, Pallas kernels, solve(): pl.pallas_call(functools.partial(solve_kernel, first, edges, again), grid...  20.4 us
    pallas_call x4, Pallas kernels, finish(): pl.pallas_call(functools.partial(finish_kernel, late, parts is not None),...  10.2 us
    pallas_call x2, Pallas kernels, late_sum(): pl.pallas_call(late_sum_kernel, grid=(count,), in_specs=[pl.BlockSpec(mem...  9.26 us
    pallas_call x2, Pallas kernels, early_edges(): pl.pallas_call(early_edges_kernel, grid=(count,), in_specs=[pl.BlockSpec(...  8.85 us
    all_to_all x1, starting transfers between devices, body(): lax.all_to_all(parts, ('energy', 'mom'), split_axis=0, concat_axis=0, til...  4.93 us
  transfers between devices with their start and end apart: 24, of which 8 were waited for; matrix products, arithmetic and copies ran while one was open for 0% of the time, Pallas kernels for 40%

profile of v5, /device:TPU:24, one launch (start us, length us, event | category | flops | bytes accessed | tf_op | source)
XLA Modules:
  0.0 111.4 jit_solution(16596684679914199073)
XLA Ops:
  0.6 5.2 %solve.4 = (bf16[2,2,2,256,256]{4,3,2,1,0:T(8,128)(2,1)}, f32[2,8,256]{2,1,0:T(8,128)}, bf16[2,2,256,256]{3,2,1,0:T(8,128)(2,1)}, bf16[2,2,256,256]{3,2,1,0:T(8,128)(2,1)}) custom-call(bf16[2,2,1,2048,256]{4,3,2,1,0:T(8,128)(2,1)} %refs_0_.7, bf16[2,1,2048,256]{3,2,1,0:T(8,128)(2,1)} %refs_1_.7), custom_call_target="tpu_custom_call" | custom-call | flops 575000018944 | tf_op jit(solution)/shard_map/solve/pallas_call | solution.py:149
  5.9 0.0 collective-permute-start
  5.9 1.5 %collective-permute-start.6 = (bf16[2,2,256,256]{3,2,1,0:T(8,128)(2,1)}, bf16[2,2,256,256]{3,2,1,0:T(8,128)(2,1)}, u32[]{:S(2)}, u32[]{:S(2)}) collective-permute-start(bf16[2,2,256,256]{3,2,1,0:T(8,128)(2,1)} %get-tuple-element.51), channel_id=1, source_target_pairs={{0,4},{4,0},{8,12},{12,8},{16,20},{20,16},{24,28},{28,24},{1,5},{5... | collective-permute-start | bytes 1572872 | tf_op jit(solution)/shard_map/down0/ppermute | solution.py:455
  7.4 1.5 %collective-permute-done.refs_3_.refs_0_ = bf16[2,2,2,256,256]{4,3,2,1,0:T(8,128)(2,1)} collective-permute-done((bf16[2,2,2,256,256]{4,3,2,1,0:T(8,128)(2,1)}, bf16[2,2,2,256,256]{4,3,2,1,0:T(8,128)(2,1)}, u32[]{:S(2)}, u32[]{:S(2)}) %collective-permute-start) | collective-permute-done | bytes 1048608 | tf_op jit(solution)/shard_map/core0/ppermute | solution.py:455
  8.9 4.7 %solve.5 = (bf16[2,2,2,256,256]{4,3,2,1,0:T(8,128)(2,1)}, f32[2,8,256]{2,1,0:T(8,128)}) custom-call(bf16[2,2,1,2048,256]{4,3,2,1,0:T(8,128)(2,1)} %refs_0_.7, bf16[2,1,2048,256]{3,2,1,0:T(8,128)(2,1)} %refs_1_.7, bf16[2,2,2,256,256]{4,3,2,1,0:T(8,128)(2,1)} %get-tuple-element.38.refs_2_.refs_0_, bf16[2,2,2,256,256]{4,3,2,1,0:T(8,128)(2,1)} %collective-permute-done.refs_3_.refs_0_), custom_call_target="tpu_custom_call" | custom-call | flops 575000018944 | tf_op jit(solution)/shard_map/solve/pallas_call | solution.py:149
  13.6 0.1 collective-permute-start.1
  13.7 1.5 %collective-permute-start.9 = (bf16[2,2,2,256,256]{4,3,2,1,0:T(8,128)(2,1)}, bf16[2,2,2,256,256]{4,3,2,1,0:T(8,128)(2,1)}, u32[]{:S(2)}, u32[]{:S(2)}) collective-permute-start(bf16[2,2,2,256,256]{4,3,2,1,0:T(8,128)(2,1)} %get-tuple-element.39.refs_2_.refs_1_.refs_0_), channel_id=1, source_target_pairs={{0,2},{1,3},{2,0},{3,1},{4,6},{5,7},{6,4},{7,5},{8,10},{9,11},{10,... | collective-permute-start | bytes 3145736 | tf_op jit(solution)/shard_map/pair1/ppermute | solution.py:455
  15.2 3.2 %collective-permute-start.5 = (bf16[2,2,256,256]{3,2,1,0:T(8,128)(2,1)}, bf16[2,2,256,256]{3,2,1,0:T(8,128)(2,1)}, u32[]{:S(2)}, u32[]{:S(2)}) collective-permute-start(bf16[2,2,256,256]{3,2,1,0:T(8,128)(2,1)} %gate.14), channel_id=1, source_target_pairs={{4,8},{12,16},{20,24},{8,4},{16,12},{24,20},{5,9},{13,17},{21,25},... | collective-permute-start | bytes 1572872 | tf_op jit(solution)/shard_map/up0/ppermute | solution.py:455
  18.5 0.0 collective-permute-done.1.refs_3_.refs_0_
  18.5 4.9 %solve.6 = (bf16[2,2,2,256,256]{4,3,2,1,0:T(8,128)(2,1)}, f32[2,8,256]{2,1,0:T(8,128)}, bf16[2,2,2,256,256]{4,3,2,1,0:T(8,128)(2,1)}) custom-call(bf16[2,2,1,2048,256]{4,3,2,1,0:T(8,128)(2,1)} %refs_0_.7, bf16[2,1,2048,256]{3,2,1,0:T(8,128)(2,1)} %refs_1_.7, bf16[2,2,2,256,256]{4,3,2,1,0:T(8,128)(2,1)} %get-tuple-element.39.refs_2_.refs_1_.refs_0_, ...), custom_call_target="tpu_custom_call" | custom-call | flops 575000018944 | tf_op jit(solution)/shard_map/solve/pallas_call | solution.py:149
  23.4 5.5 %solve.7 = (bf16[2,2,2,256,256]{4,3,2,1,0:T(8,128)(2,1)}, f32[2,8,256]{2,1,0:T(8,128)}, bf16[2,2,256,256]{3,2,1,0:T(8,128)(2,1)}, bf16[2,2,256,256]{3,2,1,0:T(8,128)(2,1)}, bf16[2,2,2,256,256]{4,3,2,1,0:T(8,128)(2,1)}) custom-call(bf16[2,2,1,2048,256]{4,3,2,1,0:T(8,128)(2,1)} %refs_0_.7, bf16[2,1,2048,256]{3,2,1,0:T(8,128)(2,1)} %refs_1_.7, ...), custom_call_target="tpu_custom_call" | custom-call | flops 575000018944 | tf_op jit(solution)/shard_map/solve/pallas_call | solution.py:149
  28.9 0.1 collective-permute-start.4
  29.0 0.1 collective-permute-start.2
  29.1 1.7 %own_weights.1.w_ref = f32[2,3,4]{2,1,0:T(4,128)} custom-call(s32[4]{0:T(128)} %shift_ref.1, f32[4,4,4]{2,1,0:T(4,128)} %emission_ref.1, f32[4,4,4]{2,1,0:T(4,128)} %absorption_ref.1, f32[2,8,256]{2,1,0:T(8,128)} %get-tuple-element.41.refs_0_.refs_3_), custom_call_target="tpu_custom_call" | custom-call | flops 57500000256 | tf_op jit(solution)/shard_map/own_weights/pallas_call | solution.py:427
  30.9 0.0 collective-permute-done.6.refs_1_
  30.9 2.8 %collective-permute-start.15 = (bf16[2,2,2,256,256]{4,3,2,1,0:T(8,128)(2,1)}, bf16[2,2,2,256,256]{4,3,2,1,0:T(8,128)(2,1)}, u32[]{:S(2)}, u32[]{:S(2)}) collective-permute-start(bf16[2,2,2,256,256]{4,3,2,1,0:T(8,128)(2,1)} %get-tuple-element.40.refs_2_.refs_0_), channel_id=1, source_target_pairs={{0,2},{1,3},{2,0},{3,1},{4,6},{5,7},{6,4},{7,5},{8,10},{9,11},{10,... | collective-permute-start | bytes 3145736 | tf_op jit(solution)/shard_map/pair3/ppermute | solution.py:455
  33.7 0.0 collective-permute-done.5.refs_0_
  33.7 3.2 %collective-permute-start.3 = (bf16[2,2,256,256]{3,2,1,0:T(8,128)(2,1)}, bf16[2,2,256,256]{3,2,1,0:T(8,128)(2,1)}, u32[]{:S(2)}, u32[]{:S(2)}) collective-permute-start(bf16[2,2,256,256]{3,2,1,0:T(8,128)(2,1)} %get-tuple-element.47), channel_id=1, source_target_pairs={{4,8},{12,16},{20,24},{8,4},{16,12},{24,20},{5,9},{13,17},{21,25},... | collective-permute-start | bytes 1572872 | tf_op jit(solution)/shard_map/up2/ppermute | solution.py:455
  36.9 0.0 collective-permute-done.2.refs_3_.refs_0_
  36.9 3.1 %collective-permute-done.9.refs_0_ = bf16[2,2,2,256,256]{4,3,2,1,0:T(8,128)(2,1)} collective-permute-done((bf16[2,2,2,256,256]{4,3,2,1,0:T(8,128)(2,1)}, bf16[2,2,2,256,256]{4,3,2,1,0:T(8,128)(2,1)}, u32[]{:S(2)}, u32[]{:S(2)}) %collective-permute-start.9) | collective-permute-done | bytes 1048608 | tf_op jit(solution)/shard_map/pair1/ppermute | solution.py:455
  40.0 0.0 collective-permute-start.10
  40.0 0.5 collective-permute-start.11
  40.5 2.5 %collective-permute-done.10.refs_3_ = bf16[2,2,2,256,256]{4,3,2,1,0:T(8,128)(2,1)} collective-permute-done((bf16[2,2,2,256,256]{4,3,2,1,0:T(8,128)(2,1)}, bf16[2,2,2,256,256]{4,3,2,1,0:T(8,128)(2,1)}, u32[]{:S(2)}, u32[]{:S(2)}) %collective-permute-start.10) | collective-permute-done | bytes 1048608 | tf_op jit(solution)/shard_map/core_pair1/ppermute | solution.py:455
  43.0 0.1 collective-permute-start.7
  43.1 1.4 %collective-permute-done.11.refs_4_.refs_1_ = bf16[2,2,2,256,256]{4,3,2,1,0:T(8,128)(2,1)} collective-permute-done((bf16[2,2,2,256,256]{4,3,2,1,0:T(8,128)(2,1)}, bf16[2,2,2,256,256]{4,3,2,1,0:T(8,128)(2,1)}, u32[]{:S(2)}, u32[]{:S(2)}) %collective-permute-start.11) | collective-permute-done | bytes 1048608 | tf_op jit(solution)/shard_map/core3/ppermute | solution.py:455
  44.5 0.1 collective-permute-start.8
  44.6 4.4 %early_edges.2 = (bf16[2,2,256,256]{3,2,1,0:T(8,128)(2,1)}, bf16[2,2,256,256]{3,2,1,0:T(8,128)(2,1)}, bf16[2,2,2,256,256]{4,3,2,1,0:T(8,128)(2,1)}) custom-call(f32[2,3,4]{2,1,0:T(4,128)} %own_weights.1.w_ref, bf16[2,2,2,256,256]{4,3,2,1,0:T(8,128)(2,1)} %get-tuple-element.39.refs_2_.refs_1_.refs_0_, bf16[2,2,2,256,256]{4,3,2,1,0:T(8,128)(2,1)} %gate.19.refs_1_, ...), custom_call_target="tpu_custom_call" | custom-call | flops 390999998464 | tf_op jit(solution)/shard_map/early_edges/pallas_call | solution.py:239
  49.1 0.0 collective-permute-done.7.refs_4_
  49.1 0.4 collective-permute-start.12
  49.5 0.0 collective-permute-done.8.refs_5_
  49.5 4.6 %late_sum.2 = (bf16[2,2,2,256,256]{4,3,2,1,0:T(8,128)(2,1)}, bf16[2,2,2,256,256]{4,3,2,1,0:T(8,128)(2,1)}) custom-call(f32[2,3,4]{2,1,0:T(4,128)} %own_weights.1.w_ref, bf16[2,2,2,256,256]{4,3,2,1,0:T(8,128)(2,1)} %get-tuple-element.38.refs_2_.refs_0_, bf16[2,2,2,256,256]{4,3,2,1,0:T(8,128)(2,1)} %gate.17.refs_2_.refs_1_, ...), custom_call_target="tpu_custom_call" | custom-call | flops 413999988736 | tf_op jit(solution)/shard_map/late_sum/pallas_call | solution.py:284
  54.1 1.5 %collective-permute-start.22 = (bf16[2,2,2,256,256]{4,3,2,1,0:T(8,128)(2,1)}, bf16[2,2,2,256,256]{4,3,2,1,0:T(8,128)(2,1)}, u32[]{:S(2)}, u32[]{:S(2)}) collective-permute-start(bf16[2,2,2,256,256]{4,3,2,1,0:T(8,128)(2,1)} %get-tuple-element.62.refs_1_), channel_id=1, source_target_pairs={{0,2},{1,3},{2,0},{3,1},{4,6},{5,7},{6,4},{7,5},{8,10},{9,11},{10,... | collective-permute-start | bytes 3145736 | tf_op jit(solution)/shard_map/pair0/ppermute | solution.py:455
  55.7 0.0 collective-permute-done.12.refs_2_
  55.7 3.4 %collective-permute-start.20 = (bf16[2,2,256,256]{3,2,1,0:T(8,128)(2,1)}, bf16[2,2,256,256]{3,2,1,0:T(8,128)(2,1)}, u32[]{:S(2)}, u32[]{:S(2)}) collective-permute-start(bf16[2,2,256,256]{3,2,1,0:T(8,128)(2,1)} %get-tuple-element.71), channel_id=1, source_target_pairs={{4,8},{12,16},{20,24},{8,4},{16,12},{24,20},{5,9},{13,17},{21,25},... | collective-permute-start | bytes 1572872 | tf_op jit(solution)/shard_map/up1/ppermute | solution.py:455
  59.1 0.0 collective-permute-done.3.refs_0_
  59.1 0.0 collective-permute-done.4.refs_1_
  59.1 0.1 collective-permute-start.13
  59.2 0.5 collective-permute-start.14
  59.7 2.8 %collective-permute-done.15.refs_0_ = bf16[2,2,2,256,256]{4,3,2,1,0:T(8,128)(2,1)} collective-permute-done((bf16[2,2,2,256,256]{4,3,2,1,0:T(8,128)(2,1)}, bf16[2,2,2,256,256]{4,3,2,1,0:T(8,128)(2,1)}, u32[]{:S(2)}, u32[]{:S(2)}) %collective-permute-start.15) | collective-permute-done | bytes 1048608 | tf_op jit(solution)/shard_map/pair3/ppermute | solution.py:455
  62.5 1.5 %collective-permute-start.21 = (bf16[2,2,256,256]{3,2,1,0:T(8,128)(2,1)}, bf16[2,2,256,256]{3,2,1,0:T(8,128)(2,1)}, u32[]{:S(2)}, u32[]{:S(2)}) collective-permute-start(bf16[2,2,256,256]{3,2,1,0:T(8,128)(2,1)} %get-tuple-element.72), channel_id=1, source_target_pairs={{0,4},{4,0},{8,12},{12,8},{16,20},{20,16},{24,28},{28,24},{1,5},{5... | collective-permute-start | bytes 1572872 | tf_op jit(solution)/shard_map/down1/ppermute | solution.py:455
  63.9 0.0 collective-permute-done.13.refs_2_.refs_4_
  63.9 0.0 collective-permute-done.14.refs_3_.refs_5_
  63.9 0.0 collective-permute-start.17
  63.9 4.6 %late_sum.3 = (bf16[2,2,2,256,256]{4,3,2,1,0:T(8,128)(2,1)}, bf16[2,2,2,256,256]{4,3,2,1,0:T(8,128)(2,1)}) custom-call(f32[2,3,4]{2,1,0:T(4,128)} %own_weights.1.w_ref, bf16[2,2,2,256,256]{4,3,2,1,0:T(8,128)(2,1)} %get-tuple-element.42.refs_0_, bf16[2,2,2,256,256]{4,3,2,1,0:T(8,128)(2,1)} %gate.24.refs_1_, ...), custom_call_target="tpu_custom_call" | custom-call | flops 413999988736 | tf_op jit(solution)/shard_map/late_sum/pallas_call | solution.py:284
  68.6 1.5 %collective-permute-start.16 = (bf16[2,2,2,256,256]{4,3,2,1,0:T(8,128)(2,1)}, bf16[2,2,2,256,256]{4,3,2,1,0:T(8,128)(2,1)}, u32[]{:S(2)}, u32[]{:S(2)}) collective-permute-start(bf16[2,2,2,256,256]{4,3,2,1,0:T(8,128)(2,1)} %get-tuple-element.66.refs_4_), channel_id=1, source_target_pairs={{0,2},{1,3},{2,0},{3,1},{4,6},{5,7},{6,4},{7,5},{8,10},{9,11},{10,... | collective-permute-start | bytes 3145736 | tf_op jit(solution)/shard_map/pair2/ppermute | solution.py:455
  70.1 0.0 collective-permute-done.17.refs_3_
  70.1 4.4 %early_edges.3 = (bf16[2,2,256,256]{3,2,1,0:T(8,128)(2,1)}, bf16[2,2,256,256]{3,2,1,0:T(8,128)(2,1)}, bf16[2,2,2,256,256]{4,3,2,1,0:T(8,128)(2,1)}) custom-call(f32[2,3,4]{2,1,0:T(4,128)} %own_weights.1.w_ref, bf16[2,2,2,256,256]{4,3,2,1,0:T(8,128)(2,1)} %get-tuple-element.40.refs_2_.refs_0_, ...), custom_call_target="tpu_custom_call" | custom-call | flops 390999998464 | tf_op jit(solution)/shard_map/early_edges/pallas_call | solution.py:239
  74.5 0.6 collective-permute-start.19
  75.1 1.9 %range_parts.1.refs_1_ = f32[32,1,128]{2,1,0:T(1,128)} custom-call(s32[32]{0:T(128)} %range_ref.1, f32[2,8,256]{2,1,0:T(8,128)} %gate.15.refs_2_.refs_0_, f32[2,8,256]{2,1,0:T(8,128)} %get-tuple-element.61.refs_1_, f32[2,8,256]{2,1,0:T(8,128)} %gate.22.refs_2_, f32[2,8,256]{2,1,0:T(8,128)} %gate.21.refs_6_.refs_3_, ...), custom_call_target="tpu_custom_call" | custom-call | flops 253000007680 | tf_op jit(solution)/shard_map/range_parts/pallas_call | solution.py:396
  77.1 4.9 %all-to-all-start = ((f32[32,1,128]{2,1,0:T(1,128)}), f32[32,1,128]{2,1,0:T(1,128)}, u32[]{:S(2)}, u32[]{:S(2)}) async-start(f32[32,1,128]{2,1,0:T(1,128)} %range_parts.1.refs_1_), calls=%async_computation | async-start | bytes 32768 | tf_op jit(solution)/shard_map/all_to_all | solution.py:537
  82.0 3.0 %collective-permute-done.22.refs_0_ = bf16[2,2,2,256,256]{4,3,2,1,0:T(8,128)(2,1)} collective-permute-done((bf16[2,2,2,256,256]{4,3,2,1,0:T(8,128)(2,1)}, bf16[2,2,2,256,256]{4,3,2,1,0:T(8,128)(2,1)}, u32[]{:S(2)}, u32[]{:S(2)}) %collective-permute-start.22) | collective-permute-done | bytes 1048608 | tf_op jit(solution)/shard_map/pair0/ppermute | solution.py:455
  85.0 3.3 %collective-permute-start.18 = (bf16[2,2,256,256]{3,2,1,0:T(8,128)(2,1)}, bf16[2,2,256,256]{3,2,1,0:T(8,128)(2,1)}, u32[]{:S(2)}, u32[]{:S(2)}) collective-permute-start(bf16[2,2,256,256]{3,2,1,0:T(8,128)(2,1)} %get-tuple-element.69), channel_id=1, source_target_pairs={{4,8},{12,16},{20,24},{8,4},{16,12},{24,20},{5,9},{13,17},{21,25},... | collective-permute-start | bytes 1572872 | tf_op jit(solution)/shard_map/up3/ppermute | solution.py:455
  88.2 2.5 %finish.4.refs_2_ = bf16[2,2,1,2048,256]{4,3,2,1,0:T(8,128)(2,1)} custom-call(f32[8,1,256]{2,1,0:T(1,128)} %bitcast.1, bf16[2,2,2,256,256]{4,3,2,1,0:T(8,128)(2,1)} %get-tuple-element.73.local_ref, bf16[2,2,2,256,256]{4,3,2,1,0:T(8,128)(2,1)} %collective-permute-done.22.refs_0_, f32[32,1,128]{2,1,0:T(1,128)} %range_parts.1.refs_1_), custom_call_target="tpu_custom_call" | custom-call | flops 506000015360 | tf_op jit(solution)/shard_map/finish/pallas_call | solution.py:356
  90.8 0.0 collective-permute-done.20.refs_0_
  90.8 0.0 collective-permute-done.21.refs_1_
  90.8 2.6 %finish.5.refs_2_ = bf16[2,2,1,2048,256]{4,3,2,1,0:T(8,128)(2,1)} custom-call(f32[8,1,256]{2,1,0:T(1,128)} %bitcast.2, bf16[2,2,2,256,256]{4,3,2,1,0:T(8,128)(2,1)} %get-tuple-element.70.local_ref, bf16[2,2,256,256]{3,2,1,0:T(8,128)(2,1)} %collective-permute-done.20.refs_0_, ...), custom_call_target="tpu_custom_call", output_to_operand_aliasing={{}: (4, {})} | custom-call | flops 506000015360 | tf_op jit(solution)/shard_map/finish/pallas_call | solution.py:356
  93.4 7.6 %collective-permute-done.18.refs_0_ = bf16[2,2,256,256]{3,2,1,0:T(8,128)(2,1)} collective-permute-done((bf16[2,2,256,256]{3,2,1,0:T(8,128)(2,1)}, bf16[2,2,256,256]{3,2,1,0:T(8,128)(2,1)}, u32[]{:S(2)}, u32[]{:S(2)}) %collective-permute-start.18) | collective-permute-done | bytes 524320 | tf_op jit(solution)/shard_map/up3/ppermute | solution.py:455
  101.0 5.3 %collective-permute-done.19.refs_1_ = bf16[2,2,256,256]{3,2,1,0:T(8,128)(2,1)} collective-permute-done((bf16[2,2,256,256]{3,2,1,0:T(8,128)(2,1)}, bf16[2,2,256,256]{3,2,1,0:T(8,128)(2,1)}, u32[]{:S(2)}, u32[]{:S(2)}) %collective-permute-start.19) | collective-permute-done | bytes 524320 | tf_op jit(solution)/shard_map/down3/ppermute | solution.py:455
  106.3 2.6 %finish.6.refs_2_ = bf16[2,2,1,2048,256]{4,3,2,1,0:T(8,128)(2,1)} custom-call(f32[8,1,256]{2,1,0:T(1,128)} %bitcast.3, bf16[2,2,2,256,256]{4,3,2,1,0:T(8,128)(2,1)} %get-tuple-element.68.local_ref, bf16[2,2,256,256]{3,2,1,0:T(8,128)(2,1)} %collective-permute-done.18.refs_0_, ...), custom_call_target="tpu_custom_call", output_to_operand_aliasing={{}: (4, {})} | custom-call | flops 506000015360 | tf_op jit(solution)/shard_map/finish/pallas_call | solution.py:356
  108.9 0.0 collective-permute-done.16.refs_0_
  108.9 0.0 all-to-all-done.refs_1_
  108.9 2.6 %finish.7 = (bf16[2,2,1,2048,256]{4,3,2,1,0:T(8,128)(2,1)}, f32[1]{0:T(128)}) custom-call(f32[8,1,256]{2,1,0:T(1,128)} %bitcast.4, bf16[2,2,2,256,256]{4,3,2,1,0:T(8,128)(2,1)} %get-tuple-element.65.local_ref, bf16[2,2,2,256,256]{4,3,2,1,0:T(8,128)(2,1)} %collective-permute-done.16.refs_0_, ...), custom_call_target="tpu_custom_call", output_to_operand_aliasing={{0}: (4, {})} | custom-call | flops 506000015360 | tf_op jit(solution)/shard_map/finish/pallas_call | solution.py:356
  (13 shorter events, 0.0 us)
Async XLA Ops:
  5.9 3.0 %collective-permute-start = (bf16[2,2,2,256,256]{4,3,2,1,0:T(8,128)(2,1)}, bf16[2,2,2,256,256]{4,3,2,1,0:T(8,128)(2,1)}, u32[]{:S(2)}, u32[]{:S(2)}) collective-permute-start(bf16[2,2,2,256,256]{4,3,2,1,0:T(8,128)(2,1)} %get-tuple-element.38.refs_2_.refs_0_), channel_id=1, source_target_pairs={{0,1},{1,0},{2,3},{3,2},{4,5},{5,4},{6,7},{7,6},{8,9},{9,8},{10,11... | collective-permute-start | bytes 3145736 | tf_op jit(solution)/shard_map/core0/ppermute | solution.py:455
  5.9 25.0 %collective-permute-start.6 = (bf16[2,2,256,256]{3,2,1,0:T(8,128)(2,1)}, bf16[2,2,256,256]{3,2,1,0:T(8,128)(2,1)}, u32[]{:S(2)}, u32[]{:S(2)}) collective-permute-start(bf16[2,2,256,256]{3,2,1,0:T(8,128)(2,1)} %get-tuple-element.51), channel_id=1, source_target_pairs={{0,4},{4,0},{8,12},{12,8},{16,20},{20,16},{24,28},{28,24},{1,5},{5... | collective-permute-start | bytes 1572872 | tf_op jit(solution)/shard_map/down0/ppermute | solution.py:455
  13.6 4.9 %collective-permute-start.1 = (bf16[2,2,2,256,256]{4,3,2,1,0:T(8,128)(2,1)}, bf16[2,2,2,256,256]{4,3,2,1,0:T(8,128)(2,1)}, u32[]{:S(2)}, u32[]{:S(2)}) collective-permute-start(bf16[2,2,2,256,256]{4,3,2,1,0:T(8,128)(2,1)} %get-tuple-element.39.refs_2_.refs_1_.refs_0_), channel_id=1, source_target_pairs={{0,1},{1,0},{2,3},{3,2},{4,5},{5,4},{6,7},{7,6},{8,9},{9,8},{10,11... | collective-permute-start | bytes 3145736 | tf_op jit(solution)/shard_map/core1/ppermute | solution.py:455
  13.7 26.3 %collective-permute-start.9 = (bf16[2,2,2,256,256]{4,3,2,1,0:T(8,128)(2,1)}, bf16[2,2,2,256,256]{4,3,2,1,0:T(8,128)(2,1)}, u32[]{:S(2)}, u32[]{:S(2)}) collective-permute-start(bf16[2,2,2,256,256]{4,3,2,1,0:T(8,128)(2,1)} %get-tuple-element.39.refs_2_.refs_1_.refs_0_), channel_id=1, source_target_pairs={{0,2},{1,3},{2,0},{3,1},{4,6},{5,7},{6,4},{7,5},{8,10},{9,11},{10,... | collective-permute-start | bytes 3145736 | tf_op jit(solution)/shard_map/pair1/ppermute | solution.py:455
  15.2 18.4 %collective-permute-start.5 = (bf16[2,2,256,256]{3,2,1,0:T(8,128)(2,1)}, bf16[2,2,256,256]{3,2,1,0:T(8,128)(2,1)}, u32[]{:S(2)}, u32[]{:S(2)}) collective-permute-start(bf16[2,2,256,256]{3,2,1,0:T(8,128)(2,1)} %gate.14), channel_id=1, source_target_pairs={{4,8},{12,16},{20,24},{8,4},{16,12},{24,20},{5,9},{13,17},{21,25},... | collective-permute-start | bytes 1572872 | tf_op jit(solution)/shard_map/up0/ppermute | solution.py:455
  28.9 30.2 %collective-permute-start.4 = (bf16[2,2,256,256]{3,2,1,0:T(8,128)(2,1)}, bf16[2,2,256,256]{3,2,1,0:T(8,128)(2,1)}, u32[]{:S(2)}, u32[]{:S(2)}) collective-permute-start(bf16[2,2,256,256]{3,2,1,0:T(8,128)(2,1)} %get-tuple-element.48.refs_1_), channel_id=1, source_target_pairs={{0,4},{4,0},{8,12},{12,8},{16,20},{20,16},{24,28},{28,24},{1,5},{5... | collective-permute-start | bytes 1572872 | tf_op jit(solution)/shard_map/down2/ppermute | solution.py:455
  29.0 7.9 %collective-permute-start.2 = (bf16[2,2,2,256,256]{4,3,2,1,0:T(8,128)(2,1)}, bf16[2,2,2,256,256]{4,3,2,1,0:T(8,128)(2,1)}, u32[]{:S(2)}, u32[]{:S(2)}) collective-permute-start(bf16[2,2,2,256,256]{4,3,2,1,0:T(8,128)(2,1)} %get-tuple-element.46), channel_id=1, source_target_pairs={{0,1},{1,0},{2,3},{3,2},{4,5},{5,4},{6,7},{7,6},{8,9},{9,8},{10,11... | collective-permute-start | bytes 3145736 | tf_op jit(solution)/shard_map/core2/ppermute | solution.py:455
  30.9 31.6 %collective-permute-start.15 = (bf16[2,2,2,256,256]{4,3,2,1,0:T(8,128)(2,1)}, bf16[2,2,2,256,256]{4,3,2,1,0:T(8,128)(2,1)}, u32[]{:S(2)}, u32[]{:S(2)}) collective-permute-start(bf16[2,2,2,256,256]{4,3,2,1,0:T(8,128)(2,1)} %get-tuple-element.40.refs_2_.refs_0_), channel_id=1, source_target_pairs={{0,2},{1,3},{2,0},{3,1},{4,6},{5,7},{6,4},{7,5},{8,10},{9,11},{10,... | collective-permute-start | bytes 3145736 | tf_op jit(solution)/shard_map/pair3/ppermute | solution.py:455
  33.7 25.4 %collective-permute-start.3 = (bf16[2,2,256,256]{3,2,1,0:T(8,128)(2,1)}, bf16[2,2,256,256]{3,2,1,0:T(8,128)(2,1)}, u32[]{:S(2)}, u32[]{:S(2)}) collective-permute-start(bf16[2,2,256,256]{3,2,1,0:T(8,128)(2,1)} %get-tuple-element.47), channel_id=1, source_target_pairs={{4,8},{12,16},{20,24},{8,4},{16,12},{24,20},{5,9},{13,17},{21,25},... | collective-permute-start | bytes 1572872 | tf_op jit(solution)/shard_map/up2/ppermute | solution.py:455
  40.0 3.0 %collective-permute-start.10 = (bf16[2,2,2,256,256]{4,3,2,1,0:T(8,128)(2,1)}, bf16[2,2,2,256,256]{4,3,2,1,0:T(8,128)(2,1)}, u32[]{:S(2)}, u32[]{:S(2)}) collective-permute-start(bf16[2,2,2,256,256]{4,3,2,1,0:T(8,128)(2,1)} %get-tuple-element.56.refs_1_.refs_2_), channel_id=1, source_target_pairs={{0,1},{1,0},{2,3},{3,2},{4,5},{5,4},{6,7},{7,6},{8,9},{9,8},{10,11... | collective-permute-start | bytes 3145736 | tf_op jit(solution)/shard_map/core_pair1/ppermute | solution.py:455
  40.0 4.5 %collective-permute-start.11 = (bf16[2,2,2,256,256]{4,3,2,1,0:T(8,128)(2,1)}, bf16[2,2,2,256,256]{4,3,2,1,0:T(8,128)(2,1)}, u32[]{:S(2)}, u32[]{:S(2)}) collective-permute-start(bf16[2,2,2,256,256]{4,3,2,1,0:T(8,128)(2,1)} %get-tuple-element.57), channel_id=1, source_target_pairs={{0,1},{1,0},{2,3},{3,2},{4,5},{5,4},{6,7},{7,6},{8,9},{9,8},{10,11... | collective-permute-start | bytes 3145736 | tf_op jit(solution)/shard_map/core3/ppermute | solution.py:455
  43.0 6.1 %collective-permute-start.7 = (bf16[2,2,256,256]{3,2,1,0:T(8,128)(2,1)}, bf16[2,2,256,256]{3,2,1,0:T(8,128)(2,1)}, u32[]{:S(2)}, u32[]{:S(2)}) collective-permute-start(bf16[2,2,256,256]{3,2,1,0:T(8,128)(2,1)} %get-tuple-element.53.refs_1_.refs_2_), channel_id=1, source_target_pairs={{0,1},{1,0},{2,3},{3,2},{4,5},{5,4},{6,7},{7,6},{8,9},{9,8},{10,11... | collective-permute-start | bytes 1572872 | tf_op jit(solution)/shard_map/core_up0/ppermute | solution.py:455
  44.5 5.0 %collective-permute-start.8 = (bf16[2,2,256,256]{3,2,1,0:T(8,128)(2,1)}, bf16[2,2,256,256]{3,2,1,0:T(8,128)(2,1)}, u32[]{:S(2)}, u32[]{:S(2)}) collective-permute-start(bf16[2,2,256,256]{3,2,1,0:T(8,128)(2,1)} %get-tuple-element.54.refs_3_), channel_id=1, source_target_pairs={{0,1},{1,0},{2,3},{3,2},{4,5},{5,4},{6,7},{7,6},{8,9},{9,8},{10,11... | collective-permute-start | bytes 1572872 | tf_op jit(solution)/shard_map/core_down0/ppermute | solution.py:455
  49.1 6.6 %collective-permute-start.12 = (f32[2,8,256]{2,1,0:T(8,128)}, f32[2,8,256]{2,1,0:T(8,128)}, u32[]{:S(2)}, u32[]{:S(2)}) collective-permute-start(f32[2,8,256]{2,1,0:T(8,128)} %get-tuple-element.61.refs_1_), channel_id=1, source_target_pairs={{0,1},{1,0},{2,3},{3,2},{4,5},{5,4},{6,7},{7,6},{8,9},{9,8},{10,11... | collective-permute-start | bytes 49160 | tf_op jit(solution)/shard_map/beat1/ppermute | solution.py:455
  54.1 30.8 %collective-permute-start.22 = (bf16[2,2,2,256,256]{4,3,2,1,0:T(8,128)(2,1)}, bf16[2,2,2,256,256]{4,3,2,1,0:T(8,128)(2,1)}, u32[]{:S(2)}, u32[]{:S(2)}) collective-permute-start(bf16[2,2,2,256,256]{4,3,2,1,0:T(8,128)(2,1)} %get-tuple-element.62.refs_1_), channel_id=1, source_target_pairs={{0,2},{1,3},{2,0},{3,1},{4,6},{5,7},{6,4},{7,5},{8,10},{9,11},{10,... | collective-permute-start | bytes 3145736 | tf_op jit(solution)/shard_map/pair0/ppermute | solution.py:455
  55.7 35.1 %collective-permute-start.20 = (bf16[2,2,256,256]{3,2,1,0:T(8,128)(2,1)}, bf16[2,2,256,256]{3,2,1,0:T(8,128)(2,1)}, u32[]{:S(2)}, u32[]{:S(2)}) collective-permute-start(bf16[2,2,256,256]{3,2,1,0:T(8,128)(2,1)} %get-tuple-element.71), channel_id=1, source_target_pairs={{4,8},{12,16},{20,24},{8,4},{16,12},{24,20},{5,9},{13,17},{21,25},... | collective-permute-start | bytes 1572872 | tf_op jit(solution)/shard_map/up1/ppermute | solution.py:455
  59.1 4.8 %collective-permute-start.13 = (bf16[2,2,256,256]{3,2,1,0:T(8,128)(2,1)}, bf16[2,2,256,256]{3,2,1,0:T(8,128)(2,1)}, u32[]{:S(2)}, u32[]{:S(2)}) collective-permute-start(bf16[2,2,256,256]{3,2,1,0:T(8,128)(2,1)} %get-tuple-element.63.refs_1_.refs_2_), channel_id=1, source_target_pairs={{0,1},{1,0},{2,3},{3,2},{4,5},{5,4},{6,7},{7,6},{8,9},{9,8},{10,11... | collective-permute-start | bytes 1572872 | tf_op jit(solution)/shard_map/core_up2/ppermute | solution.py:455
  59.2 4.7 %collective-permute-start.14 = (bf16[2,2,256,256]{3,2,1,0:T(8,128)(2,1)}, bf16[2,2,256,256]{3,2,1,0:T(8,128)(2,1)}, u32[]{:S(2)}, u32[]{:S(2)}) collective-permute-start(bf16[2,2,256,256]{3,2,1,0:T(8,128)(2,1)} %get-tuple-element.64.refs_3_), channel_id=1, source_target_pairs={{0,1},{1,0},{2,3},{3,2},{4,5},{5,4},{6,7},{7,6},{8,9},{9,8},{10,11... | collective-permute-start | bytes 1572872 | tf_op jit(solution)/shard_map/core_down2/ppermute | solution.py:455
  62.5 28.3 %collective-permute-start.21 = (bf16[2,2,256,256]{3,2,1,0:T(8,128)(2,1)}, bf16[2,2,256,256]{3,2,1,0:T(8,128)(2,1)}, u32[]{:S(2)}, u32[]{:S(2)}) collective-permute-start(bf16[2,2,256,256]{3,2,1,0:T(8,128)(2,1)} %get-tuple-element.72), channel_id=1, source_target_pairs={{0,4},{4,0},{8,12},{12,8},{16,20},{20,16},{24,28},{28,24},{1,5},{5... | collective-permute-start | bytes 1572872 | tf_op jit(solution)/shard_map/down1/ppermute | solution.py:455
  63.9 6.2 %collective-permute-start.17 = (bf16[2,2,2,256,256]{4,3,2,1,0:T(8,128)(2,1)}, bf16[2,2,2,256,256]{4,3,2,1,0:T(8,128)(2,1)}, u32[]{:S(2)}, u32[]{:S(2)}) collective-permute-start(bf16[2,2,2,256,256]{4,3,2,1,0:T(8,128)(2,1)} %gate.25.refs_6_.refs_2_), channel_id=1, source_target_pairs={{0,1},{1,0},{2,3},{3,2},{4,5},{5,4},{6,7},{7,6},{8,9},{9,8},{10,11... | collective-permute-start | bytes 3145736 | tf_op jit(solution)/shard_map/core_pair3/ppermute | solution.py:455
  68.6 40.3 %collective-permute-start.16 = (bf16[2,2,2,256,256]{4,3,2,1,0:T(8,128)(2,1)}, bf16[2,2,2,256,256]{4,3,2,1,0:T(8,128)(2,1)}, u32[]{:S(2)}, u32[]{:S(2)}) collective-permute-start(bf16[2,2,2,256,256]{4,3,2,1,0:T(8,128)(2,1)} %get-tuple-element.66.refs_4_), channel_id=1, source_target_pairs={{0,2},{1,3},{2,0},{3,1},{4,6},{5,7},{6,4},{7,5},{8,10},{9,11},{10,... | collective-permute-start | bytes 3145736 | tf_op jit(solution)/shard_map/pair2/ppermute | solution.py:455
  74.5 31.8 %collective-permute-start.19 = (bf16[2,2,256,256]{3,2,1,0:T(8,128)(2,1)}, bf16[2,2,256,256]{3,2,1,0:T(8,128)(2,1)}, u32[]{:S(2)}, u32[]{:S(2)}) collective-permute-start(bf16[2,2,256,256]{3,2,1,0:T(8,128)(2,1)} %get-tuple-element.67.refs_4_), channel_id=1, source_target_pairs={{0,4},{4,0},{8,12},{12,8},{16,20},{20,16},{24,28},{28,24},{1,5},{5... | collective-permute-start | bytes 1572872 | tf_op jit(solution)/shard_map/down3/ppermute | solution.py:455
  77.1 31.8 %all-to-all-start = ((f32[32,1,128]{2,1,0:T(1,128)}), f32[32,1,128]{2,1,0:T(1,128)}, u32[]{:S(2)}, u32[]{:S(2)}) async-start(f32[32,1,128]{2,1,0:T(1,128)} %range_parts.1.refs_1_), calls=%async_computation | async-start | bytes 32768 | tf_op jit(solution)/shard_map/all_to_all | solution.py:537
  85.0 16.0 %collective-permute-start.18 = (bf16[2,2,256,256]{3,2,1,0:T(8,128)(2,1)}, bf16[2,2,256,256]{3,2,1,0:T(8,128)(2,1)}, u32[]{:S(2)}, u32[]{:S(2)}) collective-permute-start(bf16[2,2,256,256]{3,2,1,0:T(8,128)(2,1)} %get-tuple-element.69), channel_id=1, source_target_pairs={{4,8},{12,16},{20,24},{8,4},{16,12},{24,20},{5,9},{13,17},{21,25},... | collective-permute-start | bytes 1572872 | tf_op jit(solution)/shard_map/up3/ppermute | solution.py:455
